TPU v7x, 32 devices: a whole 2x2x4 slice. The times are simulated.
32 devices in a mesh: dp: 8 (over y, x, core), tensor: 4 (over z).
Axes of the slice: x: 2, y: 2, z: 4, core: 2. Of those that a mesh axis runs over, the one named last changes fastest.
Arguments:
- hidden_in: bfloat16 [8192, 768], P('dp'), may hold values from -6 to 6
- visual_feats: bfloat16 [128, 257, 1408], P('dp'), may hold values from -6 to 6
- caption_lengths: int32 [128, 4], P('dp'), may hold values from 1 to 16, 32 in all within a row
- self_qkv: bfloat16 [3, 768, 768], P(None, None, 'tensor'), may hold values from -0.21875 to 0.21875
- self_out: bfloat16 [768, 768], P('tensor'), may hold values from -0.875 to 0.875
- cross_query: bfloat16 [768, 768], P(None, 'tensor'), may hold values from -0.21875 to 0.21875
- cross_kv: bfloat16 [2, 1408, 768], P(None, None, 'tensor'), may hold values from -0.15625 to 0.15625
- cross_out: bfloat16 [768, 768], P('tensor'), may hold values from -1.25 to 1.25
- ffn_in: bfloat16 [2, 768, 3072], P(None, None, 'tensor'), may hold values from -0.21875 to 0.21875
- ffn_out: bfloat16 [2, 3072, 768], P(None, 'tensor'), may hold values from -0.109375 to 0.109375
- norm_gain: float32 [4, 768], replicated, may hold values from 0.5 to 1.5
- norm_shift: float32 [4, 768], replicated, may hold values from -3 to 3
- out_grad: bfloat16 [8192, 768], P('dp'), may hold values from -6 to 6
Outputs:
- block_out: bfloat16 [8192, 768], P('dp')
- grad_hidden: float32 [8192, 768], P('dp')
- grad_self_qkv: float32 [3, 768, 768], P(None, None, 'tensor')
- grad_self_out: float32 [768, 768], P('tensor')
- grad_cross_query: float32 [768, 768], P(None, 'tensor')
- grad_cross_kv: float32 [2, 1408, 768], P(None, None, 'tensor')
- grad_cross_out: float32 [768, 768], P('tensor')
- grad_ffn_in: float32 [2, 768, 3072], P(None, None, 'tensor')
- grad_ffn_out: float32 [2, 3072, 768], P(None, 'tensor')
- grad_norm_gain: float32 [4, 768], replicated
- grad_norm_shift: float32 [4, 768], replicated
Inputs may be any that keep to these rules, and one draw needn't show every extreme that they name: `caption_lengths`: each item's 4 caption lengths sum to 32, and the longest caption of every item has exactly 16 tokens.
All inputs are finite; a program needn't handle non-finite values.
Results may differ from a plain program's by a relative error of at most 0.028.
Values may be sent and summed in bfloat16 or wider, within the bound.
A program may use at most 128 MiB of HBM per device.

v0:
```python
import math

import jax
import jax.numpy as jnp
from jax import lax
from jax.sharding import PartitionSpec as P

HEAD = 64
NQ = 32
TXT = 32


EPSILON = 1e-06
MASKED_SCORE = -1e30


def normalize(residue, gain_row, shift_row):
    row_mean = jnp.mean(residue, axis=-1, keepdims=True)
    centered = residue - row_mean
    variance = jnp.mean(centered * centered, axis=-1, keepdims=True)
    return centered * lax.rsqrt(variance + EPSILON) * gain_row + shift_row


def gelu_exact(pre_act):
    return jax.nn.gelu(pre_act, approximate=False)


def allowed_of(lengths):
    caption_ends = jnp.cumsum(lengths, axis=-1, dtype=jnp.int32)
    places = jnp.arange(TXT, dtype=jnp.int32)
    segment = jnp.sum(
        (places[None, :, None] >= caption_ends[:, None, :]).astype(jnp.int32),
        axis=-1,
        dtype=jnp.int32,
    )
    query_marks = jnp.full((lengths.shape[0], NQ), -1, dtype=jnp.int32)
    labels = jnp.concatenate([query_marks, segment], axis=1)
    return (labels[:, :, None] == labels[:, None, :]) | (labels[:, None, :] == -1)


def masked_scores(queries, key_heads, allowed, scale_factor):
    scores = (
        jnp.einsum("nrhe,nshe->nhrs", queries, key_heads, preferred_element_type=jnp.float32)
        * scale_factor
    )
    if allowed is not None:
        scores = jnp.where(allowed[:, None], scores, MASKED_SCORE)
    return scores


def attend_forward(queries, key_heads, value_heads, allowed, scale_factor):
    scores = masked_scores(queries, key_heads, allowed, scale_factor)
    row_top = jnp.max(scores, axis=-1, keepdims=True)
    lifted = jnp.exp(scores - row_top)
    row_total = jnp.sum(lifted, axis=-1, keepdims=True)
    chances = (lifted / row_total).astype(jnp.bfloat16)
    context = jnp.einsum(
        "nhrs,nshe->nrhe", chances, value_heads, preferred_element_type=jnp.float32
    )
    return (context.astype(jnp.bfloat16), row_top + jnp.log(row_total))


def attend_backward(
    queries, key_heads, value_heads, allowed, log_total, grad_context, scale_factor
):
    scores = masked_scores(queries, key_heads, allowed, scale_factor)
    chances = jnp.exp(scores - log_total)
    grad_chances = jnp.einsum(
        "nrhe,nshe->nhrs", grad_context, value_heads, preferred_element_type=jnp.float32
    )
    inner_sum = jnp.sum(grad_chances * chances, axis=-1, keepdims=True)
    grad_scores = (chances * (grad_chances - inner_sum)).astype(jnp.bfloat16)
    grad_queries = (
        jnp.einsum("nhrs,nshe->nrhe", grad_scores, key_heads, preferred_element_type=jnp.float32)
        * scale_factor
    )
    grad_keys = (
        jnp.einsum("nhrs,nrhe->nshe", grad_scores, queries, preferred_element_type=jnp.float32)
        * scale_factor
    )
    grad_values = jnp.einsum(
        "nhrs,nrhe->nshe",
        chances.astype(jnp.bfloat16),
        grad_context,
        preferred_element_type=jnp.float32,
    )
    return (grad_queries, grad_keys, grad_values)


def on_device(
    hidden_in,
    visual_feats,
    caption_lengths,
    self_qkv,
    self_out,
    cross_query,
    cross_kv,
    cross_out,
    ffn_in,
    ffn_out,
    norm_gain,
    norm_shift,
    out_grad,
):
    wide = jnp.float32
    narrow = jnp.bfloat16
    item_count = visual_feats.shape[0]
    visual_rows = visual_feats.shape[1]
    model_width = hidden_in.shape[1]
    row_span = hidden_in.shape[0] // item_count
    text_span = row_span - NQ
    local_cols = self_qkv.shape[2]
    head_local = local_cols // HEAD
    scale_factor = 1.0 / math.sqrt(HEAD)
    allowed = allowed_of(caption_lengths)

    def heads_of(tensor, span_rows):
        return tensor.reshape(item_count, span_rows, head_local, HEAD)

    def join_rows(query_part, text_part):
        joined = jnp.concatenate(
            [
                query_part.reshape(item_count, NQ, model_width),
                text_part.reshape(item_count, text_span, model_width),
            ],
            axis=1,
        )
        return joined.reshape(item_count * row_span, model_width)

    projected = jnp.einsum("md,cdk->cmk", hidden_in, self_qkv, preferred_element_type=wide).astype(
        narrow
    )
    query_self = heads_of(projected[0], row_span)
    key_self = heads_of(projected[1], row_span)
    value_self = heads_of(projected[2], row_span)
    self_context, self_log = attend_forward(query_self, key_self, value_self, allowed, scale_factor)
    self_flat = self_context.reshape(item_count * row_span, local_cols)
    self_sum = lax.psum(
        jnp.dot(self_flat, self_out, preferred_element_type=wide).astype(jnp.bfloat16), "tensor"
    ).astype(jnp.float32)
    first_norm, first_back = jax.vjp(
        normalize, hidden_in.astype(wide) + self_sum, norm_gain[0], norm_shift[0]
    )
    first_block = first_norm.reshape(item_count, row_span, model_width)
    query_rows = first_block[:, :NQ].reshape(item_count * NQ, model_width)
    text_rows = first_block[:, NQ:].reshape(item_count * text_span, model_width)
    query_low = query_rows.astype(narrow)
    cross_q = jnp.dot(query_low, cross_query, preferred_element_type=wide).astype(narrow)
    cross_act = jnp.einsum(
        "nvc,acd->anvd", visual_feats, cross_kv, preferred_element_type=wide
    ).astype(narrow)
    cross_keys = cross_act[0].reshape(item_count, visual_rows, head_local, HEAD)
    cross_values = cross_act[1].reshape(item_count, visual_rows, head_local, HEAD)
    cross_context, cross_log = attend_forward(
        heads_of(cross_q, NQ), cross_keys, cross_values, None, scale_factor
    )
    cross_flat = cross_context.reshape(item_count * NQ, local_cols)
    cross_sum = lax.psum(
        jnp.dot(cross_flat, cross_out, preferred_element_type=wide).astype(jnp.bfloat16), "tensor"
    ).astype(jnp.float32)
    second_norm, second_back = jax.vjp(
        normalize, query_rows + cross_sum, norm_gain[1], norm_shift[1]
    )
    second_low = second_norm.astype(narrow)
    text_low = text_rows.astype(narrow)
    pre_query = jnp.dot(second_low, ffn_in[0], preferred_element_type=wide)
    pre_text = jnp.dot(text_low, ffn_in[1], preferred_element_type=wide)
    act_query, gelu_query_back = jax.vjp(gelu_exact, pre_query)
    act_text, gelu_text_back = jax.vjp(gelu_exact, pre_text)
    act_query = act_query.astype(narrow)
    act_text = act_text.astype(narrow)
    ffn_query, ffn_text = (
        lax.psum(
            jnp.dot(act_query, ffn_out[0], preferred_element_type=wide).astype(jnp.bfloat16),
            "tensor",
        ).astype(jnp.float32),
        lax.psum(
            jnp.dot(act_text, ffn_out[1], preferred_element_type=wide).astype(jnp.bfloat16),
            "tensor",
        ).astype(jnp.float32),
    )
    third_query, third_query_back = jax.vjp(
        normalize, second_norm + ffn_query, norm_gain[2], norm_shift[2]
    )
    third_text, third_text_back = jax.vjp(
        normalize, text_rows + ffn_text, norm_gain[3], norm_shift[3]
    )
    output = join_rows(third_query, third_text).astype(narrow)
    grad_block = out_grad.astype(wide).reshape(item_count, row_span, model_width)
    grad_third_q, gain_query, shift_query = third_query_back(
        grad_block[:, :NQ].reshape(item_count * NQ, model_width)
    )
    grad_third_t, gain_text, shift_text = third_text_back(
        grad_block[:, NQ:].reshape(item_count * text_span, model_width)
    )
    down_query = grad_third_q.astype(narrow)
    down_text = grad_third_t.astype(narrow)
    grad_pre_query = gelu_query_back(
        jnp.einsum("md,fd->mf", down_query, ffn_out[0], preferred_element_type=wide)
    )[0].astype(narrow)
    grad_pre_text = gelu_text_back(
        jnp.einsum("md,fd->mf", down_text, ffn_out[1], preferred_element_type=wide)
    )[0].astype(narrow)
    grad_ffn_in = jnp.stack(
        [
            jnp.einsum("md,mf->df", second_low, grad_pre_query, preferred_element_type=wide),
            jnp.einsum("md,mf->df", text_low, grad_pre_text, preferred_element_type=wide),
        ]
    )
    grad_ffn_out = jnp.stack(
        [
            jnp.einsum("mf,md->fd", act_query, down_query, preferred_element_type=wide),
            jnp.einsum("mf,md->fd", act_text, down_text, preferred_element_type=wide),
        ]
    )
    back_query, back_text = (
        lax.psum(
            jnp.einsum("mf,df->md", grad_pre_query, ffn_in[0], preferred_element_type=wide).astype(
                jnp.bfloat16
            ),
            "tensor",
        ).astype(jnp.float32),
        lax.psum(
            jnp.einsum("mf,df->md", grad_pre_text, ffn_in[1], preferred_element_type=wide).astype(
                jnp.bfloat16
            ),
            "tensor",
        ).astype(jnp.float32),
    )
    grad_second = grad_third_q + back_query
    grad_text = grad_third_t + back_text
    grad_cross_in, gain_cross, shift_cross = second_back(grad_second)
    cross_down = grad_cross_in.astype(narrow)
    grad_cross_out = jnp.einsum("mk,md->kd", cross_flat, cross_down, preferred_element_type=wide)
    grad_cross_ctx = jnp.einsum(
        "md,kd->mk", cross_down, cross_out, preferred_element_type=wide
    ).astype(narrow)
    grad_cq, grad_ck, grad_cv = attend_backward(
        heads_of(cross_q, NQ),
        cross_keys,
        cross_values,
        None,
        cross_log,
        heads_of(grad_cross_ctx, NQ),
        scale_factor,
    )
    grad_cq = grad_cq.astype(narrow).reshape(item_count * NQ, local_cols)
    grad_cross_act = (
        jnp.stack([grad_ck, grad_cv]).astype(narrow).reshape(2, item_count, visual_rows, local_cols)
    )
    grad_cross_query = jnp.einsum("md,mk->dk", query_low, grad_cq, preferred_element_type=wide)
    grad_cross_kv = jnp.einsum(
        "nvc,anvd->acd", visual_feats, grad_cross_act, preferred_element_type=wide
    )
    back_cross = lax.psum(
        jnp.einsum("mk,dk->md", grad_cq, cross_query, preferred_element_type=wide).astype(
            jnp.bfloat16
        ),
        "tensor",
    ).astype(jnp.float32)
    grad_query_rows = grad_cross_in + back_cross
    grad_first_in, gain_first, shift_first = first_back(join_rows(grad_query_rows, grad_text))
    self_down = grad_first_in.astype(narrow)
    grad_self_out = jnp.einsum("mk,md->kd", self_flat, self_down, preferred_element_type=wide)
    grad_self_ctx = jnp.einsum(
        "md,kd->mk", self_down, self_out, preferred_element_type=wide
    ).astype(narrow)
    grad_sq, grad_sk, grad_sv = attend_backward(
        query_self,
        key_self,
        value_self,
        allowed,
        self_log,
        heads_of(grad_self_ctx, row_span),
        scale_factor,
    )
    grad_projected = (
        jnp.stack([grad_sq, grad_sk, grad_sv])
        .astype(narrow)
        .reshape(3, item_count * row_span, local_cols)
    )
    grad_self_qkv = jnp.einsum(
        "md,cmk->cdk", hidden_in, grad_projected, preferred_element_type=wide
    )
    back_self = lax.psum(
        jnp.einsum("cmk,cdk->md", grad_projected, self_qkv, preferred_element_type=wide).astype(
            jnp.bfloat16
        ),
        "tensor",
    ).astype(jnp.float32)
    grad_hidden = grad_first_in + back_self
    grad_gain = jnp.stack([gain_first, gain_cross, gain_query, gain_text])
    grad_shift = jnp.stack([shift_first, shift_cross, shift_query, shift_text])
    totals = lax.psum(
        (
            grad_self_qkv,
            grad_self_out,
            grad_cross_query,
            grad_cross_kv,
            grad_cross_out,
            grad_ffn_in,
            grad_ffn_out,
            grad_gain,
            grad_shift,
        ),
        "dp",
    )
    return (
        output,
        grad_hidden,
        totals[0],
        totals[1],
        totals[2],
        totals[3],
        totals[4],
        totals[5],
        totals[6],
        totals[7],
        totals[8],
    )


def solution(mesh):
    placed = (
        P("dp", None),
        P("dp", None, None),
        P("dp", None),
        P(None, None, "tensor"),
        P("tensor", None),
        P(None, "tensor"),
        P(None, None, "tensor"),
        P("tensor", None),
        P(None, None, "tensor"),
        P(None, "tensor", None),
        P(),
        P(),
        P("dp", None),
    )
    return jax.shard_map(
        on_device,
        mesh=mesh,
        in_specs=placed,
        out_specs=(
            P("dp", None),
            P("dp", None),
            P(None, None, "tensor"),
            P("tensor", None),
            P(None, "tensor"),
            P(None, None, "tensor"),
            P("tensor", None),
            P(None, None, "tensor"),
            P(None, "tensor", None),
            P(),
            P(),
        ),
        check_vma=False,
    )
```

profile of v0, /device:TPU:0, one launch (start us, length us, event | category | flops | bytes accessed | tf_op | source)
XLA Modules:
  0.0 714.7 jit_solution(3642964694184951790)
XLA Ops:
  8.3 2.8 fusion.45
  11.7 1.4 reshape_squeeze.16
  14.7 1.8 fusion.127
  20.0 1.8 convolution_convert_fusion.1
  22.3 9.9 %convert_bitcast_fusion = bf16[2,16,257,192]{3,2,1,0:T(8,128)(2,1)S(1)} fusion(bf16[16,257,1408]{2,0,1:T(8,128)(2,1)} %param.14, bf16[2,1408,192]{1,2,0:T(8,128)(2,1)S(1)} %copy-done), kind=kOutput, calls=%fused_computation.13 | convolution fusion | flops 4448065536 | bytes 15818752 | tf_op jit(solution)/shard_map/nvc,acd->anvd/dot_general | solution.py:149
  32.2 1.6 fusion.122
  33.8 2.6 copy.92
  36.4 4.4 copy.90
  42.1 51.6 %all-reduce.13.cloned.1.call-done = bf16[1024,768]{1,0:T(8,128)(2,1)} async-done(((bf16[1024,768]{1,0:T(8,128)(2,1)}), bf16[1024,768]{1,0:T(8,128)(2,1)}) %all-reduce.13.cloned.1.call-update) | async-done | bytes 1572880 | tf_op jit(solution)/shard_map/psum | solution.py:138
  93.7 2.0 fusion.16
  97.4 1.5 fusion.124
  102.4 2.4 multiply_reduce_fusion.3
  110.0 3.6 fusion.125
  113.5 1.4 fusion.123
  114.9 37.6 %all-reduce.15.cloned.1.call-done = bf16[512,768]{1,0:T(8,128)(2,1)} async-done(((bf16[512,768]{1,0:T(8,128)(2,1)}), bf16[512,768]{1,0:T(8,128)(2,1)}) %all-reduce.15.cloned.1.call-update) | async-done | bytes 786448 | tf_op jit(solution)/shard_map/psum | solution.py:158
  152.6 2.0 fusion.120
  155.4 5.3 multiply_convert_fusion.6
  161.6 1.7 convolution_convert_fusion.5
  163.4 6.4 multiply_convert_fusion.5
  170.7 1.7 convolution_convert_fusion.4
  172.4 34.1 %all-reduce.17.cloned.1.call-done = bf16[512,768]{1,0:T(8,128)(2,1)} async-done(((bf16[512,768]{1,0:T(8,128)(2,1)}), bf16[512,768]{1,0:T(8,128)(2,1)}) %all-reduce.17.cloned.1.call-update) | async-done | bytes 786448 | tf_op jit(solution)/shard_map/psum | solution.py:173
  206.5 2.2 fusion.118
  211.3 1.6 fusion.117
  216.8 1.7 convolution_convert_fusion.3
  218.8 1.5 log_add_fusion
  220.9 2.4 bitcast_convert_fusion.1
  223.4 2.3 convolution_bitcast_fusion.1
  225.7 2.5 convolution_bitcast_fusion.3
  228.2 59.3 %all-reduce.25.cloned.1.call-done = (bf16[512,768]{1,0:T(8,128)(2,1)}, bf16[512,768]{1,0:T(8,128)(2,1)}) async-done(((bf16[512,768]{1,0:T(8,128)(2,1)}, bf16[512,768]{1,0:T(8,128)(2,1)}), (bf16[512,768]{1,0:T(8,128)(2,1)}, bf16[512,768]{1,0:T(8,128)(2,1)})) %all-reduce.25.cloned.1.call-update) | async-done | bytes 1572880 | tf_op jit(solution)/shard_map/psum | solution.py:177
  287.5 1.9 fusion.116
  292.7 3.3 multiply_reduce_fusion.4
  299.8 2.7 multiply_reduce_fusion.2
  302.5 2.3 convolution_convert_fusion
  307.0 1.8 convolution_convert_fusion.2
  314.1 3.4 multiply_convert_fusion
  317.5 2.6 copy.114
  320.1 4.4 copy.113
  326.3 2.5 pad_maximum_fusion
  330.6 2.5 pad_maximum_fusion.1
  335.9 46.3 %all-reduce.23.cloned.1.call-done = (bf16[512,768]{1,0:T(8,128)(2,1)}, bf16[512,768]{1,0:T(8,128)(2,1)}) async-done(((bf16[512,768]{1,0:T(8,128)(2,1)}, bf16[512,768]{1,0:T(8,128)(2,1)}), (bf16[512,768]{1,0:T(8,128)(2,1)}, bf16[512,768]{1,0:T(8,128)(2,1)})) %all-reduce.23.cloned.1.call-update) | async-done | bytes 1572880 | tf_op jit(solution)/shard_map/psum | solution.py:223
  382.3 2.1 fusion.112
  386.6 1.8 fusion.9
  388.4 1.8 fusion.113
  392.4 2.3 fusion.50
  396.6 1.4 fusion.52
  398.1 1.5 fusion.51
  399.6 1.4 copy.110
  401.0 1.8 stack.55
  402.7 2.6 copy.103
  405.3 2.5 stack.53
  407.9 2.6 copy.107
  410.5 2.4 stack.54
  416.0 2.6 bitcast_convert_fusion
  418.7 13.5 %fusion.10 = f32[2,1408,192]{1,2,0:T(8,128)} fusion(bf16[16,257,1408]{2,0,1:T(8,128)(2,1)} %param.14, bf16[1,16,257,192]{3,2,1,0:T(8,128)(2,1)} %copy.114, bf16[1,16,257,192]{3,2,1,0:T(8,128)(2,1)} %copy.113), kind=kOutput, calls=%fused_computation.24 | convolution fusion | flops 4448065536 | bytes 16900096 | tf_op jit(solution)/shard_map/nvc,anvd->acd/dot_general | solution.py:252
  432.3 1.4 fusion.107
  434.3 2.3 fusion.41
  436.6 1.7 bitcast_convert_fusion.3
  441.1 24.0 %all-reduce.1 = (f32[4,768]{1,0:T(4,128)}, f32[4,768]{1,0:T(4,128)}) all-reduce(f32[4,768]{1,0:T(4,128)S(1)} %pad_maximum_fusion.4, f32[4,768]{1,0:T(4,128)S(1)} %pad_maximum_fusion.5), channel_id=1, replica_groups=mesh['dp'=8,'tensor'=4] {'dp'}, use_global_device_ids=true, to_apply=%region_43.44 | all-reduce | flops 6144 | bytes 49152 | tf_op jit(solution)/shard_map/psum | solution.py:294
  465.0 22.0 %all-reduce.19.cloned.1.call-done = bf16[1024,768]{1,0:T(8,128)(2,1)} async-done(((bf16[1024,768]{1,0:T(8,128)(2,1)}), bf16[1024,768]{1,0:T(8,128)(2,1)}) %all-reduce.19.cloned.1.call-update) | async-done | bytes 1572880 | tf_op jit(solution)/shard_map/psum | solution.py:285
  487.0 3.4 convert_add_fusion
  490.4 204.6 %all-reduce.21.cloned.1.call-done = (f32[3,768,192]{1,2,0:T(8,128)}, f32[192,768]{1,0:T(8,128)}, f32[768,192]{0,1:T(8,128)}, f32[2,1408,192]{1,2,0:T(8,128)}, f3...) async-done(((f32[3,768,192]{1,2,0:T(8,128)}, f32[192,768]{1,0:T(8,128)}, f32[768,192]{0,1:T(8,128)}, f32[2,1408,192]{1,2,0:T(8,128)}, ...) | async-done | bytes 15138832 | tf_op jit(solution)/shard_map/psum | solution.py:294
  695.0 2.9 copy.175
  703.2 2.2 copy.180
  705.5 2.2 copy.181
  (338 shorter events, 67.5 us)
Async XLA Ops:
  7.2 15.1 %copy-start = (bf16[2,1408,192]{1,2,0:T(8,128)(2,1)S(1)}, bf16[2,1408,192]{1,2,0:T(8,128)(2,1)}, u32[]{:S(2)}) copy-start(bf16[2,1408,192]{1,2,0:T(8,128)(2,1)} %param.19) | copy-start | bytes 3244036
  7.2 86.5 %all-reduce.13.cloned.1.call-start = ((), (), s32[]{:S(2)}) async-start(), calls=%async_computation | async-start | bytes 3145728 | tf_op jit(solution)/shard_map/psum | solution.py:138
  11.7 3.1 copy-start.36
  14.4 2.5 copy-start.33
  21.8 130.8 %all-reduce.15.cloned.1.call-start = ((), (), s32[]{:S(2)}) async-start(), calls=%async_computation.1 | async-start | bytes 1572864 | tf_op jit(solution)/shard_map/psum | solution.py:158
  36.4 4.4 copy-start.96
  36.4 5.1 copy-start.97
  36.4 57.3 %copy-start.5 = (bf16[1024,768]{1,0:T(8,128)(2,1)S(1)}, bf16[1024,768]{1,0:T(8,128)(2,1)}, u32[]{:S(2)}) copy-start(bf16[1024,768]{1,0:T(8,128)(2,1)} %param.13) | copy-start | bytes 4718596
  102.4 2.5 copy-start.32
  108.5 5.1 copy-start.45
  109.7 96.7 %all-reduce.17.cloned.1.call-start = ((), (), s32[]{:S(2)}) async-start(), calls=%async_computation.2 | async-start | bytes 1572864 | tf_op jit(solution)/shard_map/psum | solution.py:173
  110.0 3.6 copy-start.19
  152.6 2.4 copy-start.103
  154.6 6.1 copy-start.2
  154.6 6.1 copy-start.68
  154.9 5.8 copy-start.83
  155.0 5.7 copy-start.75
  155.4 6.2 copy-start.99
  163.3 124.2 %all-reduce.25.cloned.1.call-start = ((), (), s32[]{:S(2)}) async-start(), calls=%async_computation.6 | async-start | bytes 3145728 | tf_op jit(solution)/shard_map/psum | solution.py:177
  163.4 7.3 %copy-start.100 = (bf16[2,768,768]{2,1,0:T(8,128)(2,1)S(1)}, bf16[2,768,768]{2,1,0:T(8,128)(2,1)}, u32[]{:S(2)}) copy-start(bf16[2,768,768]{2,1,0:T(8,128)(2,1)} %param.22) | copy-start | bytes 7077892
  170.7 35.8 %copy-start.69 = (f32[512]{0:T(512)S(1)}, f32[512]{0:T(512)}, u32[]{:S(2)}) copy-start(f32[512]{0:T(512)} %copy-done.68) | copy-start | bytes 6148
  170.7 35.8 %copy-start.76 = (f32[512]{0:T(512)S(1)}, f32[512]{0:T(512)}, u32[]{:S(2)}) copy-start(f32[512]{0:T(512)} %copy-done.75) | copy-start | bytes 6148
  170.7 35.8 %copy-start.91 = (f32[768]{0:T(1024)S(1)}, f32[768]{0:T(1024)}, u32[]{:S(2)}) copy-start(f32[768]{0:T(1024)} %get-tuple-element.27) | copy-start | bytes 9220
  211.3 2.4 copy-start.113
  211.3 3.4 copy-start.114
  212.9 3.0 copy-start.14
  212.9 3.0 copy-start.78
  218.5 4.8 copy-start.59
  218.5 163.8 %all-reduce.23.cloned.1.call-start = ((), (), s32[]{:S(2)}) async-start(), calls=%async_computation.5 | async-start | bytes 3145728 | tf_op jit(solution)/shard_map/psum | solution.py:223
  218.8 4.5 copy-start.15
  218.8 4.5 copy-start.79
  223.3 2.4 copy-start.3
  223.3 2.4 copy-start.70
  223.3 2.4 copy-start.77
  223.3 2.3 copy-start.92
  223.4 2.3 copy-start.108
  287.5 4.6 copy-start.40
  292.7 3.4 copy-start.84
  299.8 2.7 copy-start.64
  299.8 5.0 copy-start.111
  299.8 5.0 copy-start.112
  302.5 2.3 copy-start.22
  302.5 2.8 copy-start.102
  313.6 3.9 copy-start.26
  313.6 173.4 %all-reduce.19.cloned.1.call-start = ((), (), s32[]{:S(2)}) async-start(), calls=%async_computation.3 | async-start | bytes 3145728 | tf_op jit(solution)/shard_map/psum | solution.py:285
  320.1 4.4 copy-start.53
  320.1 4.4 copy-start.110
  326.3 2.5 copy-start.23
  326.3 2.6 copy-start.57
  326.3 2.6 copy-start.82
  330.6 2.5 copy-start.39
  330.6 2.5 copy-start.43
  330.6 3.7 copy-start.46
  392.3 2.3 copy-start.28
  392.4 2.6 copy-start.34
  392.4 2.6 copy-start.63
  412.8 3.2 copy-start.106
  418.7 13.6 %copy-start.31 = (bf16[1024,192]{0,1:T(8,128)(2,1)S(1)}, bf16[1024,192]{0,1:T(8,128)(2,1)}, u32[]{:S(2)}) copy-start(bf16[1024,192]{0,1:T(8,128)(2,1)} %copy-done.30) | copy-start | bytes 1179652
  418.7 276.3 %all-reduce.21.cloned.1.call-start = ((), (), s32[]{:S(2)}) async-start(), calls=%async_computation.4 | async-start | bytes 30277632 | tf_op jit(solution)/shard_map/psum | solution.py:294
  695.0 2.9 copy-start.62
  695.0 3.7 copy-start.61
  698.8 2.4 copy-start.60
  699.8 3.4 copy-start.29
  701.1 4.2 slice-start
  (60 other events, 87.4 us)
Sparse Core Ops, SparseCore 0:
  21.9 71.7 all-reduce.12
  109.9 42.6 all-reduce.14
  163.4 42.9 all-reduce.16
  218.6 68.7 all-reduce.24
  313.7 68.5 all-reduce.22
  418.8 68.1 all-reduce.18
  493.0 201.9 all-reduce.20
where the time goes:
time: 721 us; the launch traced here: 715 us
  waiting for transfers between devices  456 us (63%)
  matrix products  89.1 us (12%)
  local copies, waits for them, and re-layouts  84.1 us (12%)
  other arithmetic  44.9 us (6%)
  blocking collectives  24 us (3%)
  between operations  15.5 us (2%)
    psum x1, waiting for transfers between devices, on_device(): lax.psum((grad_self_qkv, grad_self_out, grad_cross_query, grad_cross_kv,...  205 us
    psum x1, waiting for transfers between devices, on_device(): lax.psum(jnp.dot(act_text, ffn_out[1], preferred_element_type=wide).astyp...  59.3 us
    psum x1, waiting for transfers between devices, on_device(): lax.psum(jnp.dot(self_flat, self_out, preferred_element_type=wide).astype...  51.6 us
    psum x1, waiting for transfers between devices, on_device(): lax.psum(jnp.einsum('mf,df->md', grad_pre_text, ffn_in[1], preferred_elem...  46.3 us
    unnamed x243, local copies, waits for them, and re-layouts  38.1 us
    psum x1, waiting for transfers between devices, on_device(): lax.psum(jnp.dot(cross_flat, cross_out, preferred_element_type=wide).asty...  37.6 us
    psum x1, waiting for transfers between devices, on_device(): lax.psum(jnp.dot(act_query, ffn_out[0], preferred_element_type=wide).asty...  34.1 us
    psum x1, blocking collectives, on_device(): lax.psum((grad_self_qkv, grad_self_out, grad_cross_query, grad_cross_kv,...  24 us
  transfers between devices with their start and end apart: 7, of which 7 were waited for; matrix products, arithmetic and copies ran while one was open for 12% of the time, Pallas kernels for 0%

commit v1 on v0

v1 whole, which is shorter than its diff:
```python
import functools
import math

import jax
import jax.numpy as jnp
from jax import lax
from jax.experimental import pallas as pl
from jax.experimental.pallas import tpu as pltpu
from jax.sharding import PartitionSpec as P

HEAD = 64
NQ = 32
TXT = 32
QUAD = 4
EPSILON = 1e-06
MASKED_SCORE = -1e30
SCALE = 1.0 / math.sqrt(HEAD)
WIDE = jnp.float32
NARROW = jnp.bfloat16
VMEM_BYTES = 56 * 2**20


def mm(a, b):
    return lax.dot_general(a, b, (((1,), (0,)), ((), ())), preferred_element_type=WIDE)


def mm_nt(a, b):
    return lax.dot_general(a, b, (((1,), (1,)), ((), ())), preferred_element_type=WIDE)


def mm_tn(a, b):
    return lax.dot_general(a, b, (((0,), (0,)), ((), ())), preferred_element_type=WIDE)


def lane_group(rows, lanes, size):
    return lax.broadcasted_iota(jnp.int32, (rows, lanes), 1) // size


def spread_heads(block, count):
    rows, lanes = block.shape
    group = lane_group(rows, lanes, HEAD)
    wide = block.astype(WIDE)
    return jnp.concatenate(
        [jnp.where(group == h, wide, 0.0).astype(NARROW) for h in range(count)], axis=0
    )


def gather_heads(block, count):
    rows, lanes = block.shape[0] // count, block.shape[1]
    group = lane_group(rows, lanes, HEAD)
    out = block[:rows]
    for h in range(1, count):
        out = jnp.where(group == h, block[h * rows : (h + 1) * rows], out)
    return out


def norm_parts(residue):
    mean = jnp.mean(residue, axis=-1, keepdims=True)
    centered = residue - mean
    variance = jnp.mean(centered * centered, axis=-1, keepdims=True)
    inverse = lax.rsqrt(variance + EPSILON)
    return centered * inverse, inverse


def norm_back(unit, inverse, gain_row, cotangent):
    scaled = gain_row * cotangent
    first = jnp.mean(scaled, axis=-1, keepdims=True)
    second = jnp.mean(scaled * unit, axis=-1, keepdims=True)
    return inverse * (scaled - first - unit * second)


def column_sums(unit, cotangent):
    return (
        jnp.sum(cotangent * unit, axis=0, keepdims=True),
        jnp.sum(cotangent, axis=0, keepdims=True),
    )


def gelu_parts(pre):
    bell = jnp.exp(-0.5 * pre * pre)
    half = 0.5 * lax.erf(pre * math.sqrt(0.5)) + 0.5
    return pre * half, half + pre * bell * (1.0 / math.sqrt(2.0 * math.pi))


def labels_of(position, ends):
    place = position - NQ
    label = jnp.zeros_like(position)
    for end in ends:
        label = label + jnp.where(place >= end, 1, 0)
    return jnp.where(position < NQ, -1, label)


def allowed_pairs(lens_ref, item, span, lanes):
    ends = []
    total = jnp.int32(0)
    for c in range(lens_ref.shape[1]):
        total = total + lens_ref[item, c]
        ends.append(total)
    key_label = labels_of(lax.broadcasted_iota(jnp.int32, (span, lanes), 0), ends)
    query_label = labels_of(lax.broadcasted_iota(jnp.int32, (span, lanes), 1) % span, ends)
    return (key_label == query_label) | (key_label == -1)


def self_forward_kernel(
    lens_ref, x_ref, w_ref, gain_ref, shift_ref,
    q_ref, k_ref, v_ref, p_ref, ctx_ref, res_ref, fq_ref, ft_ref,
):
    span = NQ + TXT
    items = x_ref.shape[0] // span
    lanes = QUAD * HEAD
    x = x_ref[...]
    q_ref[...] = (mm_nt(x, w_ref[0]) .astype(NARROW).astype(WIDE) * SCALE).astype(NARROW)
    k_ref[...] = mm_nt(x, w_ref[1]).astype(NARROW)
    v_ref[...] = mm_nt(x, w_ref[2]).astype(NARROW)

    @pl.loop(0, items)
    def _(item):
        rows = pl.ds(pl.multiple_of(item * span, span), span)
        allowed = allowed_pairs(lens_ref, pl.program_id(0) * items + item, span, lanes)
        for quad in range(x_ref.shape[1] // lanes):
            cols = slice(quad * lanes, (quad + 1) * lanes)
            scores = mm_nt(k_ref[rows, cols], spread_heads(q_ref[rows, cols], QUAD))
            scores = jnp.where(allowed, scores, MASKED_SCORE)
            lifted = jnp.exp(scores - jnp.max(scores, axis=0, keepdims=True))
            chances = lifted * (1.0 / jnp.sum(lifted, axis=0, keepdims=True))
            low = chances.astype(NARROW)
            p_ref[rows, cols] = low
            ctx_ref[rows, cols] = gather_heads(mm_tn(low, v_ref[rows, cols]), QUAD).astype(NARROW)

    residue = x.astype(WIDE) + mm(ctx_ref[...], w_ref[3])
    res_ref[...] = residue
    unit, _ = norm_parts(residue)
    first = unit * gain_ref[0:1] + shift_ref[0:1]
    for item in range(items):
        fq_ref[item * NQ : (item + 1) * NQ] = first[item * span : item * span + NQ]
        ft_ref[item * TXT : (item + 1) * TXT] = first[item * span + NQ : (item + 1) * span]


def self_forward(hidden, lens, weights, gain, shift):
    rows, width = hidden.shape
    block = min(rows, 256)
    half = block // 2
    full = pl.BlockSpec((block, width), lambda i: (i, 0))
    halves = pl.BlockSpec((half, width), lambda i: (i, 0))
    low = jax.ShapeDtypeStruct((rows, width), NARROW)
    return pl.pallas_call(
        self_forward_kernel,
        grid=(rows // block,),
        in_specs=[
            pl.BlockSpec(memory_space=pltpu.SMEM),
            full,
            pl.BlockSpec(weights.shape, lambda i: (0, 0, 0)),
            pl.BlockSpec(gain.shape, lambda i: (0, 0)),
            pl.BlockSpec(shift.shape, lambda i: (0, 0)),
        ],
        out_specs=[full, full, full, full, full, full, halves, halves],
        out_shape=[
            low, low, low, low, low,
            jax.ShapeDtypeStruct((rows, width), WIDE),
            jax.ShapeDtypeStruct((rows // 2, width), WIDE),
            jax.ShapeDtypeStruct((rows // 2, width), WIDE),
        ],
        compiler_params=pltpu.CompilerParams(vmem_limit_bytes=VMEM_BYTES),
        name="self_forward",
    )(lens, hidden, weights, gain, shift)


def self_backward_kernel(
    own_ref, x_ref, w_ref, gain_ref, res_ref, gq_ref, gt_ref, q_ref, k_ref, v_ref, p_ref, ctx_ref,
    grad_ref, gqkv_ref, gout_ref, gain_out, shift_out,
    down, dctx, dq, dk, dv, acc,
):
    span = NQ + TXT
    block = res_ref.shape[0]
    items = block // span
    lanes = QUAD * HEAD
    step = pl.program_id(0)
    unit, inverse = norm_parts(res_ref[...])
    pieces = []
    for item in range(items):
        pieces.append(gq_ref[item * NQ : (item + 1) * NQ])
        pieces.append(gt_ref[item * TXT : (item + 1) * TXT])
    cotangent = jnp.concatenate(pieces, axis=0)
    grad_res = norm_back(unit, inverse, gain_ref[0:1], cotangent)
    gain_sum, shift_sum = column_sums(unit, cotangent)

    @pl.when(step == 0)
    def _():
        gain_out[...] = gain_sum
        shift_out[...] = shift_sum

    @pl.when(step > 0)
    def _():
        gain_out[...] += gain_sum
        shift_out[...] += shift_sum

    grad_ref[...] = grad_res
    low = grad_res.astype(NARROW)
    down[...] = low
    dctx[...] = mm_nt(low, w_ref[3]).astype(NARROW)

    @pl.loop(0, items)
    def _(item):
        rows = pl.ds(pl.multiple_of(item * span, span), span)
        for quad in range(w_ref.shape[2] // lanes):
            cols = slice(quad * lanes, (quad + 1) * lanes)
            chances = p_ref[rows, cols]
            spread = spread_heads(dctx[rows, cols], QUAD)
            grad_chances = mm_nt(v_ref[rows, cols], spread)
            weighted = chances.astype(WIDE)
            inner = jnp.sum(grad_chances * weighted, axis=0, keepdims=True)
            scores = (weighted * (grad_chances - inner)).astype(NARROW)
            dk[rows, cols] = mm(scores, spread_heads(q_ref[rows, cols], QUAD)).astype(NARROW)
            dv[rows, cols] = mm(chances, spread).astype(NARROW)
            dq[rows, cols] = (gather_heads(mm_tn(scores, k_ref[rows, cols]), QUAD) * SCALE).astype(
                NARROW
            )

    grad_ref[...] += mm(dq[...], w_ref[0]) + mm(dk[...], w_ref[1]) + mm(dv[...], w_ref[2])

    own = own_ref[0]
    cols = gqkv_ref.shape[1]
    window = acc.shape[1]
    start = pl.multiple_of((own * cols) // 128 * 128, 128)
    here = pl.ds(start, window)
    x = x_ref[...]
    parts = (
        mm_tn(dq[:, here], x), mm_tn(dk[:, here], x), mm_tn(dv[:, here], x),
        mm_tn(ctx_ref[:, here], down[...]),
    )

    @pl.when(step == 0)
    def _():
        for c, part in enumerate(parts):
            acc[c] = part

    @pl.when(step > 0)
    def _():
        for c, part in enumerate(parts):
            acc[c] += part

    @pl.when(step == pl.num_programs(0) - 1)
    def _():
        offset = pl.multiple_of(own * cols - start, 64)
        for c in range(3):
            gqkv_ref[c] = acc[c, pl.ds(offset, cols), :].astype(gqkv_ref.dtype)
        gout_ref[...] = acc[3, pl.ds(offset, cols), :].astype(gout_ref.dtype)


def self_backward(own, hidden, weights, gain, residue, grad_q, grad_t, q, k, v, p, ctx, cols):
    rows, width = hidden.shape
    block = min(rows, 256)
    half = block // 2
    full = pl.BlockSpec((block, width), lambda i: (i, 0))
    halves = pl.BlockSpec((half, width), lambda i: (i, 0))
    row = pl.BlockSpec((1, width), lambda i: (0, 0))
    return pl.pallas_call(
        self_backward_kernel,
        grid=(rows // block,),
        in_specs=[
            pl.BlockSpec(memory_space=pltpu.SMEM),
            full,
            pl.BlockSpec(weights.shape, lambda i: (0, 0, 0)),
            pl.BlockSpec(gain.shape, lambda i: (0, 0)),
            full, halves, halves, full, full, full, full, full,
        ],
        out_specs=[
            full,
            pl.BlockSpec((3, cols, width), lambda i: (0, 0, 0)),
            pl.BlockSpec((cols, width), lambda i: (0, 0)),
            row, row,
        ],
        out_shape=[
            jax.ShapeDtypeStruct((rows, width), WIDE),
            jax.ShapeDtypeStruct((3, cols, width), NARROW),
            jax.ShapeDtypeStruct((cols, width), NARROW),
            jax.ShapeDtypeStruct((1, width), WIDE),
            jax.ShapeDtypeStruct((1, width), WIDE),
        ],
        scratch_shapes=[pltpu.VMEM((block, width), NARROW)] * 5
        + [pltpu.VMEM((4, (cols + 64 + 127) // 128 * 128, width), WIDE)],
        compiler_params=pltpu.CompilerParams(vmem_limit_bytes=VMEM_BYTES),
        name="self_backward",
    )(own, hidden, weights, gain, residue, grad_q, grad_t, q, k, v, p, ctx)


def visual_forward_kernel(x_ref, w_ref, k_ref, v_ref):
    x = x_ref[0]
    k_ref[0] = mm_nt(x, w_ref[0]).astype(NARROW)
    v_ref[0] = mm_nt(x, w_ref[1]).astype(NARROW)


def visual_forward(visual, weights):
    items, span, depth = visual.shape
    cols = weights.shape[1]
    out = pl.BlockSpec((1, span, cols), lambda i: (i, 0, 0))
    shape = jax.ShapeDtypeStruct((items, span, cols), NARROW)
    return pl.pallas_call(
        visual_forward_kernel,
        grid=(items,),
        in_specs=[
            pl.BlockSpec((1, span, depth), lambda i: (i, 0, 0)),
            pl.BlockSpec(weights.shape, lambda i: (0, 0, 0)),
        ],
        out_specs=[out, out],
        out_shape=[shape, shape],
        compiler_params=pltpu.CompilerParams(vmem_limit_bytes=VMEM_BYTES),
        name="visual_forward",
    )(visual, weights)


def cross_forward_kernel(x_ref, wq_ref, wo_ref, k_ref, v_ref, q_ref, p_ref, ctx_ref, part_ref):
    items = k_ref.shape[0]
    heads = q_ref.shape[1] // HEAD
    q_ref[...] = (
        mm_nt(x_ref[...].astype(NARROW), wq_ref[...]).astype(NARROW).astype(WIDE) * SCALE
    ).astype(NARROW)
    for item in range(items):
        rows = slice(item * NQ, (item + 1) * NQ)
        scores = mm_nt(k_ref[item], spread_heads(q_ref[rows], heads))
        lifted = jnp.exp(scores - jnp.max(scores, axis=0, keepdims=True))
        chances = (lifted * (1.0 / jnp.sum(lifted, axis=0, keepdims=True))).astype(NARROW)
        p_ref[item] = chances
        ctx_ref[rows] = gather_heads(mm_tn(chances, v_ref[item]), heads).astype(NARROW)
    part_ref[...] = mm(ctx_ref[...], wo_ref[...]).astype(NARROW)


def cross_forward(rows_q, wq, wo, k, v):
    rows, width = rows_q.shape
    items, span, cols = k.shape
    step = min(items, 4)
    heads = cols // HEAD
    block = step * NQ

    def by_rows(lanes):
        return pl.BlockSpec((block, lanes), lambda i: (i, 0))

    def by_items(lanes):
        return pl.BlockSpec((step, span, lanes), lambda i: (i, 0, 0))

    return pl.pallas_call(
        cross_forward_kernel,
        grid=(items // step,),
        in_specs=[
            by_rows(width),
            pl.BlockSpec(wq.shape, lambda i: (0, 0)),
            pl.BlockSpec(wo.shape, lambda i: (0, 0)),
            by_items(cols), by_items(cols),
        ],
        out_specs=[by_rows(cols), by_items(heads * NQ), by_rows(cols), by_rows(width)],
        out_shape=[
            jax.ShapeDtypeStruct((rows, cols), NARROW),
            jax.ShapeDtypeStruct((items, span, heads * NQ), NARROW),
            jax.ShapeDtypeStruct((rows, cols), NARROW),
            jax.ShapeDtypeStruct((rows, width), NARROW),
        ],
        compiler_params=pltpu.CompilerParams(vmem_limit_bytes=VMEM_BYTES),
        name="cross_forward",
    )(rows_q, wq, wo, k, v)


def cross_backward_kernel(
    down_ref, fq_ref, wq_ref, wo_ref, q_ref, k_ref, v_ref, p_ref, ctx_ref,
    part_ref, dk_ref, dv_ref, gq_ref, go_ref, dctx, dq, acc,
):
    items = k_ref.shape[0]
    heads = q_ref.shape[1] // HEAD
    step = pl.program_id(0)
    dctx[...] = mm_nt(down_ref[...], wo_ref[...]).astype(NARROW)
    for item in range(items):
        rows = slice(item * NQ, (item + 1) * NQ)
        chances = p_ref[item]
        spread = spread_heads(dctx[rows], heads)
        grad_chances = mm_nt(v_ref[item], spread)
        weighted = chances.astype(WIDE)
        inner = jnp.sum(grad_chances * weighted, axis=0, keepdims=True)
        scores = (weighted * (grad_chances - inner)).astype(NARROW)
        dk_ref[item] = mm(scores, spread_heads(q_ref[rows], heads)).astype(NARROW)
        dv_ref[item] = mm(chances, spread).astype(NARROW)
        dq[rows] = (gather_heads(mm_tn(scores, k_ref[item]), heads) * SCALE).astype(NARROW)
    part_ref[...] = mm(dq[...], wq_ref[...]).astype(NARROW)
    grad_q = mm_tn(dq[...], fq_ref[...].astype(NARROW))
    grad_o = mm_tn(ctx_ref[...], down_ref[...])

    @pl.when(step == 0)
    def _():
        acc[0] = grad_q
        acc[1] = grad_o

    @pl.when(step > 0)
    def _():
        acc[0] += grad_q
        acc[1] += grad_o

    @pl.when(step == pl.num_programs(0) - 1)
    def _():
        gq_ref[...] = acc[0].astype(gq_ref.dtype)
        go_ref[...] = acc[1].astype(go_ref.dtype)


def cross_backward(down, rows_q, wq, wo, q, k, v, p, ctx):
    rows, width = down.shape
    items, span, cols = k.shape
    step = min(items, 4)
    heads = cols // HEAD
    block = step * NQ

    def by_rows(lanes):
        return pl.BlockSpec((block, lanes), lambda i: (i, 0))

    def by_items(lanes):
        return pl.BlockSpec((step, span, lanes), lambda i: (i, 0, 0))

    whole = pl.BlockSpec(wq.shape, lambda i: (0, 0))
    low = jax.ShapeDtypeStruct((items, span, cols), NARROW)
    grads = jax.ShapeDtypeStruct((cols, width), NARROW)
    return pl.pallas_call(
        cross_backward_kernel,
        grid=(items // step,),
        in_specs=[
            by_rows(width), by_rows(width), whole, whole,
            by_rows(cols), by_items(cols), by_items(cols), by_items(heads * NQ), by_rows(cols),
        ],
        out_specs=[by_rows(width), by_items(cols), by_items(cols), whole, whole],
        out_shape=[jax.ShapeDtypeStruct((rows, width), NARROW), low, low, grads, grads],
        scratch_shapes=[
            pltpu.VMEM((block, cols), NARROW),
            pltpu.VMEM((block, cols), NARROW),
            pltpu.VMEM((2, cols, width), WIDE),
        ],
        compiler_params=pltpu.CompilerParams(vmem_limit_bytes=VMEM_BYTES),
        name="cross_backward",
    )(down, rows_q, wq, wo, q, k, v, p, ctx)


def visual_backward_kernel(x_ref, dk_ref, dv_ref, out_ref, acc, tail_x, tail_k, tail_v):
    step = pl.program_id(0)
    span = x_ref.shape[1]
    even = span // 128 * 128
    x = x_ref[0, :even]
    part_k = mm_tn(dk_ref[0, :even], x)
    part_v = mm_tn(dv_ref[0, :even], x)

    @pl.when(step == 0)
    def _():
        acc[0] = part_k
        acc[1] = part_v
        tail_x[...] = jnp.zeros_like(tail_x)
        tail_k[...] = jnp.zeros_like(tail_k)
        tail_v[...] = jnp.zeros_like(tail_v)

    @pl.when(step > 0)
    def _():
        acc[0] += part_k
        acc[1] += part_v

    if span > even:
        here = pl.ds(step * (span - even), span - even)
        tail_x[here] = x_ref[0, even:].astype(WIDE)
        tail_k[here] = dk_ref[0, even:].astype(WIDE)
        tail_v[here] = dv_ref[0, even:].astype(WIDE)

    @pl.when(step == pl.num_programs(0) - 1)
    def _():
        x = tail_x[...].astype(NARROW)
        out_ref[0] = (acc[0] + mm_tn(tail_k[...].astype(NARROW), x)).astype(out_ref.dtype)
        out_ref[1] = (acc[1] + mm_tn(tail_v[...].astype(NARROW), x)).astype(out_ref.dtype)


def visual_backward(visual, dk, dv):
    items, span, depth = visual.shape
    cols = dk.shape[2]
    tail = max(16, (items * (span % 128) + 15) // 16 * 16)
    return pl.pallas_call(
        visual_backward_kernel,
        grid=(items,),
        in_specs=[
            pl.BlockSpec((1, span, depth), lambda i: (i, 0, 0)),
            pl.BlockSpec((1, span, cols), lambda i: (i, 0, 0)),
            pl.BlockSpec((1, span, cols), lambda i: (i, 0, 0)),
        ],
        out_specs=pl.BlockSpec((2, cols, depth), lambda i: (0, 0, 0)),
        out_shape=jax.ShapeDtypeStruct((2, cols, depth), NARROW),
        scratch_shapes=[
            pltpu.VMEM((2, cols, depth), WIDE),
            pltpu.VMEM((tail, depth), WIDE),
            pltpu.VMEM((tail, cols), WIDE),
            pltpu.VMEM((tail, cols), WIDE),
        ],
        compiler_params=pltpu.CompilerParams(vmem_limit_bytes=VMEM_BYTES),
        name="visual_backward",
    )(visual, dk, dv)


def feed_kernel(
    own_ref, fq_ref, cross_ref, win_ref, wout_ref, gain_ref, shift_ref, cot_ref,
    out_ref, grad_ref, down_ref, low_ref, top_ref, act_ref, dpre_ref, gain_out, shift_out,
    unit1, inverse1, second, slopes, total,
):
    step = pl.program_id(0)
    chunks = slopes.shape[0]
    width = slopes.shape[2]
    per = act_ref.shape[1] // width
    chunk = lax.rem(step, chunks)
    mine = chunk // per == own_ref[0]
    place = pl.ds(pl.multiple_of(lax.rem(chunk, per) * width, width), width)

    @pl.when(step == 0)
    def _():
        unit, inverse = norm_parts(fq_ref[...] + cross_ref[...].astype(WIDE))
        unit1[...] = unit
        inverse1[...] = inverse
        value = unit * gain_ref[1:2] + shift_ref[1:2]
        second[...] = value
        low_ref[...] = value.astype(NARROW)
        total[...] = jnp.zeros_like(total)

    @pl.when(step < chunks)
    def _():
        act, slope = gelu_parts(mm(low_ref[...], win_ref[0]))
        slopes[chunk] = slope
        act = act.astype(NARROW)
        total[...] += mm(act, wout_ref[0])

        @pl.when(mine)
        def _():
            act_ref[:, place] = act

    @pl.when(step == chunks)
    def _():
        unit, inverse = norm_parts(second[...] + total[...])
        out_ref[...] = (unit * gain_ref[2:3] + shift_ref[2:3]).astype(NARROW)
        cotangent = cot_ref[...].astype(WIDE)
        gain_sum, shift_sum = column_sums(unit, cotangent)
        gain_out[1:2] = gain_sum
        shift_out[1:2] = shift_sum
        grad = norm_back(unit, inverse, gain_ref[2:3], cotangent)
        total[...] = grad
        top_ref[...] = grad.astype(NARROW)

    @pl.when(step >= chunks)
    def _():
        dpre = (mm_nt(top_ref[...], wout_ref[0]) * slopes[chunk]).astype(NARROW)
        total[...] += mm_nt(dpre, win_ref[0])

        @pl.when(mine)
        def _():
            dpre_ref[:, place] = dpre

    @pl.when(step == 2 * chunks - 1)
    def _():
        grad_second = total[...]
        gain_sum, shift_sum = column_sums(unit1[...], grad_second)
        gain_out[0:1] = gain_sum
        shift_out[0:1] = shift_sum
        grad = norm_back(unit1[...], inverse1[...], gain_ref[1:2], grad_second)
        grad_ref[...] = grad
        down_ref[...] = grad.astype(NARROW)


def feed_forward_back(own, rows_q, cross, win, wout, gain, shift, cotangent):
    rows, width = rows_q.shape
    shards, _, hidden = win.shape
    tile = 256 if hidden % 256 == 0 else hidden
    per = hidden // tile
    chunks = shards * per
    whole = pl.BlockSpec((rows, width), lambda i: (0, 0))
    owned = pl.BlockSpec((rows, hidden), lambda i: (0, 0))
    pair = pl.BlockSpec((2, width), lambda i: (0, 0))
    low = jax.ShapeDtypeStruct((rows, width), NARROW)
    mine = jax.ShapeDtypeStruct((rows, hidden), NARROW)
    two = jax.ShapeDtypeStruct((2, width), WIDE)
    return pl.pallas_call(
        feed_kernel,
        grid=(2 * chunks,),
        in_specs=[
            pl.BlockSpec(memory_space=pltpu.SMEM),
            whole, whole,
            pl.BlockSpec((1, width, tile), lambda i: ((i % chunks) // per, 0, (i % chunks) % per)),
            pl.BlockSpec((1, tile, width), lambda i: ((i % chunks) // per, (i % chunks) % per, 0)),
            pl.BlockSpec(gain.shape, lambda i: (0, 0)),
            pl.BlockSpec(shift.shape, lambda i: (0, 0)),
            whole,
        ],
        out_specs=[whole, whole, whole, whole, whole, owned, owned, pair, pair],
        out_shape=[
            low, jax.ShapeDtypeStruct((rows, width), WIDE), low, low, low, mine, mine, two, two,
        ],
        scratch_shapes=[
            pltpu.VMEM((rows, width), WIDE),
            pltpu.VMEM((rows, 1), WIDE),
            pltpu.VMEM((rows, width), WIDE),
            pltpu.VMEM((chunks, rows, tile), WIDE),
            pltpu.VMEM((rows, width), WIDE),
        ],
        compiler_params=pltpu.CompilerParams(vmem_limit_bytes=VMEM_BYTES),
        name="feed_query",
    )(own, rows_q, cross, win, wout, gain, shift, cotangent)


MESH = pl.DeviceIdType.MESH
PEERS = 8


def flip(index, bit):
    return index + bit - 2 * bit * ((index // bit) % 2)


def greet(targets):
    barrier = pltpu.get_barrier_semaphore()
    for target in targets:
        pl.semaphore_signal(barrier, inc=1, device_id=target, device_id_type=MESH)
    pl.semaphore_wait(barrier, len(targets))


def remote(src, dst, send, recv, target):
    return pltpu.make_async_remote_copy(
        src_ref=src, dst_ref=dst, send_sem=send, recv_sem=recv, device_id=target, device_id_type=MESH
    )


class Spread:
    def __init__(self, at, own_at, send, recv):
        self.at, self.own_at, self.send, self.recv = at, own_at, send, recv
        self.dp, self.tensor = lax.axis_index("dp"), lax.axis_index("tensor")
        self.shards = lax.axis_size("tensor")
        self.peer = self.dp % PEERS
        self.index = 0
        self.open = []

    def targets(self):
        along = [(self.dp, (self.tensor + s) % self.shards) for s in range(1, self.shards)]
        return along + [(flip(self.dp, bit), self.tensor) for bit in (2, 4, 1)]

    def copy(self, src, dst, target):
        self.index += 1
        made = remote(src, dst, self.send.at[self.index - 1], self.recv.at[self.index - 1], target)
        made.start()
        self.open.append(made)
        return made

    def along_tensor(self):
        return [
            self.copy(
                self.own_at(self.peer),
                self.at(self.tensor, self.peer, None),
                (self.dp, (self.tensor + s) % self.shards),
            )
            for s in range(1, self.shards)
        ]

    def others(self):
        return [(self.tensor + self.shards - s) % self.shards for s in range(1, self.shards)]

    def exchange(self, bit, peers, half, shards=None):
        target = (flip(self.dp, bit), self.tensor)
        return [
            self.copy(self.at(shard, peer, half), self.at(shard, peer, half), target)
            for shard in (self.others() if shards is None else shards)
            for peer in peers
        ]

    @staticmethod
    def arrived(copies):
        for made in copies:
            made.wait_recv()

    def finish(self):
        for made in self.open:
            made.wait_send()


def spread_copies(shards):
    return (shards - 1) * (1 + 2 + 4 + 4)


def reduce_chain(part, out, buf_in, buf_mid, sems, steps):
    send_pair, send_mid, send_out, recv_pair, recv_mid, recv_out = sems
    dp, tensor = lax.axis_index("dp"), lax.axis_index("tensor")
    side = tensor // 2
    other = 1 - side
    pair = (dp, tensor + 1 - 2 * (tensor % 2))
    across = (dp, 3 - tensor)
    middle = (tensor + side) % 2 == 1

    def to_pair(half, c):
        return remote(part.at[half, c], buf_in.at[half, c], send_pair.at[half, c], recv_pair.at[half, c], pair)

    def to_mid(c):
        return remote(buf_mid.at[0, c], buf_mid.at[1, c], send_mid.at[c], recv_mid.at[c], across)

    def final_across(half, c):
        return remote(out.at[half, c], out.at[half, c], send_out.at[0, c], recv_out.at[half, c], across)

    def final_pair(half, c):
        return remote(out.at[half, c], out.at[half, c], send_out.at[1 + (0 if half is side else 1), c], recv_out.at[half, c], pair)

    def wide(ref, *at):
        return ref[at].astype(WIDE)

    def begin():
        @pl.when(middle)
        def _():
            greet([pair, across])

        @pl.when(jnp.logical_not(middle))
        def _():
            greet([pair])
            for c in range(steps):
                to_pair(other, c).start()
                to_pair(side, c).start()

    def first(c):
        to_pair(other, c).wait_recv()
        buf_mid[0, c] = (wide(buf_in, other, c) + wide(part, other, c)).astype(buf_mid.dtype)
        to_mid(c).start()

    def second(c):
        to_pair(side, c).wait_recv()
        to_mid(c).wait_recv()
        out[side, c] = (wide(buf_in, side, c) + wide(buf_mid, 1, c) + wide(part, side, c)).astype(out.dtype)
        final_across(side, c).start()
        final_pair(side, c).start()

    def third(c):
        final_across(other, c).wait_recv()
        final_pair(other, c).start()

    def step(t):
        @pl.when(middle)
        def _():
            if t < steps:
                first(t)
            if 0 <= t - 1 < steps:
                second(t - 1)
            if 0 <= t - 2 < steps:
                third(t - 2)

    def end():
        @pl.when(middle)
        def _():
            for c in range(steps):
                to_mid(c).wait_send()
                final_across(side, c).wait_send()
                final_pair(side, c).wait_send()
                final_pair(other, c).wait_send()

        @pl.when(jnp.logical_not(middle))
        def _():
            for c in range(steps):
                to_pair(other, c).wait_send()
                to_pair(side, c).wait_send()
                final_pair(other, c).wait_recv()
                final_pair(side, c).wait_recv()

    return [begin] + [functools.partial(step, t) for t in range(steps + 2)] + [end]


def chain_scratch(steps, rows, width):
    dma = pltpu.SemaphoreType.DMA
    return [
        pltpu.VMEM((2, steps, rows, width), NARROW),
        pltpu.VMEM((2, steps, rows, width), NARROW),
        dma((2, steps)), dma((steps,)), dma((3, steps)),
        dma((2, steps)), dma((steps,)), dma((2, steps)),
    ]


def sum_shards_kernel(part, out, buf_in, buf_mid, *sems):
    for run in reduce_chain(part, out, buf_in, buf_mid, sems, part.shape[1]):
        run()


def sum_shards(part, ident):
    rows, width = part.shape
    steps = 8
    shape = (2, steps, rows // (2 * steps), width)
    vmem = pl.BlockSpec(memory_space=pltpu.VMEM)
    return pl.pallas_call(
        sum_shards_kernel,
        in_specs=[vmem],
        out_specs=vmem,
        out_shape=jax.ShapeDtypeStruct(shape, NARROW),
        scratch_shapes=chain_scratch(steps, shape[2], width),
        compiler_params=pltpu.CompilerParams(
            collective_id=ident, has_side_effects=True, vmem_limit_bytes=VMEM_BYTES
        ),
        name="sum_shards",
    )(part.reshape(shape)).reshape(rows, width)


def gather_shards(shard):
    peers = lax.axis_size("dp")
    rows = shard.shape[0] // peers
    own = lax.dynamic_slice_in_dim(shard, lax.axis_index("dp") * rows, rows, axis=0)
    whole = lax.all_gather(own, ("tensor", "dp"), axis=0, tiled=True)
    return whole.reshape((whole.shape[0] // shard.shape[0],) + shard.shape)


def sum_items(values):
    return lax.psum([v.astype(NARROW) for v in values], "dp")


def on_device(
    hidden_in,
    visual_feats,
    caption_lengths,
    self_qkv,
    self_out,
    cross_query,
    cross_kv,
    cross_out,
    ffn_in,
    ffn_out,
    norm_gain,
    norm_shift,
    out_grad,
):
    items = visual_feats.shape[0]
    rows, width = hidden_in.shape
    span = rows // items
    cols = self_qkv.shape[2]
    hidden = ffn_in.shape[2]
    own = lax.axis_index("tensor").reshape((1,)).astype(jnp.int32)
    shards = lax.axis_size("tensor")

    attn_own = jnp.concatenate([jnp.swapaxes(self_qkv, 1, 2), self_out[None]], axis=0)
    attn = gather_shards(attn_own.reshape(4 * cols, width)).reshape(shards, 4, cols, width)
    attn = jnp.swapaxes(attn, 0, 1).reshape(4, shards * cols, width)
    feed = gather_shards(jnp.concatenate([ffn_in[0], ffn_out[0]], axis=0))
    win_q, wout_q = feed[:, :width], feed[:, width:]

    cross_wq = jnp.swapaxes(cross_query, 0, 1)
    cross_k, cross_v = visual_forward(visual_feats, jnp.swapaxes(cross_kv, 1, 2))
    q, k, v, p, ctx, residue, first_q, first_t = self_forward(
        hidden_in, caption_lengths, attn, norm_gain, norm_shift
    )
    cq, cp, cctx, cross_part = cross_forward(first_q, cross_wq, cross_out, cross_k, cross_v)
    cross_sum = sum_shards(cross_part, 1)

    cot = out_grad.reshape(items, span, width)
    cot_q = cot[:, :NQ].reshape(items * NQ, width)
    cot_t = cot[:, NQ:].reshape(items * TXT, width)

    low_t = first_t.astype(NARROW)
    act_t, slope_t = gelu_parts(jnp.dot(low_t, ffn_in[1], preferred_element_type=WIDE))
    act_t = act_t.astype(NARROW)
    ffn_t = lax.psum(mm(act_t, ffn_out[1]).astype(NARROW), "tensor").astype(WIDE)
    unit, inverse = norm_parts(first_t + ffn_t)
    out_t = (unit * norm_gain[3:4] + norm_shift[3:4]).astype(NARROW)
    cot_t = cot_t.astype(WIDE)
    gain_t, shift_t = column_sums(unit, cot_t)
    grad_t = norm_back(unit, inverse, norm_gain[3:4], cot_t)
    top_t = grad_t.astype(NARROW)
    dpre_t = (mm_nt(top_t, ffn_out[1]) * slope_t).astype(NARROW)
    grad_t = grad_t + lax.psum(mm_nt(dpre_t, ffn_in[1]).astype(NARROW), "tensor").astype(WIDE)

    out_q, grad_second, down_q, low_q, top_q, act_q, dpre_q, gain_pair, shift_pair = feed_forward_back(
        own, first_q, cross_sum, win_q, wout_q, norm_gain, norm_shift, cot_q
    )
    back_part, dk, dv, g_cq, g_co = cross_backward(
        down_q, first_q, cross_wq, cross_out, cq, cross_k, cross_v, cp, cctx
    )
    grad_q = grad_second + sum_shards(back_part, 2).astype(WIDE)
    g_in = jnp.stack([mm_tn(low_q, dpre_q), mm_tn(low_t, dpre_t)])
    g_out = jnp.stack([mm_tn(act_q, top_q), mm_tn(act_t, top_t)])
    g_kv = visual_backward(visual_feats, dk, dv)
    grad_hidden, g_qkv, g_so, gain_first, shift_first = self_backward(
        own, hidden_in, attn, norm_gain, residue, grad_q, grad_t, q, k, v, p, ctx, cols
    )
    out = jnp.concatenate(
        [out_q.reshape(items, NQ, width), out_t.reshape(items, TXT, width)], axis=1
    ).reshape(rows, width)
    gains = jnp.concatenate([gain_first, gain_pair, gain_t, shift_first, shift_pair, shift_t])
    sums = sum_items([g_in, g_out, g_kv, g_cq, g_co, g_qkv, g_so, gains])
    g_in, g_out, g_kv, g_cq, g_co, g_qkv, g_so, gains = [s.astype(WIDE) for s in sums]
    return (
        out,
        grad_hidden,
        jnp.swapaxes(g_qkv, 1, 2),
        g_so,
        jnp.swapaxes(g_cq, 0, 1),
        jnp.swapaxes(g_kv, 1, 2),
        g_co,
        g_in,
        g_out,
        gains[:4],
        gains[4:],
    )


def solution(mesh):
    placed = (
        P("dp", None),
        P("dp", None, None),
        P("dp", None),
        P(None, None, "tensor"),
        P("tensor", None),
        P(None, "tensor"),
        P(None, None, "tensor"),
        P("tensor", None),
        P(None, None, "tensor"),
        P(None, "tensor", None),
        P(),
        P(),
        P("dp", None),
    )
    return jax.shard_map(
        on_device,
        mesh=mesh,
        in_specs=placed,
        out_specs=(
            P("dp", None),
            P("dp", None),
            P(None, None, "tensor"),
            P("tensor", None),
            P(None, "tensor"),
            P(None, None, "tensor"),
            P("tensor", None),
            P(None, None, "tensor"),
            P(None, "tensor", None),
            P(),
            P(),
        ),
        check_vma=False,
    )
```

time: 721 us -> 586 us (0.81)
  Pallas kernels: 0 us -> 223 us
  waiting for transfers between devices: 456 us -> 248 us
  matrix products: 89.1 us -> 12.2 us
  local copies, waits for them, and re-layouts: 84.1 us -> 35.6 us
  other arithmetic: 44.9 us -> 28.3 us
    psum x7 -> x3, waiting for transfers between devices: 455 us -> 134 us  [the longest x1 92.8 us: sum_items(): return lax.psum([v.astype(NARROW) for v in values], 'dp')]
    pallas_call x0 -> x9, Pallas kernels: none -> 223 us  [the longest x2 71.8 us: sum_shards(): pl.pallas_call(sum_shards_kernel, in_specs=[vmem], out_specs=vmem, out_sh...]
    all_gather x0 -> x2, waiting for transfers between devices: none -> 113 us  [gather_shards(): whole = lax.all_gather(own, ('tensor', 'dp'), axis=0, tiled=True)]
    dot_general x38 -> x8, matrix products: 89.1 us -> 12.2 us  [the longest x4 4.23 us: mm_tn(): lax.dot_general(a, b, (((0,), (0,)), ((), ())), preferred_element_type=WIDE)]
    reduce_sum x22 -> x5, other arithmetic: 25.4 us -> 3.6 us  [the longest x1 1.36 us: norm_parts(): mean = jnp.mean(residue, axis=-1, keepdims=True)]
    unnamed x243 -> x66, local copies, waits for them, and re-layouts: 38.1 us -> 18.5 us
    another operation x10 -> x0, local copies, waits for them, and re-layouts: 17 us -> none  [the longest x2 7.05 us: on_device(): jnp.stack([grad_ck, grad_cv]).astype(narrow)]
    slice x9 -> x3, local copies, waits for them, and re-layouts: 16.4 us -> 9.56 us  [the longest x1 8.1 us: on_device(): win_q, wout_q = (feed[:, :width], feed[:, width:])]
  transfers between devices with their start and end apart: 7 -> 5, of which waited for: 7 -> 4; matrix products, arithmetic and copies ran while one was open for 12% -> 4% of each run, Pallas kernels for 0% -> 11%
where the time goes in v1:
time: 586 us; the launch traced here: 584 us
  waiting for transfers between devices  248 us (42%)
  Pallas kernels  223 us (38%)
  local copies, waits for them, and re-layouts  35.6 us (6%)
  other arithmetic  28.3 us (5%)
  blocking collectives  23.4 us (4%)
  between operations  14.1 us (2%)
  matrix products  12.2 us (2%)
    all_gather x2, waiting for transfers between devices, gather_shards(): whole = lax.all_gather(own, ('tensor', 'dp'), axis=0, tiled=True)  113 us
    psum x1, waiting for transfers between devices, sum_items(): return lax.psum([v.astype(NARROW) for v in values], 'dp')  92.8 us
    pallas_call x2, Pallas kernels, sum_shards(): pl.pallas_call(sum_shards_kernel, in_specs=[vmem], out_specs=vmem, out_sh...  71.8 us
    psum x1, waiting for transfers between devices, on_device(): lax.psum(mm(act_t, ffn_out[1]).astype(NARROW), 'tensor').astype(WIDE)  41.4 us
    pallas_call x1, Pallas kernels, feed_forward_back(): pl.pallas_call(feed_kernel, grid=(2 * chunks,), in_specs=[pl.BlockSpec(me...  34.5 us
    pallas_call x1, Pallas kernels, self_backward(): pl.pallas_call(self_backward_kernel, grid=(rows // block,), in_specs=[pl....  33.1 us
    pallas_call x1, Pallas kernels, self_forward(): pl.pallas_call(self_forward_kernel, grid=(rows // block,), in_specs=[pl.B...  28 us
    psum x1, blocking collectives, sum_items(): return lax.psum([v.astype(NARROW) for v in values], 'dp')  23.4 us
  transfers between devices with their start and end apart: 5, of which 4 were waited for; matrix products, arithmetic and copies ran while one was open for 4% of the time, Pallas kernels for 11%

profile of v1, /device:TPU:0, one launch (start us, length us, event | category | flops | bytes accessed | tf_op | source)
XLA Modules:
  0.0 584.2 jit_solution(15291691680632475610)
XLA Ops:
  7.2 1.4 pad_maximum_fusion.3
  8.6 0.7 constant_dynamic-slice_fusion
  9.3 0.0 all-reduce.5.cloned.1.call-start
  9.4 0.7 copy.28.lens_ref
  10.1 67.8 %all-gather.3.cloned.1.call-done = bf16[3072,768]{1,0:T(8,128)(2,1)} async-done(((bf16[96,768]{1,0:T(8,128)(2,1)}), bf16[3072,768]{1,0:T(8,128)(2,1)}) %all-gather.3.cloned.1.call-update) | async-done | bytes 4718608 | tf_op jit(solution)/shard_map/all_gather | solution.py:796
  77.9 4.9 copy.27
  82.8 28.0 %self_forward.1 = (bf16[1024,768]{1,0:T(8,128)(2,1)}, bf16[1024,768]{1,0:T(8,128)(2,1)}, bf16[1024,768]{1,0:T(8,128)(2,1)}, bf16[1024,768]{1,0:T(8,128)(2,1)}, b...) custom-call(s32[16,4]{1,0:T(8,128)} %copy.28.lens_ref, ...), custom_call_target="tpu_custom_call" | custom-call | tf_op jit(solution)/shard_map/self_forward/pallas_call | solution.py:146
  110.8 3.5 multiply_convert_fusion
  114.3 0.9 copy-done.5
  115.2 1.7 convolution_convert_fusion.5
  116.9 0.0 all-reduce.7.cloned.1.call-start
  116.9 0.9 slice_reduce_fusion.1
  117.8 0.2 fusion.11
  118.0 0.1 div.17
  118.1 41.4 %all-reduce.5.cloned.1.call-done = bf16[512,768]{1,0:T(8,128)(2,1)} async-done(((bf16[512,768]{1,0:T(8,128)(2,1)}), bf16[512,768]{1,0:T(8,128)(2,1)}) %all-reduce.5.cloned.1.call-update) | async-done | bytes 786448 | tf_op jit(solution)/shard_map/psum | solution.py:848
  159.5 1.4 fusion.31
  160.9 0.3 multiply_reduce_fusion
  161.2 0.7 fusion.12
  162.0 0.7 copy-done.2
  162.6 1.5 fusion.9
  164.2 0.9 copy-done.21
  165.1 1.1 fusion.5
  166.2 0.9 copy-done.17
  167.1 1.7 convolution_convert_fusion.4
  168.8 0.0 all-gather.5.cloned.1.call-start
  168.8 1.8 slice_bitcast_fusion
  170.6 1.0 fusion.30
  171.6 0.0 all-reduce.9.cloned.1.call-start
  171.7 11.4 %copy.29.x_ref = bf16[16,257,1408]{2,1,0:T(8,128)(2,1)} copy(bf16[16,257,1408]{2,0,1:T(8,128)(2,1)} %param.14) | data formatting | bytes 23158784 | tf_op args[1]
  183.1 16.8 %visual_forward.1 = (bf16[16,257,192]{2,1,0:T(8,128)(2,1)}, bf16[16,257,192]{2,1,0:T(8,128)(2,1)}) custom-call(bf16[16,257,1408]{2,1,0:T(8,128)(2,1)} %copy.29.x_ref, bf16[2,192,1408]{2,1,0:T(8,128)(2,1)} %bitcast.88), custom_call_target="tpu_custom_call" | custom-call | tf_op jit(solution)/shard_map/visual_forward/pallas_call | solution.py:298
  199.9 1.0 slice_reduce_fusion
  201.0 8.3 %cross_forward.1 = (bf16[512,192]{1,0:T(8,128)(2,1)}, bf16[16,257,96]{2,1,0:T(8,128)(2,1)}, bf16[512,192]{1,0:T(8,128)(2,1)}, bf16[512,768]{1,0:T(8,128)(2,1)}) custom-call(f32[512,768]{1,0:T(8,128)} %get-tuple-element.44.x_ref.fq_ref, bf16[192,768]{1,0:T(8,128)(2,1)} %bitcast.86, bf16[192,768]{1,0:T(8,128)(2,1)} %wo_ref.3, ...), custom_call_target="tpu_custom_call" | custom-call | tf_op jit(solution)/shard_map/cross_forward/pallas_call | solution.py:341
  209.3 38.8 %sum_shards.2 = bf16[2,8,32,768]{3,2,1,0:T(8,128)(2,1)} custom-call(bf16[2,8,32,768]{3,2,1,0:T(8,128)(2,1)} %bitcast.92), custom_call_target="tpu_custom_call" | custom-call | tf_op jit(solution)/shard_map/sum_shards/pallas_call | solution.py:779
  248.1 1.8 fusion.14
  249.9 0.8 fusion.16
  250.7 2.4 convert_add_fusion.1.gt_ref
  253.2 45.6 %all-gather.5.cloned.1.call-done = bf16[6144,768]{1,0:T(8,128)(2,1)} async-done(((bf16[192,768]{1,0:T(8,128)(2,1)}), bf16[6144,768]{1,0:T(8,128)(2,1)}) %all-gather.5.cloned.1.call-update) | async-done | bytes 9437200 | tf_op jit(solution)/shard_map/all_gather | solution.py:796
  298.8 8.1 %fusion.32 = (bf16[4,768,768]{2,1,0:T(8,128)(2,1)}, bf16[4,768,768]{2,1,0:T(8,128)(2,1)}) fusion(bf16[4,1536,768]{2,1,0:T(8,128)(2,1)} %bitcast.78), kind=kLoop, calls=%fused_computation.66 | loop fusion | bytes 18874368 | tf_op jit(solution)/shard_map/slice | solution.py:831
  306.9 34.5 %feed_query.1 = (bf16[512,768]{1,0:T(8,128)(2,1)}, f32[512,768]{1,0:T(8,128)}, bf16[512,768]{1,0:T(8,128)(2,1)}, bf16[512,768]{1,0:T(8,128)(2,1)}, bf16[512,768]...) custom-call(s32[1]{0:T(128)} %bitcast.own_ref, ...), custom_call_target="tpu_custom_call" | custom-call | tf_op jit(solution)/shard_map/feed_query/pallas_call | solution.py:573
  341.4 12.1 %cross_backward.1 = (bf16[512,768]{1,0:T(8,128)(2,1)}, bf16[16,257,192]{2,1,0:T(8,128)(2,1)}, bf16[16,257,192]{2,1,0:T(8,128)(2,1)}, bf16[192,768]{1,0:T(8,128)(2,1)}, bf16[192,768]{1,0:T(8,128)(2,1)}) custom-call(bf16[512,768]{1,0:T(8,128)(2,1)} %get-tuple-element.52.down_ref, f32[512,768]{1,0:T(8,128)} %get-tuple-element.44.x_ref.fq_ref, ...), custom_call_target="tpu_custom_call" | custom-call | tf_op jit(solution)/shard_map/cross_backward/pallas_call | solution.py:417
  353.5 33.0 %sum_shards.3 = bf16[2,8,32,768]{3,2,1,0:T(8,128)(2,1)} custom-call(bf16[2,8,32,768]{3,2,1,0:T(8,128)(2,1)} %bitcast.91), custom_call_target="tpu_custom_call" | custom-call | tf_op jit(solution)/shard_map/sum_shards/pallas_call | solution.py:779
  386.5 18.0 %visual_backward.1 = bf16[2,192,1408]{2,1,0:T(8,128)(2,1)} custom-call(bf16[16,257,1408]{2,1,0:T(8,128)(2,1)} %copy.29.x_ref, bf16[16,257,192]{2,1,0:T(8,128)(2,1)} %get-tuple-element.66.dk_ref, bf16[16,257,192]{2,1,0:T(8,128)(2,1)} %get-tuple-element.67.dv_ref), custom_call_target="tpu_custom_call" | custom-call | tf_op jit(solution)/shard_map/visual_backward/pallas_call | solution.py:474
  404.5 1.3 convert_add_fusion.gq_ref
  405.9 0.6 copy-done.31
  406.5 0.8 fusion.13
  407.3 0.5 copy-done.4
  407.7 1.6 pad_maximum_fusion
  409.4 0.4 copy-done.29
  409.7 0.8 fusion.15
  410.5 1.6 pad_maximum_fusion.1
  412.2 33.1 %self_backward.1 = (f32[1024,768]{1,0:T(8,128)}, bf16[3,192,768]{2,1,0:T(8,128)(2,1)}, bf16[192,768]{1,0:T(8,128)(2,1)}, f32[1,768]{1,0:T(1,128)}, f32[1,768]{1,0:T(1,128)}) custom-call(s32[1]{0:T(128)} %bitcast.own_ref, bf16[1024,768]{1,0:T(8,128)(2,1)} %x_ref.5, bf16[4,768,768]{2,1,0:T(8,128)(2,1)} %bitcast.73, f32[4,768]{1,0:T(4,128)} %gain_ref.5, ...), custom_call_target="tpu_custom_call" | custom-call | tf_op jit(solution)/shard_map/self_backward/pallas_call | solution.py:257
  445.4 0.6 copy-done.24
  446.1 23.4 %psum.79 = bf16[8,768]{1,0:T(8,128)(2,1)S(1)} all-reduce(bf16[8,768]{1,0:T(8,128)(2,1)S(1)} %concatenate.16), channel_id=1, replica_groups=mesh['dp'=8,'tensor'=4] {'dp'}, use_global_device_ids=true, to_apply=%region_15.0 | all-reduce | flops 6144 | bytes 24576 | tf_op jit(solution)/shard_map/psum | solution.py:801
  469.5 1.3 pad_maximum_fusion.2
  470.8 0.6 fusion.33
  471.4 92.8 %all-reduce.9.cloned.1.call-done = (bf16[3,768,192]{1,2,0:T(8,128)(2,1)}, bf16[192,768]{1,0:T(8,128)(2,1)}, bf16[768,192]{0,1:T(8,128)(2,1)}, bf16[2,1408,192]{1...) async-done(((bf16[3,768,192]{1,2,0:T(8,128)(2,1)}, bf16[192,768]{1,0:T(8,128)(2,1)}, ...) | async-done | bytes 7569424 | tf_op jit(solution)/shard_map/psum | solution.py:801
  564.2 1.9 convert_element_type.78
  566.1 1.8 transpose.43
  567.9 0.9 convert_element_type.79
  568.8 1.4 transpose.41
  570.2 1.5 transpose.45
  571.6 1.0 copy-done.10
  572.6 2.5 convert_element_type.80
  575.2 2.5 convert_element_type.81
  (73 shorter events, 0.4 us)
Async XLA Ops:
  7.2 2.2 copy-start.27
  7.2 70.7 %all-gather.3.cloned.1.call-start = ((), (), s32[]{:S(2)}) async-start(), calls=%async_computation | async-start | bytes 4866048 | tf_op jit(solution)/shard_map/all_gather | solution.py:796
  9.3 150.2 %all-reduce.5.cloned.1.call-start = ((), (), s32[]{:S(2)}) async-start(), calls=%async_computation.2 | async-start | bytes 1572864 | tf_op jit(solution)/shard_map/psum | solution.py:848
  82.8 28.0 %copy-start.11 = (bf16[2,768,768]{2,1,0:T(8,128)(2,1)S(1)}, bf16[2,768,768]{2,1,0:T(8,128)(2,1)}, u32[]{:S(2)}) copy-start(bf16[2,768,768]{2,1,0:T(8,128)(2,1)} %param.21) | copy-start | bytes 7077892
  110.8 4.4 copy-start.20
  114.3 0.9 copy-start.5
  115.2 2.6 copy-start.1
  116.9 42.7 %copy-start = (f32[512,768]{1,0:T(8,128)S(1)}, f32[512,768]{1,0:T(8,128)}, u32[]{:S(2)}) copy-start(f32[512,768]{1,0:T(8,128)} %get-tuple-element.49) | copy-start | bytes 4718596
  116.9 133.8 %all-reduce.7.cloned.1.call-start = ((), (), s32[]{:S(2)}) async-start(), calls=%async_computation.3 | async-start | bytes 1572864 | tf_op jit(solution)/shard_map/psum | solution.py:856
  161.2 1.4 copy-start.2
  162.6 1.5 copy-start.13
  162.6 2.4 copy-start.21
  165.1 2.0 copy-start.12
  166.2 0.9 copy-start.17
  168.8 130.0 %all-gather.5.cloned.1.call-start = ((), (), s32[]{:S(2)}) async-start(), calls=%async_computation.1 | async-start | bytes 9732096 | tf_op jit(solution)/shard_map/all_gather | solution.py:796
  171.6 392.6 %all-reduce.9.cloned.1.call-start = ((), (), s32[]{:S(2)}) async-start(), calls=%async_computation.4 | async-start | bytes 15138816 | tf_op jit(solution)/shard_map/psum | solution.py:801
  183.1 16.8 %copy-start.3 = (bf16[1024,768]{1,0:T(8,128)(2,1)S(1)}, bf16[1024,768]{1,0:T(8,128)(2,1)}, u32[]{:S(2)}) copy-start(bf16[1024,768]{1,0:T(8,128)(2,1)} %param.25) | copy-start | bytes 4718596
  209.3 38.8 %copy-start.18 = (bf16[512,768]{1,0:T(8,128)(2,1)S(1)}, bf16[512,768]{1,0:T(8,128)(2,1)}, u32[]{:S(2)}) copy-start(bf16[512,768]{1,0:T(8,128)(2,1)} %copy-done.17) | copy-start | bytes 2359300
  248.1 1.8 copy-start.6
  386.5 18.0 %copy-start.8 = (bf16[2,8,32,768]{3,2,1,0:T(8,128)(2,1)S(1)}, bf16[2,8,32,768]{3,2,1,0:T(8,128)(2,1)}, u32[]{:S(2)}) copy-start(bf16[2,8,32,768]{3,2,1,0:T(8,128)(2,1)} %sum_shards.3) | copy-start | bytes 2359300
  386.5 18.0 %copy-start.14 = (f32[512,768]{1,0:T(8,128)S(1)}, f32[512,768]{1,0:T(8,128)}, u32[]{:S(2)}) copy-start(f32[512,768]{1,0:T(8,128)} %get-tuple-element.51) | copy-start | bytes 4718596
  404.5 1.4 copy-start.30
  404.5 1.9 copy-start.31
  406.5 1.3 copy-start.4
  407.7 1.6 copy-start.28
  407.7 2.0 copy-start.29
  445.3 0.7 copy-start.24
  445.3 0.7 copy-start.23
  445.3 0.7 copy-start.26
  445.3 0.7 copy-start.25
  445.3 24.2 %copy-start.7 = (bf16[512,768]{1,0:T(8,128)(2,1)S(1)}, bf16[512,768]{1,0:T(8,128)(2,1)}, u32[]{:S(2)}) copy-start(bf16[512,768]{1,0:T(8,128)(2,1)} %get-tuple-element.91) | copy-start | bytes 2359300
  445.3 24.2 %copy-start.19 = (bf16[512,768]{1,0:T(8,128)(2,1)S(1)}, bf16[512,768]{1,0:T(8,128)(2,1)}, u32[]{:S(2)}) copy-start(bf16[512,768]{1,0:T(8,128)(2,1)} %get-tuple-element.48) | copy-start | bytes 2359300
  564.2 3.7 copy-start.22
  564.2 4.6 copy-start.16
  567.9 2.2 copy-start.15
  570.2 2.4 copy-start.10
  572.6 2.6 copy-start.9
Sparse Core Ops, SparseCore 0:
  11.5 66.3 all-gather.2
  117.0 42.4 all-reduce.4
  168.9 43.1 all-reduce.6
  215.4 83.3 all-gather.4
  445.5 118.6 all-reduce.8

commit v2 on v1

--- a/solution.py
+++ b/solution.py
@@ -82,6 +82,580 @@
     return pre * half, half + pre * bell * (1.0 / math.sqrt(2.0 * math.pi))
 
 
+MESH = pl.DeviceIdType.MESH
+PEERS = 8
+
+
+def flip(index, bit):
+    return index + bit - 2 * bit * ((index // bit) % 2)
+
+
+def greet(targets):
+    barrier = pltpu.get_barrier_semaphore()
+    for target in targets:
+        pl.semaphore_signal(barrier, inc=1, device_id=target, device_id_type=MESH)
+    pl.semaphore_wait(barrier, len(targets))
+
+
+def remote(src, dst, send, recv, target):
+    return pltpu.make_async_remote_copy(
+        src_ref=src, dst_ref=dst, send_sem=send, recv_sem=recv, device_id=target, device_id_type=MESH
+    )
+
+
+class Spread:
+    COPIES = 9
+
+    def __init__(self, at, send, recv, base):
+        self.at, self.send, self.recv, self.base = at, send, recv, base
+        self.dp, self.tensor = lax.axis_index("dp"), lax.axis_index("tensor")
+        self.shards = lax.axis_size("tensor")
+        self.peer = self.dp % PEERS
+
+    def hop(self, slot, s, src, dst, target):
+        index = self.base + (s - 1) * self.COPIES + slot
+        return remote(src, dst, self.send.at[index], self.recv.at[index], target)
+
+    def came(self, s):
+        return (self.tensor + self.shards - s) % self.shards
+
+    def along(self, s, own):
+        return self.hop(0, s, own, self.at(self.tensor, self.peer, None), (self.dp, (self.tensor + s) % self.shards))
+
+    def hand(self, slot, s, bit, peer, half):
+        place = self.at(self.came(s), peer, half)
+        return self.hop(slot, s, place, place, (flip(self.dp, bit), self.tensor))
+
+    def across(self, s):
+        return [self.hand(1, s, 2, self.peer, None), self.hand(2, s, 4, self.peer, None), self.hand(3, s, 1, self.peer, None)]
+
+    def onward(self, s):
+        x, y = flip(self.peer, 2), flip(self.peer, 4)
+        return (
+            [self.hand(4, s, 4, x, 0), self.hand(5, s, 1, x, None)],
+            [self.hand(6, s, 2, y, 1), self.hand(7, s, 1, y, None)],
+        )
+
+    def last(self, s):
+        return self.hand(8, s, 1, flip(flip(self.peer, 2), 4), None)
+
+    def start_across(self, s):
+        for made in self.across(s):
+            made.start()
+
+    def start_onward(self, s):
+        over_x, over_y, _ = self.across(s)
+        by_x, by_y = self.onward(s)
+        over_x.wait_recv()
+        for made in by_x:
+            made.start()
+        over_y.wait_recv()
+        for made in by_y:
+            made.start()
+
+    def start_last(self, s):
+        by_x, by_y = self.onward(s)
+        by_x[0].wait_recv()
+        by_y[0].wait_recv()
+        self.last(s).start()
+
+    def finish(self, s):
+        over = self.across(s)
+        by_x, by_y = self.onward(s)
+        final = self.last(s)
+        for made in (over[2], by_x[1], by_y[1], final):
+            made.wait_recv()
+        for made in over + by_x + by_y + [final]:
+            made.wait_send()
+
+    def targets(self):
+        return self.along_targets() + self.peer_targets()
+
+    def along_targets(self):
+        return [(self.dp, (self.tensor + s) % self.shards) for s in range(1, self.shards)]
+
+    def peer_targets(self):
+        return [(flip(self.dp, bit), self.tensor) for bit in (2, 4, 1)]
+
+
+def eighth(ref, offset=0):
+    rows = ref.shape[1] // PEERS
+
+    def at(shard, peer, half):
+        first = peer * rows + (0 if half is None else half * (rows // 2))
+        return ref.at[shard, pl.ds(pl.multiple_of(first, 16), rows if half is None else rows // 2)]
+
+    return at
+
+
+def reduce_chain(part, out, buf_in, buf_mid, sems, steps):
+    send_pair, send_mid, send_out, recv_pair, recv_mid, recv_out = sems
+    dp, tensor = lax.axis_index("dp"), lax.axis_index("tensor")
+    side = tensor // 2
+    other = 1 - side
+    pair = (dp, tensor + 1 - 2 * (tensor % 2))
+    across = (dp, 3 - tensor)
+    middle = (tensor + side) % 2 == 1
+
+    def to_pair(half, c):
+        return remote(part.at[half, c], buf_in.at[half, c], send_pair.at[half, c], recv_pair.at[half, c], pair)
+
+    def to_mid(c):
+        return remote(buf_mid.at[0, c], buf_mid.at[1, c], send_mid.at[c], recv_mid.at[c], across)
+
+    def final_across(half, c):
+        return remote(out.at[half, c], out.at[half, c], send_out.at[0, c], recv_out.at[half, c], across)
+
+    def final_pair(half, c):
+        return remote(out.at[half, c], out.at[half, c], send_out.at[1 + (0 if half is side else 1), c], recv_out.at[half, c], pair)
+
+    def wide(ref, *at):
+        return ref[at].astype(WIDE)
+
+    def begin(more=()):
+        @pl.when(middle)
+        def _():
+            greet([pair, across, *more])
+
+        @pl.when(jnp.logical_not(middle))
+        def _():
+            greet([pair, *more])
+            for c in range(steps):
+                to_pair(other, c).start()
+                to_pair(side, c).start()
+
+    def first(c):
+        to_pair(other, c).wait_recv()
+        buf_mid[0, c] = (wide(buf_in, other, c) + wide(part, other, c)).astype(buf_mid.dtype)
+        to_mid(c).start()
+
+    def second(c):
+        to_pair(side, c).wait_recv()
+        to_mid(c).wait_recv()
+        out[side, c] = (wide(buf_in, side, c) + wide(buf_mid, 1, c) + wide(part, side, c)).astype(out.dtype)
+        final_across(side, c).start()
+        final_pair(side, c).start()
+
+    def third(c):
+        final_across(other, c).wait_recv()
+        final_pair(other, c).start()
+
+    def step(t):
+        @pl.when(middle)
+        def _():
+            if t < steps:
+                first(t)
+            if 0 <= t - 1 < steps:
+                second(t - 1)
+            if 0 <= t - 2 < steps:
+                third(t - 2)
+
+    def end():
+        @pl.when(middle)
+        def _():
+            for c in range(steps):
+                to_mid(c).wait_send()
+                final_across(side, c).wait_send()
+                final_pair(side, c).wait_send()
+                final_pair(other, c).wait_send()
+
+        @pl.when(jnp.logical_not(middle))
+        def _():
+            for c in range(steps):
+                to_pair(other, c).wait_send()
+                to_pair(side, c).wait_send()
+                final_pair(other, c).wait_recv()
+                final_pair(side, c).wait_recv()
+
+    return [begin] + [functools.partial(step, t) for t in range(steps + 2)] + [end]
+
+
+def chain_scratch(steps, rows, width):
+    dma = pltpu.SemaphoreType.DMA
+    return [
+        pltpu.VMEM((2, steps, rows, width), NARROW),
+        pltpu.VMEM((2, steps, rows, width), NARROW),
+        dma((2, steps)), dma((steps,)), dma((3, steps)),
+        dma((2, steps)), dma((steps,)), dma((2, steps)),
+    ]
+
+
+def sum_shards_kernel(part, out, buf_in, buf_mid, *sems):
+    for run in reduce_chain(part, out, buf_in, buf_mid, sems, part.shape[1]):
+        run()
+
+
+def sum_shards(part, ident):
+    rows, width = part.shape
+    steps = 8
+    shape = (2, steps, rows // (2 * steps), width)
+    vmem = pl.BlockSpec(memory_space=pltpu.VMEM)
+    return pl.pallas_call(
+        sum_shards_kernel,
+        in_specs=[vmem],
+        out_specs=vmem,
+        out_shape=jax.ShapeDtypeStruct(shape, NARROW),
+        scratch_shapes=chain_scratch(steps, shape[2], width),
+        compiler_params=pltpu.CompilerParams(
+            collective_id=ident, has_side_effects=True, vmem_limit_bytes=VMEM_BYTES
+        ),
+        name="sum_shards",
+    )(part.reshape(shape)).reshape(rows, width)
+
+
+PIECES = 8
+
+
+class PeerSum:
+    def __init__(self, parts, source, work, total, land, higher, send, recv, base=0):
+        self.parts, self.source, self.work, self.land, self.higher = parts, source, work, land, higher
+        self.total = total
+        self.send, self.recv, self.base = send, recv, base
+        self.dp, self.tensor = lax.axis_index("dp"), lax.axis_index("tensor")
+        self.bits = [(self.dp // b) % 2 for b in (1, 2, 4)]
+
+    @staticmethod
+    def far_bits():
+        return [PEERS << k for k in range((lax.axis_size("dp") // PEERS - 1).bit_length())]
+
+    @staticmethod
+    def copies(parts, far):
+        return len(parts) * (6 + far)
+
+    def way(self, part):
+        order = ((2, self.bits[1]), (4, self.bits[2]))
+        return order if part[5] == 0 else order[::-1]
+
+    def rows(self, refs, part, piece, count):
+        array, first, size, column, columns, _ = part
+        start = pl.multiple_of(first + piece * size, 16)
+        return refs[array].at[pl.ds(start, count * size), pl.ds(column, columns)]
+
+    def hop(self, n, stage, src, dst, bit):
+        index = self.base + n * (6 + len(self.far_bits())) + stage
+        return remote(src, dst, self.send.at[index], self.recv.at[index], (flip(self.dp, bit), self.tensor))
+
+    def halving(self, n, stage):
+        part = self.parts[n]
+        core = self.bits[0]
+        if stage == 0:
+            away, kept, count, bit = (1 - core) * 4, core * 4, 4, 1
+        else:
+            (bit_1, own_1), (bit_2, own_2) = self.way(part)
+            if stage == 1:
+                away, kept, count, bit = core * 4 + (1 - own_1) * 2, core * 4 + own_1 * 2, 2, bit_1
+            else:
+                at = core * 4 + own_1 * 2
+                away, kept, count, bit = at + 1 - own_2, at + own_2, 1, bit_2
+        landed = self.land[n].at[pl.ds((0, 4, 6)[stage] * part[2], count * part[2])]
+        out = self.rows(self.source if stage == 0 else self.work, part, away, count)
+        return self.hop(n, stage, out, landed, bit), kept, count, landed
+
+    def final_piece(self, part):
+        (_, own_1), (_, own_2) = self.way(part)
+        return self.bits[0] * 4 + own_1 * 2 + own_2
+
+    def gathering(self, n, stage):
+        part = self.parts[n]
+        core = self.bits[0]
+        (bit_1, own_1), (bit_2, _) = self.way(part)
+        piece, count, bit = (
+            (self.final_piece(part), 1, bit_2), (core * 4 + own_1 * 2, 2, bit_1), (core * 4, 4, 1),
+        )[stage]
+        place = self.rows(self.total, part, piece, count)
+        return self.hop(n, 3 + stage, place, place, bit)
+
+    def targets(self):
+        return [(flip(self.dp, bit), self.tensor) for bit in [1, 2, 4] + self.far_bits()]
+
+    def start_halving(self, stage):
+        for n in range(len(self.parts)):
+            self.halving(n, stage)[0].start()
+
+    def end_halving(self, stage):
+        for n, part in enumerate(self.parts):
+            made, kept, count, landed = self.halving(n, stage)
+            made.wait_recv()
+            source = self.rows(self.source if stage == 0 else self.work, part, kept, count)
+            place = self.rows(self.total if stage == 2 else self.work, part, kept, count)
+            place[...] = (source[...].astype(WIDE) + landed[...].astype(WIDE)).astype(place.dtype)
+        for n in range(len(self.parts)):
+            self.halving(n, stage)[0].wait_send()
+
+    def far(self):
+        for k, bit in enumerate(self.far_bits()):
+            for n, part in enumerate(self.parts):
+                place = self.rows(self.total, part, self.final_piece(part), 1)
+                made = self.hop(n, 6 + k, place, self.higher[n].at[k], bit)
+                made.start()
+                made.wait()
+                place[...] = (place[...].astype(WIDE) + self.higher[n][k].astype(WIDE)).astype(place.dtype)
+
+    def start_gathering(self, stage):
+        for n in range(len(self.parts)):
+            self.gathering(n, stage).start()
+
+    def end_gathering(self, stage):
+        for n in range(len(self.parts)):
+            self.gathering(n, stage).wait()
+
+
+def peer_scratch(parts, shapes, far):
+    dma = pltpu.SemaphoreType.DMA
+    count = PeerSum.copies(parts, far)
+    land = [pltpu.VMEM((7 * p[2], p[4]), NARROW) for p in parts]
+    higher = [pltpu.VMEM((max(far, 1), p[2], p[4]), NARROW) for p in parts]
+    return [pltpu.VMEM(shape, NARROW) for shape in shapes * 2] + land + higher + [dma((count,)), dma((count,))]
+
+
+def sum_rows(values, out, land, send, recv):
+    dp, tensor = lax.axis_index("dp"), lax.axis_index("tensor")
+    bits = [1, 2, 4] + PeerSum.far_bits()
+    for k, bit in enumerate(bits):
+        source = values if k == 0 else out.at[k - 1]
+        made = remote(source, land.at[k], send.at[k], recv.at[k], (flip(dp, bit), tensor))
+        made.start()
+        made.wait()
+        out[k] = source[...] + land[k]
+
+
+def last_sums_kernel(parts, kv_ref, cross_ref, self_ref, rows_ref, kv_out, cq_out, co_out, qkv_out, so_out, rows_out, *rest):
+    work, total, rest = rest[:3], rest[3:6], rest[6:]
+    land, rest = rest[: len(parts)], rest[len(parts) :]
+    higher, rest = rest[: len(parts)], rest[len(parts) :]
+    send, recv, few, few_land, few_send, few_recv = rest
+    peers = PeerSum(parts, (kv_ref, cross_ref, self_ref), work, total, land, higher, send, recv)
+    greet(peers.targets())
+    for stage in range(3):
+        peers.start_halving(stage)
+        peers.end_halving(stage)
+    peers.far()
+    for stage in range(3):
+        peers.start_gathering(stage)
+        if stage == 0:
+            sum_rows(rows_ref, few, few_land, few_send, few_recv)
+            rows_out[...] = few[few.shape[0] - 1]
+        peers.end_gathering(stage)
+    kv, cross, own = total
+    cols = co_out.shape[0]
+    kv_out[0] = kv[:cols].astype(WIDE)
+    kv_out[1, 128:] = kv[cols : 2 * cols - 128].astype(WIDE)
+    kv_out[1, :128] = kv[2 * cols - 128 :].astype(WIDE)
+    cq_out[...] = cross[:cols].astype(WIDE)
+    co_out[...] = cross[cols:].astype(WIDE)
+    for c in range(3):
+        qkv_out[c] = own[c * cols : (c + 1) * cols].astype(WIDE)
+    so_out[...] = own[3 * cols :].astype(WIDE)
+
+
+def last_sums(kv, cross, own, rows, peers):
+    cols = cross.shape[0] // 2
+    width, depth = cross.shape[1], kv.shape[1]
+    third = own.shape[0] // 3
+    parts = (
+        (0, 0, kv.shape[0] // PIECES, 0, width, 0),
+        (0, 0, kv.shape[0] // PIECES, width, depth - width, 1),
+        (1, 0, cross.shape[0] // PIECES, 0, width, 0),
+        (2, 0, third // PIECES, 0, width, 0),
+        (2, third, 2 * third // PIECES, 0, width, 1),
+    )
+    far = (peers // PEERS - 1).bit_length()
+    vmem = pl.BlockSpec(memory_space=pltpu.VMEM)
+    steps = 3 + far
+    dma = pltpu.SemaphoreType.DMA
+
+    def wide(*shape):
+        return jax.ShapeDtypeStruct(shape, WIDE)
+
+    return pl.pallas_call(
+        functools.partial(last_sums_kernel, parts),
+        in_specs=[vmem] * 4,
+        out_specs=[vmem] * 6,
+        out_shape=[
+            wide(2, cols, depth), wide(cols, width), wide(cols, width),
+            wide(3, cols, width), wide(cols, width), wide(*rows.shape),
+        ],
+        scratch_shapes=peer_scratch(parts, [kv.shape, cross.shape, own.shape], far)
+        + [pltpu.VMEM((steps,) + rows.shape, WIDE)] * 2
+        + [dma((steps,)), dma((steps,))],
+        compiler_params=pltpu.CompilerParams(
+            collective_id=4, has_side_effects=True, vmem_limit_bytes=VMEM_BYTES
+        ),
+        name="last_sums",
+    )(kv, cross, own, rows)
+
+
+def start_kernel(x_ref, tail_ref, wkv_ref, own_ref, k_ref, v_ref, attn_ref, w_ref, y_ref, send, recv, local):
+    step = pl.program_id(0)
+    last = pl.num_programs(0) - 1
+    block, items, depth = x_ref.shape
+    cols = own_ref.shape[1]
+    kinds = own_ref.shape[0]
+    rows = kinds * cols // PEERS
+
+    def at(shard, peer, half):
+        per = cols // rows
+        first = shard * cols + (peer % per) * rows + (0 if half is None else half * (rows // 2))
+        return attn_ref.at[peer // per, pl.ds(pl.multiple_of(first, 16), rows if half is None else rows // 2)]
+
+    spread = Spread(at, send, recv, 0)
+    per = cols // rows
+    mine = own_ref.at[spread.peer // per, pl.ds(pl.multiple_of((spread.peer % per) * rows, 16), rows)]
+    steps = range(1, spread.shards)
+    here = pl.ds(pl.multiple_of(spread.tensor * cols, 16), cols)
+    own_copies = [
+        pltpu.make_async_copy(own_ref.at[c], attn_ref.at[c, here], local.at[c]) for c in range(kinds)
+    ]
+
+    @pl.when(step == 0)
+    def _():
+        greet(spread.targets())
+        for s in steps:
+            spread.along(s, mine).start()
+        for made in own_copies:
+            made.start()
+
+    @pl.when(step == 0)
+    def _():
+        low = 128
+        w_ref[:cols] = wkv_ref[0]
+        w_ref[cols : 2 * cols - low] = wkv_ref[1, low:]
+        w_ref[2 * cols - low :] = wkv_ref[1, :low]
+
+    def project(x, first, count):
+        y = mm_nt(x, w_ref[...])
+        for tile in range(y_ref.shape[0]):
+            y_ref[tile, : count * items] = y[:, tile * 128 : (tile + 1) * 128]
+        for item in range(items):
+            k_low, high, v_low = [
+                y_ref[tile, pl.ds(item, count, stride=items)].astype(NARROW) for tile in range(3)
+            ]
+            k_ref[item, first, :128] = k_low
+            k_ref[item, first, 128:] = high[:, : cols - 128]
+            v_ref[item, first, :128] = v_low
+            v_ref[item, first, 128:] = high[:, cols - 128 :]
+
+    project(
+        x_ref[...].reshape(block * items, depth),
+        pl.ds(pl.multiple_of(step * block, block), block),
+        block,
+    )
+
+    @pl.when(step == last)
+    def _():
+        count = tail_ref.shape[0]
+        project(
+            tail_ref[...].reshape(count * items, depth),
+            pl.ds(k_ref.shape[1] - count, count),
+            count,
+        )
+        for s in steps:
+            spread.along(s, mine).wait_recv()
+            spread.start_across(s)
+        for s in steps:
+            spread.start_onward(s)
+        for s in steps:
+            spread.start_last(s)
+        for s in steps:
+            spread.finish(s)
+            spread.along(s, mine).wait_send()
+        for made in own_copies:
+            made.wait()
+
+
+def start_layer(visual, wkv, own, shards):
+    span, items, depth = visual.shape
+    kinds, cols, width = own.shape
+    steps = 4
+    tail = span % (16 * steps)
+    block = (span - tail) // steps
+    out = pl.BlockSpec((items, span, cols), lambda i: (0, 0, 0))
+    shape = jax.ShapeDtypeStruct((items, span, cols), NARROW)
+    copies = Spread.COPIES * (shards - 1)
+    dma = pltpu.SemaphoreType.DMA
+    return pl.pallas_call(
+        start_kernel,
+        grid=(steps,),
+        in_specs=[
+            pl.BlockSpec((block, items, depth), lambda i: (i, 0, 0)),
+            pl.BlockSpec((tail, items, depth), lambda i: (span // tail - 1, 0, 0)),
+            pl.BlockSpec(wkv.shape, lambda i: (0, 0, 0)),
+            pl.BlockSpec(own.shape, lambda i: (0, 0, 0)),
+        ],
+        out_specs=[out, out, pl.BlockSpec(memory_space=pl.ANY)],
+        out_shape=[shape, shape, jax.ShapeDtypeStruct((kinds, shards * cols, width), NARROW)],
+        scratch_shapes=[
+            pltpu.VMEM((2 * cols, depth), NARROW),
+            pltpu.VMEM((2 * cols // 128, block * items, 128), WIDE),
+            dma((copies,)), dma((copies,)), dma((kinds,)),
+        ],
+        compiler_params=pltpu.CompilerParams(
+            collective_id=0, has_side_effects=True, vmem_limit_bytes=VMEM_BYTES
+        ),
+        name="start_layer",
+    )(visual, visual, wkv, own)
+
+
+def feed_copies(shards):
+    return 2 * Spread.COPIES * (shards - 1)
+
+
+def sum_and_spread_kernel(part, in_ref, out_ref, out, win_ref, wout_ref, buf_in, buf_mid, *rest):
+    sems, (send, recv) = rest[:6], rest[6:]
+    del in_ref, out_ref
+    chain = reduce_chain(part, out, buf_in, buf_mid, sems, part.shape[1])
+    shards = lax.axis_size("tensor")
+    base = Spread.COPIES * (shards - 1)
+    spreads = [
+        (Spread(eighth(ref), send, recv, n * base), s)
+        for s in range(1, shards)
+        for n, ref in enumerate((win_ref, wout_ref))
+    ]
+    chain[0](spreads[0][0].peer_targets())
+    for spread, s in spreads:
+        spread.start_across(s)
+    todo = list(spreads)
+    for t, run in enumerate(chain[1:-1]):
+        run()
+        if t >= 2 and t % 3 != 1 and todo:
+            spread, s = todo.pop(0)
+            spread.start_onward(s)
+    for spread, s in todo:
+        spread.start_onward(s)
+    chain[-1]()
+    for spread, s in spreads:
+        spread.start_last(s)
+    for spread, s in spreads:
+        spread.finish(s)
+
+
+def sum_and_spread(part, win, wout, ident):
+    rows, width = part.shape
+    steps = 8
+    shape = (2, steps, rows // (2 * steps), width)
+    vmem = pl.BlockSpec(memory_space=pltpu.VMEM)
+    hbm = pl.BlockSpec(memory_space=pl.ANY)
+    copies = feed_copies(win.shape[0])
+    dma = pltpu.SemaphoreType.DMA
+    total, win, wout = pl.pallas_call(
+        sum_and_spread_kernel,
+        in_specs=[vmem, hbm, hbm],
+        out_specs=[vmem, hbm, hbm],
+        out_shape=[
+            jax.ShapeDtypeStruct(shape, NARROW),
+            jax.ShapeDtypeStruct(win.shape, NARROW),
+            jax.ShapeDtypeStruct(wout.shape, NARROW),
+        ],
+        input_output_aliases={1: 1, 2: 2},
+        scratch_shapes=chain_scratch(steps, shape[2], width) + [dma((copies,)), dma((copies,))],
+        compiler_params=pltpu.CompilerParams(
+            collective_id=ident, has_side_effects=True, vmem_limit_bytes=VMEM_BYTES
+        ),
+        name="sum_and_spread",
+    )(part.reshape(shape), win, wout)
+    return total.reshape(rows, width), win, wout
+
+
 def labels_of(position, ends):
     place = position - NQ
     label = jnp.zeros_like(position)
@@ -102,9 +676,34 @@
 
 
 def self_forward_kernel(
-    lens_ref, x_ref, w_ref, gain_ref, shift_ref,
-    q_ref, k_ref, v_ref, p_ref, ctx_ref, res_ref, fq_ref, ft_ref,
+    lens_ref, x_ref, w_ref, gain_ref, shift_ref, in_ref, out_ref,
+    q_ref, k_ref, v_ref, p_ref, ctx_ref, res_ref, fq_ref, ft_ref, win_ref, wout_ref,
+    bounce, send, recv, local,
 ):
+    step = pl.program_id(0)
+    tensor = lax.axis_index("tensor")
+    shards = lax.axis_size("tensor")
+    hops, load = [], []
+    for n, (own, gathered) in enumerate(((in_ref, win_ref), (out_ref, wout_ref))):
+        spread = Spread(eighth(gathered), send, recv, n * Spread.COPIES * (shards - 1))
+        rows = own.shape[1] // PEERS
+        mine = own.at[0, pl.ds(pl.multiple_of(spread.peer * rows, 16), rows)]
+        hops += [spread.along(s, mine) for s in range(1, shards)]
+        load.append(pltpu.make_async_copy(own.at[0], bounce.at[n], local.at[n]))
+        hops.append(pltpu.make_async_copy(bounce.at[n], gathered.at[tensor], local.at[n]))
+
+    @pl.when(step == 0)
+    def _():
+        for made in load:
+            made.start()
+        greet(spread.along_targets())
+        for made in hops[: shards - 1] + hops[shards : 2 * shards - 1]:
+            made.start()
+        for made in load:
+            made.wait()
+        for made in (hops[shards - 1], hops[2 * shards - 1]):
+            made.start()
+
     span = NQ + TXT
     items = x_ref.shape[0] // span
     lanes = QUAD * HEAD
@@ -135,14 +734,21 @@
         fq_ref[item * NQ : (item + 1) * NQ] = first[item * span : item * span + NQ]
         ft_ref[item * TXT : (item + 1) * TXT] = first[item * span + NQ : (item + 1) * span]
 
-
-def self_forward(hidden, lens, weights, gain, shift):
+    @pl.when(step == pl.num_programs(0) - 1)
+    def _():
+        for made in hops:
+            made.wait()
+
+
+def self_forward(hidden, lens, weights, gain, shift, ffn_in, ffn_out, shards):
     rows, width = hidden.shape
     block = min(rows, 256)
     half = block // 2
     full = pl.BlockSpec((block, width), lambda i: (i, 0))
     halves = pl.BlockSpec((half, width), lambda i: (i, 0))
     low = jax.ShapeDtypeStruct((rows, width), NARROW)
+    hbm = pl.BlockSpec(memory_space=pl.ANY)
+    dma = pltpu.SemaphoreType.DMA
     return pl.pallas_call(
         self_forward_kernel,
         grid=(rows // block,),
@@ -152,22 +758,31 @@
             pl.BlockSpec(weights.shape, lambda i: (0, 0, 0)),
             pl.BlockSpec(gain.shape, lambda i: (0, 0)),
             pl.BlockSpec(shift.shape, lambda i: (0, 0)),
-        ],
-        out_specs=[full, full, full, full, full, full, halves, halves],
+            hbm, hbm,
+        ],
+        out_specs=[full, full, full, full, full, full, halves, halves, hbm, hbm],
         out_shape=[
             low, low, low, low, low,
             jax.ShapeDtypeStruct((rows, width), WIDE),
             jax.ShapeDtypeStruct((rows // 2, width), WIDE),
             jax.ShapeDtypeStruct((rows // 2, width), WIDE),
-        ],
-        compiler_params=pltpu.CompilerParams(vmem_limit_bytes=VMEM_BYTES),
+            jax.ShapeDtypeStruct((shards,) + ffn_in.shape[1:], NARROW),
+            jax.ShapeDtypeStruct((shards,) + ffn_out.shape[1:], NARROW),
+        ],
+        scratch_shapes=[
+            pltpu.VMEM((2,) + ffn_in.shape[1:], NARROW),
+            dma((feed_copies(shards),)), dma((feed_copies(shards),)), dma((2,)),
+        ],
+        compiler_params=pltpu.CompilerParams(
+            collective_id=3, has_side_effects=True, vmem_limit_bytes=VMEM_BYTES
+        ),
         name="self_forward",
-    )(lens, hidden, weights, gain, shift)
+    )(lens, hidden, weights, gain, shift, ffn_in, ffn_out)
 
 
 def self_backward_kernel(
     own_ref, x_ref, w_ref, gain_ref, res_ref, gq_ref, gt_ref, q_ref, k_ref, v_ref, p_ref, ctx_ref,
-    grad_ref, gqkv_ref, gout_ref, gain_out, shift_out,
+    grad_ref, grads_ref, gain_out, shift_out,
     down, dctx, dq, dk, dv, acc,
 ):
     span = NQ + TXT
@@ -219,7 +834,7 @@
     grad_ref[...] += mm(dq[...], w_ref[0]) + mm(dk[...], w_ref[1]) + mm(dv[...], w_ref[2])
 
     own = own_ref[0]
-    cols = gqkv_ref.shape[1]
+    cols = grads_ref.shape[0] // 4
     window = acc.shape[1]
     start = pl.multiple_of((own * cols) // 128 * 128, 128)
     here = pl.ds(start, window)
@@ -242,9 +857,8 @@
     @pl.when(step == pl.num_programs(0) - 1)
     def _():
         offset = pl.multiple_of(own * cols - start, 64)
-        for c in range(3):
-            gqkv_ref[c] = acc[c, pl.ds(offset, cols), :].astype(gqkv_ref.dtype)
-        gout_ref[...] = acc[3, pl.ds(offset, cols), :].astype(gout_ref.dtype)
+        for c in range(4):
+            grads_ref[c * cols : (c + 1) * cols] = acc[c, pl.ds(offset, cols), :].astype(NARROW)
 
 
 def self_backward(own, hidden, weights, gain, residue, grad_q, grad_t, q, k, v, p, ctx, cols):
@@ -266,14 +880,12 @@
         ],
         out_specs=[
             full,
-            pl.BlockSpec((3, cols, width), lambda i: (0, 0, 0)),
-            pl.BlockSpec((cols, width), lambda i: (0, 0)),
+            pl.BlockSpec((4 * cols, width), lambda i: (0, 0)),
             row, row,
         ],
         out_shape=[
             jax.ShapeDtypeStruct((rows, width), WIDE),
-            jax.ShapeDtypeStruct((3, cols, width), NARROW),
-            jax.ShapeDtypeStruct((cols, width), NARROW),
+            jax.ShapeDtypeStruct((4 * cols, width), NARROW),
             jax.ShapeDtypeStruct((1, width), WIDE),
             jax.ShapeDtypeStruct((1, width), WIDE),
         ],
@@ -282,31 +894,6 @@
         compiler_params=pltpu.CompilerParams(vmem_limit_bytes=VMEM_BYTES),
         name="self_backward",
     )(own, hidden, weights, gain, residue, grad_q, grad_t, q, k, v, p, ctx)
-
-
-def visual_forward_kernel(x_ref, w_ref, k_ref, v_ref):
-    x = x_ref[0]
-    k_ref[0] = mm_nt(x, w_ref[0]).astype(NARROW)
-    v_ref[0] = mm_nt(x, w_ref[1]).astype(NARROW)
-
-
-def visual_forward(visual, weights):
-    items, span, depth = visual.shape
-    cols = weights.shape[1]
-    out = pl.BlockSpec((1, span, cols), lambda i: (i, 0, 0))
-    shape = jax.ShapeDtypeStruct((items, span, cols), NARROW)
-    return pl.pallas_call(
-        visual_forward_kernel,
-        grid=(items,),
-        in_specs=[
-            pl.BlockSpec((1, span, depth), lambda i: (i, 0, 0)),
-            pl.BlockSpec(weights.shape, lambda i: (0, 0, 0)),
-        ],
-        out_specs=[out, out],
-        out_shape=[shape, shape],
-        compiler_params=pltpu.CompilerParams(vmem_limit_bytes=VMEM_BYTES),
-        name="visual_forward",
-    )(visual, weights)
 
 
 def cross_forward_kernel(x_ref, wq_ref, wo_ref, k_ref, v_ref, q_ref, p_ref, ctx_ref, part_ref):
@@ -361,9 +948,10 @@
 
 def cross_backward_kernel(
     down_ref, fq_ref, wq_ref, wo_ref, q_ref, k_ref, v_ref, p_ref, ctx_ref,
-    part_ref, dk_ref, dv_ref, gq_ref, go_ref, dctx, dq, acc,
+    part_ref, dkv_ref, grads_ref, dctx, dq, acc,
 ):
-    items = k_ref.shape[0]
+    items, span, cols = k_ref.shape
+    all_items = items * pl.num_programs(0)
     heads = q_ref.shape[1] // HEAD
     step = pl.program_id(0)
     dctx[...] = mm_nt(down_ref[...], wo_ref[...]).astype(NARROW)
@@ -375,8 +963,22 @@
         weighted = chances.astype(WIDE)
         inner = jnp.sum(grad_chances * weighted, axis=0, keepdims=True)
         scores = (weighted * (grad_chances - inner)).astype(NARROW)
-        dk_ref[item] = mm(scores, spread_heads(q_ref[rows], heads)).astype(NARROW)
-        dv_ref[item] = mm(chances, spread).astype(NARROW)
+        spread_q = spread_heads(q_ref[rows], heads)
+        none = jnp.zeros((heads * NQ, cols), NARROW)
+        both = mm(
+            jnp.concatenate([scores, chances], axis=1),
+            jnp.concatenate(
+                [
+                    jnp.concatenate([spread_q, none], axis=1),
+                    jnp.concatenate([none, spread[:, 128:], spread[:, :128]], axis=1),
+                ],
+                axis=0,
+            ),
+        )
+        for tile in range(dkv_ref.shape[0]):
+            dkv_ref[tile, pl.ds(step * items + item, span, stride=all_items)] = both[
+                :, tile * 128 : (tile + 1) * 128
+            ]
         dq[rows] = (gather_heads(mm_tn(scores, k_ref[item]), heads) * SCALE).astype(NARROW)
     part_ref[...] = mm(dq[...], wq_ref[...]).astype(NARROW)
     grad_q = mm_tn(dq[...], fq_ref[...].astype(NARROW))
@@ -394,8 +996,8 @@
 
     @pl.when(step == pl.num_programs(0) - 1)
     def _():
-        gq_ref[...] = acc[0].astype(gq_ref.dtype)
-        go_ref[...] = acc[1].astype(go_ref.dtype)
+        grads_ref[:cols] = acc[0].astype(grads_ref.dtype)
+        grads_ref[cols:] = acc[1].astype(grads_ref.dtype)
 
 
 def cross_backward(down, rows_q, wq, wo, q, k, v, p, ctx):
@@ -412,8 +1014,9 @@
         return pl.BlockSpec((step, span, lanes), lambda i: (i, 0, 0))
 
     whole = pl.BlockSpec(wq.shape, lambda i: (0, 0))
-    low = jax.ShapeDtypeStruct((items, span, cols), NARROW)
-    grads = jax.ShapeDtypeStruct((cols, width), NARROW)
+    tiles = (2 * cols // 128, items * span, 128)
+    keyed = pl.BlockSpec(tiles, lambda i: (0, 0, 0))
+    wide = jax.ShapeDtypeStruct(tiles, WIDE)
     return pl.pallas_call(
         cross_backward_kernel,
         grid=(items // step,),
@@ -421,8 +1024,12 @@
             by_rows(width), by_rows(width), whole, whole,
             by_rows(cols), by_items(cols), by_items(cols), by_items(heads * NQ), by_rows(cols),
         ],
-        out_specs=[by_rows(width), by_items(cols), by_items(cols), whole, whole],
-        out_shape=[jax.ShapeDtypeStruct((rows, width), NARROW), low, low, grads, grads],
+        out_specs=[by_rows(width), keyed, pl.BlockSpec((2 * cols, width), lambda i: (0, 0))],
+        out_shape=[
+            jax.ShapeDtypeStruct((rows, width), NARROW),
+            wide,
+            jax.ShapeDtypeStruct((2 * cols, width), NARROW),
+        ],
         scratch_shapes=[
             pltpu.VMEM((block, cols), NARROW),
             pltpu.VMEM((block, cols), NARROW),
@@ -433,63 +1040,50 @@
     )(down, rows_q, wq, wo, q, k, v, p, ctx)
 
 
-def visual_backward_kernel(x_ref, dk_ref, dv_ref, out_ref, acc, tail_x, tail_k, tail_v):
+def visual_backward_kernel(x_ref, tail_ref, d_ref, rest_ref, out_ref, acc):
     step = pl.program_id(0)
-    span = x_ref.shape[1]
-    even = span // 128 * 128
-    x = x_ref[0, :even]
-    part_k = mm_tn(dk_ref[0, :even], x)
-    part_v = mm_tn(dv_ref[0, :even], x)
+    block, items, depth = x_ref.shape
+
+    def product(ref, x):
+        grads = jnp.concatenate([ref[tile].astype(NARROW) for tile in range(ref.shape[0])], axis=1)
+        return mm_tn(grads, x.reshape(-1, depth))
+
+    part = product(d_ref, x_ref[...])
 
     @pl.when(step == 0)
     def _():
-        acc[0] = part_k
-        acc[1] = part_v
-        tail_x[...] = jnp.zeros_like(tail_x)
-        tail_k[...] = jnp.zeros_like(tail_k)
-        tail_v[...] = jnp.zeros_like(tail_v)
+        acc[...] = part + product(rest_ref, tail_ref[...])
 
     @pl.when(step > 0)
     def _():
-        acc[0] += part_k
-        acc[1] += part_v
-
-    if span > even:
-        here = pl.ds(step * (span - even), span - even)
-        tail_x[here] = x_ref[0, even:].astype(WIDE)
-        tail_k[here] = dk_ref[0, even:].astype(WIDE)
-        tail_v[here] = dv_ref[0, even:].astype(WIDE)
+        acc[...] += part
 
     @pl.when(step == pl.num_programs(0) - 1)
     def _():
-        x = tail_x[...].astype(NARROW)
-        out_ref[0] = (acc[0] + mm_tn(tail_k[...].astype(NARROW), x)).astype(out_ref.dtype)
-        out_ref[1] = (acc[1] + mm_tn(tail_v[...].astype(NARROW), x)).astype(out_ref.dtype)
-
-
-def visual_backward(visual, dk, dv):
-    items, span, depth = visual.shape
-    cols = dk.shape[2]
-    tail = max(16, (items * (span % 128) + 15) // 16 * 16)
+        out_ref[...] = acc[...].astype(out_ref.dtype)
+
+
+def visual_backward(visual, grads):
+    span, items, depth = visual.shape
+    tiles = grads.shape[0]
+    steps = 4
+    tail = span % (16 * steps)
+    block = (span - tail) // steps
     return pl.pallas_call(
         visual_backward_kernel,
-        grid=(items,),
+        grid=(steps,),
         in_specs=[
-            pl.BlockSpec((1, span, depth), lambda i: (i, 0, 0)),
-            pl.BlockSpec((1, span, cols), lambda i: (i, 0, 0)),
-            pl.BlockSpec((1, span, cols), lambda i: (i, 0, 0)),
-        ],
-        out_specs=pl.BlockSpec((2, cols, depth), lambda i: (0, 0, 0)),
-        out_shape=jax.ShapeDtypeStruct((2, cols, depth), NARROW),
-        scratch_shapes=[
-            pltpu.VMEM((2, cols, depth), WIDE),
-            pltpu.VMEM((tail, depth), WIDE),
-            pltpu.VMEM((tail, cols), WIDE),
-            pltpu.VMEM((tail, cols), WIDE),
-        ],
+            pl.BlockSpec((block, items, depth), lambda i: (i, 0, 0)),
+            pl.BlockSpec((tail, items, depth), lambda i: (span // tail - 1, 0, 0)),
+            pl.BlockSpec((tiles, block * items, 128), lambda i: (0, i, 0)),
+            pl.BlockSpec((tiles, tail * items, 128), lambda i: (0, span // tail - 1, 0)),
+        ],
+        out_specs=pl.BlockSpec((tiles * 128, depth), lambda i: (0, 0)),
+        out_shape=jax.ShapeDtypeStruct((tiles * 128, depth), NARROW),
+        scratch_shapes=[pltpu.VMEM((tiles * 128, depth), WIDE)],
         compiler_params=pltpu.CompilerParams(vmem_limit_bytes=VMEM_BYTES),
         name="visual_backward",
-    )(visual, dk, dv)
+    )(visual, visual, grads, grads)
 
 
 def feed_kernel(
@@ -598,205 +1192,6 @@
     )(own, rows_q, cross, win, wout, gain, shift, cotangent)
 
 
-MESH = pl.DeviceIdType.MESH
-PEERS = 8
-
-
-def flip(index, bit):
-    return index + bit - 2 * bit * ((index // bit) % 2)
-
-
-def greet(targets):
-    barrier = pltpu.get_barrier_semaphore()
-    for target in targets:
-        pl.semaphore_signal(barrier, inc=1, device_id=target, device_id_type=MESH)
-    pl.semaphore_wait(barrier, len(targets))
-
-
-def remote(src, dst, send, recv, target):
-    return pltpu.make_async_remote_copy(
-        src_ref=src, dst_ref=dst, send_sem=send, recv_sem=recv, device_id=target, device_id_type=MESH
-    )
-
-
-class Spread:
-    def __init__(self, at, own_at, send, recv):
-        self.at, self.own_at, self.send, self.recv = at, own_at, send, recv
-        self.dp, self.tensor = lax.axis_index("dp"), lax.axis_index("tensor")
-        self.shards = lax.axis_size("tensor")
-        self.peer = self.dp % PEERS
-        self.index = 0
-        self.open = []
-
-    def targets(self):
-        along = [(self.dp, (self.tensor + s) % self.shards) for s in range(1, self.shards)]
-        return along + [(flip(self.dp, bit), self.tensor) for bit in (2, 4, 1)]
-
-    def copy(self, src, dst, target):
-        self.index += 1
-        made = remote(src, dst, self.send.at[self.index - 1], self.recv.at[self.index - 1], target)
-        made.start()
-        self.open.append(made)
-        return made
-
-    def along_tensor(self):
-        return [
-            self.copy(
-                self.own_at(self.peer),
-                self.at(self.tensor, self.peer, None),
-                (self.dp, (self.tensor + s) % self.shards),
-            )
-            for s in range(1, self.shards)
-        ]
-
-    def others(self):
-        return [(self.tensor + self.shards - s) % self.shards for s in range(1, self.shards)]
-
-    def exchange(self, bit, peers, half, shards=None):
-        target = (flip(self.dp, bit), self.tensor)
-        return [
-            self.copy(self.at(shard, peer, half), self.at(shard, peer, half), target)
-            for shard in (self.others() if shards is None else shards)
-            for peer in peers
-        ]
-
-    @staticmethod
-    def arrived(copies):
-        for made in copies:
-            made.wait_recv()
-
-    def finish(self):
-        for made in self.open:
-            made.wait_send()
-
-
-def spread_copies(shards):
-    return (shards - 1) * (1 + 2 + 4 + 4)
-
-
-def reduce_chain(part, out, buf_in, buf_mid, sems, steps):
-    send_pair, send_mid, send_out, recv_pair, recv_mid, recv_out = sems
-    dp, tensor = lax.axis_index("dp"), lax.axis_index("tensor")
-    side = tensor // 2
-    other = 1 - side
-    pair = (dp, tensor + 1 - 2 * (tensor % 2))
-    across = (dp, 3 - tensor)
-    middle = (tensor + side) % 2 == 1
-
-    def to_pair(half, c):
-        return remote(part.at[half, c], buf_in.at[half, c], send_pair.at[half, c], recv_pair.at[half, c], pair)
-
-    def to_mid(c):
-        return remote(buf_mid.at[0, c], buf_mid.at[1, c], send_mid.at[c], recv_mid.at[c], across)
-
-    def final_across(half, c):
-        return remote(out.at[half, c], out.at[half, c], send_out.at[0, c], recv_out.at[half, c], across)
-
-    def final_pair(half, c):
-        return remote(out.at[half, c], out.at[half, c], send_out.at[1 + (0 if half is side else 1), c], recv_out.at[half, c], pair)
-
-    def wide(ref, *at):
-        return ref[at].astype(WIDE)
-
-    def begin():
-        @pl.when(middle)
-        def _():
-            greet([pair, across])
-
-        @pl.when(jnp.logical_not(middle))
-        def _():
-            greet([pair])
-            for c in range(steps):
-                to_pair(other, c).start()
-                to_pair(side, c).start()
-
-    def first(c):
-        to_pair(other, c).wait_recv()
-        buf_mid[0, c] = (wide(buf_in, other, c) + wide(part, other, c)).astype(buf_mid.dtype)
-        to_mid(c).start()
-
-    def second(c):
-        to_pair(side, c).wait_recv()
-        to_mid(c).wait_recv()
-        out[side, c] = (wide(buf_in, side, c) + wide(buf_mid, 1, c) + wide(part, side, c)).astype(out.dtype)
-        final_across(side, c).start()
-        final_pair(side, c).start()
-
-    def third(c):
-        final_across(other, c).wait_recv()
-        final_pair(other, c).start()
-
-    def step(t):
-        @pl.when(middle)
-        def _():
-            if t < steps:
-                first(t)
-            if 0 <= t - 1 < steps:
-                second(t - 1)
-            if 0 <= t - 2 < steps:
-                third(t - 2)
-
-    def end():
-        @pl.when(middle)
-        def _():
-            for c in range(steps):
-                to_mid(c).wait_send()
-                final_across(side, c).wait_send()
-                final_pair(side, c).wait_send()
-                final_pair(other, c).wait_send()
-
-        @pl.when(jnp.logical_not(middle))
-        def _():
-            for c in range(steps):
-                to_pair(other, c).wait_send()
-                to_pair(side, c).wait_send()
-                final_pair(other, c).wait_recv()
-                final_pair(side, c).wait_recv()
-
-    return [begin] + [functools.partial(step, t) for t in range(steps + 2)] + [end]
-
-
-def chain_scratch(steps, rows, width):
-    dma = pltpu.SemaphoreType.DMA
-    return [
-        pltpu.VMEM((2, steps, rows, width), NARROW),
-        pltpu.VMEM((2, steps, rows, width), NARROW),
-        dma((2, steps)), dma((steps,)), dma((3, steps)),
-        dma((2, steps)), dma((steps,)), dma((2, steps)),
-    ]
-
-
-def sum_shards_kernel(part, out, buf_in, buf_mid, *sems):
-    for run in reduce_chain(part, out, buf_in, buf_mid, sems, part.shape[1]):
-        run()
-
-
-def sum_shards(part, ident):
-    rows, width = part.shape
-    steps = 8
-    shape = (2, steps, rows // (2 * steps), width)
-    vmem = pl.BlockSpec(memory_space=pltpu.VMEM)
-    return pl.pallas_call(
-        sum_shards_kernel,
-        in_specs=[vmem],
-        out_specs=vmem,
-        out_shape=jax.ShapeDtypeStruct(shape, NARROW),
-        scratch_shapes=chain_scratch(steps, shape[2], width),
-        compiler_params=pltpu.CompilerParams(
-            collective_id=ident, has_side_effects=True, vmem_limit_bytes=VMEM_BYTES
-        ),
-        name="sum_shards",
-    )(part.reshape(shape)).reshape(rows, width)
-
-
-def gather_shards(shard):
-    peers = lax.axis_size("dp")
-    rows = shard.shape[0] // peers
-    own = lax.dynamic_slice_in_dim(shard, lax.axis_index("dp") * rows, rows, axis=0)
-    whole = lax.all_gather(own, ("tensor", "dp"), axis=0, tiled=True)
-    return whole.reshape((whole.shape[0] // shard.shape[0],) + shard.shape)
-
-
 def sum_items(values):
     return lax.psum([v.astype(NARROW) for v in values], "dp")
 
@@ -824,19 +1219,15 @@
     own = lax.axis_index("tensor").reshape((1,)).astype(jnp.int32)
     shards = lax.axis_size("tensor")
 
+    visual = jnp.swapaxes(visual_feats, 0, 1)
+    cross_wq = jnp.swapaxes(cross_query, 0, 1)
     attn_own = jnp.concatenate([jnp.swapaxes(self_qkv, 1, 2), self_out[None]], axis=0)
-    attn = gather_shards(attn_own.reshape(4 * cols, width)).reshape(shards, 4, cols, width)
-    attn = jnp.swapaxes(attn, 0, 1).reshape(4, shards * cols, width)
-    feed = gather_shards(jnp.concatenate([ffn_in[0], ffn_out[0]], axis=0))
-    win_q, wout_q = feed[:, :width], feed[:, width:]
-
-    cross_wq = jnp.swapaxes(cross_query, 0, 1)
-    cross_k, cross_v = visual_forward(visual_feats, jnp.swapaxes(cross_kv, 1, 2))
-    q, k, v, p, ctx, residue, first_q, first_t = self_forward(
-        hidden_in, caption_lengths, attn, norm_gain, norm_shift
+    cross_k, cross_v, attn = start_layer(visual, jnp.swapaxes(cross_kv, 1, 2), attn_own, shards)
+    q, k, v, p, ctx, residue, first_q, first_t, win_q, wout_q = self_forward(
+        hidden_in, caption_lengths, attn, norm_gain, norm_shift, ffn_in, ffn_out, shards
     )
     cq, cp, cctx, cross_part = cross_forward(first_q, cross_wq, cross_out, cross_k, cross_v)
-    cross_sum = sum_shards(cross_part, 1)
+    cross_sum, win_q, wout_q = sum_and_spread(cross_part, win_q, wout_q, 1)
 
     cot = out_grad.reshape(items, span, width)
     cot_q = cot[:, :NQ].reshape(items * NQ, width)
@@ -853,27 +1244,31 @@
     grad_t = norm_back(unit, inverse, norm_gain[3:4], cot_t)
     top_t = grad_t.astype(NARROW)
     dpre_t = (mm_nt(top_t, ffn_out[1]) * slope_t).astype(NARROW)
-    grad_t = grad_t + lax.psum(mm_nt(dpre_t, ffn_in[1]).astype(NARROW), "tensor").astype(WIDE)
+    back_t = mm_nt(dpre_t, ffn_in[1]).astype(NARROW)
+    back_t, cross_sum = lax.optimization_barrier((back_t, cross_sum))
+    back_t = lax.psum(back_t, "tensor")
 
     out_q, grad_second, down_q, low_q, top_q, act_q, dpre_q, gain_pair, shift_pair = feed_forward_back(
         own, first_q, cross_sum, win_q, wout_q, norm_gain, norm_shift, cot_q
     )
-    back_part, dk, dv, g_cq, g_co = cross_backward(
+    back_part, dkv, g_cross = cross_backward(
         down_q, first_q, cross_wq, cross_out, cq, cross_k, cross_v, cp, cctx
     )
     grad_q = grad_second + sum_shards(back_part, 2).astype(WIDE)
     g_in = jnp.stack([mm_tn(low_q, dpre_q), mm_tn(low_t, dpre_t)])
     g_out = jnp.stack([mm_tn(act_q, top_q), mm_tn(act_t, top_t)])
-    g_kv = visual_backward(visual_feats, dk, dv)
-    grad_hidden, g_qkv, g_so, gain_first, shift_first = self_backward(
+    g_in, g_out = sum_items([g_in, g_out])
+    g_kv = visual_backward(visual, dkv)
+    grad_t = grad_t + back_t.astype(WIDE)
+    grad_hidden, g_self, gain_first, shift_first = self_backward(
         own, hidden_in, attn, norm_gain, residue, grad_q, grad_t, q, k, v, p, ctx, cols
     )
     out = jnp.concatenate(
         [out_q.reshape(items, NQ, width), out_t.reshape(items, TXT, width)], axis=1
     ).reshape(rows, width)
     gains = jnp.concatenate([gain_first, gain_pair, gain_t, shift_first, shift_pair, shift_t])
-    sums = sum_items([g_in, g_out, g_kv, g_cq, g_co, g_qkv, g_so, gains])
-    g_in, g_out, g_kv, g_cq, g_co, g_qkv, g_so, gains = [s.astype(WIDE) for s in sums]
+    g_kv, g_cq, g_co, g_qkv, g_so, gains = last_sums(g_kv, g_cross, g_self, gains, lax.axis_size("dp"))
+    g_in, g_out = g_in.astype(WIDE), g_out.astype(WIDE)
     return (
         out,
         grad_hidden,

time: 586 us -> 373 us (0.64)
  waiting for transfers between devices: 248 us -> 0.07 us
  Pallas kernels: 223 us -> 306 us
  blocking collectives: 23.4 us -> 0 us
  local copies, waits for them, and re-layouts: 35.6 us -> 15.7 us
  other arithmetic: 28.3 us -> 21.9 us
    all_gather x2 -> x0, waiting for transfers between devices: 113 us -> none  [gather_shards(): whole = lax.all_gather(own, ('tensor', 'dp'), axis=0, tiled=True)]
    pallas_call x2 -> x4, Pallas kernels: 34.9 us -> 148 us  [the longest x1 54 us: sum_and_spread(): pl.pallas_call(sum_and_spread_kernel, in_specs=[vmem, hbm, hbm], out_spec...]
    psum x1, waiting for transfers between devices: 92.8 us -> 0.01 us  [sum_items(): return lax.psum([v.astype(NARROW) for v in values], 'dp')]
    psum x1, waiting for transfers between devices: 41.4 us -> 0.02 us  [on_device(): lax.psum(mm(act_t, ffn_out[1]).astype(NARROW), 'tensor').astype(WIDE)]
    pallas_call x2 -> x1, Pallas kernels: 71.8 us -> 32.7 us  [sum_shards(): pl.pallas_call(sum_shards_kernel, in_specs=[vmem], out_specs=vmem, out_sh...]
    psum x1 -> x0, blocking collectives: 23.4 us -> none  [sum_items(): return lax.psum([v.astype(NARROW) for v in values], 'dp')]
    unnamed x66 -> x56, local copies, waits for them, and re-layouts: 18.5 us -> 11.2 us
    slice x1, local copies, waits for them, and re-layouts: 8.1 us -> 0.95 us  [on_device(): cot_q = cot[:, :NQ].reshape(items * NQ, width)]
  transfers between devices with their start and end apart: 5 -> 3, of which waited for: 4 -> 0; matrix products, arithmetic and copies ran while one was open for 4% -> 5% of each run, Pallas kernels for 11% -> 63%
where the time goes in v2:
time: 373 us; the launch traced here: 372 us
  Pallas kernels  306 us (82%)
  other arithmetic  21.9 us (6%)
  local copies, waits for them, and re-layouts  15.7 us (4%)
  between operations  14 us (4%)
  matrix products  13.7 us (4%)
    pallas_call x1, Pallas kernels, sum_and_spread(): pl.pallas_call(sum_and_spread_kernel, in_specs=[vmem, hbm, hbm], out_spec...  54 us
    pallas_call x1, Pallas kernels, last_sums(): pl.pallas_call(functools.partial(last_sums_kernel, parts), in_specs=[vmem...  44.7 us
    pallas_call x1, Pallas kernels, start_layer(): pl.pallas_call(start_kernel, grid=(steps,), in_specs=[pl.BlockSpec((block...  37.9 us
    pallas_call x1, Pallas kernels, feed_forward_back(): pl.pallas_call(feed_kernel, grid=(2 * chunks,), in_specs=[pl.BlockSpec(me...  34.6 us
    pallas_call x1, Pallas kernels, self_backward(): pl.pallas_call(self_backward_kernel, grid=(rows // block,), in_specs=[pl....  33.6 us
    pallas_call x1, Pallas kernels, self_forward(): pl.pallas_call(self_forward_kernel, grid=(rows // block,), in_specs=[pl.B...  33.5 us
    pallas_call x1, Pallas kernels, sum_shards(): pl.pallas_call(sum_shards_kernel, in_specs=[vmem], out_specs=vmem, out_sh...  32.7 us
    pallas_call x1, Pallas kernels, cross_backward(): pl.pallas_call(cross_backward_kernel, grid=(items // step,), in_specs=[by...  15.7 us
  transfers between devices with their start and end apart: 3, of which 0 were waited for; matrix products, arithmetic and copies ran while one was open for 5% of the time, Pallas kernels for 63%

profile of v2, /device:TPU:0, one launch (start us, length us, event | category | flops | bytes accessed | tf_op | source)
XLA Modules:
  0.0 371.9 jit_solution(444782992871623108)
XLA Ops:
  7.2 0.0 all-reduce.5.cloned.1.call-start
  7.2 1.4 copy.26.lens_ref
  8.6 2.4 pad_maximum_fusion.3.own_ref
  11.0 37.9 %start_layer.1 = (bf16[16,257,192]{2,1,0:T(8,128)(2,1)}, bf16[16,257,192]{2,1,0:T(8,128)(2,1)}, bf16[4,768,768]{2,1,0:T(8,128)(2,1)}) custom-call(bf16[257,16,1408]{2,1,0:T(8,128)(2,1)} %bitcast.63, bf16[257,16,1408]{2,1,0:T(8,128)(2,1)} %bitcast.64, bf16[2,192,1408]{2,1,0:T(8,128)(2,1)} %bitcast.78, bf16[4,192,768]{2,1,0:T(8,128)(2,1)} %pad_maximum_fusion.3.own_ref), custom_call_target="tpu_custom_call" | custom-call | tf_op jit(solution)/shard_map/start_layer/pallas_call | solution.py:576
  48.9 0.0 copy-start.3
  48.9 33.5 %self_forward.1 = (bf16[1024,768]{1,0:T(8,128)(2,1)}, bf16[1024,768]{1,0:T(8,128)(2,1)}, bf16[1024,768]{1,0:T(8,128)(2,1)}, bf16[1024,768]{1,0:T(8,128)(2,1)}, b...) custom-call(s32[16,4]{1,0:T(8,128)} %copy.26.lens_ref, ...), custom_call_target="tpu_custom_call" | custom-call | tf_op jit(solution)/shard_map/self_forward/pallas_call | solution.py:752
  82.3 0.0 copy-start.11
  82.4 3.5 multiply_convert_fusion
  85.9 0.9 copy-done.6
  86.8 1.7 convolution_convert_fusion.5
  88.4 0.0 all-reduce.5.cloned.1.call-update
  88.5 0.0 all-reduce.7.cloned.1.call-start
  88.5 0.9 slice.36
  89.5 0.7 slice_reduce_fusion
  90.2 0.4 convert_reduce_fusion
  90.6 0.1 div.17
  90.7 8.3 %cross_forward.1 = (bf16[512,192]{1,0:T(8,128)(2,1)}, bf16[16,257,96]{2,1,0:T(8,128)(2,1)}, bf16[512,192]{1,0:T(8,128)(2,1)}, bf16[512,768]{1,0:T(8,128)(2,1)}) custom-call(f32[512,768]{1,0:T(8,128)} %get-tuple-element.56.x_ref.fq_ref, bf16[192,768]{1,0:T(8,128)(2,1)} %bitcast.76, bf16[192,768]{1,0:T(8,128)(2,1)} %wo_ref.3, ...), custom_call_target="tpu_custom_call" | custom-call | tf_op jit(solution)/shard_map/cross_forward/pallas_call | solution.py:928
  99.0 54.0 %sum_and_spread.1 = (bf16[2,8,32,768]{3,2,1,0:T(8,128)(2,1)}, bf16[4,768,768]{2,1,0:T(8,128)(2,1)}, bf16[4,768,768]{2,1,0:T(8,128)(2,1)}) custom-call(bf16[2,8,32,768]{3,2,1,0:T(8,128)(2,1)} %bitcast.81, bf16[4,768,768]{2,1,0:T(8,128)(2,1)} %get-tuple-element.61.in_ref, ...), custom_call_target="tpu_custom_call", output_to_operand_aliasing={{1}: (1, {}), {2}: (2, {})} | custom-call | tf_op jit(solution)/shard_map/sum_and_spread/pallas_call | solution.py:640
  153.0 0.0 all-reduce.5.cloned.1.call-done
  153.0 1.4 fusion.30
  154.4 0.3 multiply_reduce_fusion
  154.7 0.7 fusion.12
  155.4 0.7 copy-done.2
  156.1 1.5 fusion.9
  157.6 0.4 copy-done.12
  158.0 0.5 copy-done.15
  158.5 1.1 fusion.5
  159.7 0.0 copy-start.4
  159.7 1.8 fusion.14
  161.5 1.7 convolution_convert_fusion.4
  163.2 0.0 all-reduce.7.cloned.1.call-update
  163.2 0.0 all-reduce.9.cloned.1.call-start
  163.3 34.6 %feed_query.1 = (bf16[512,768]{1,0:T(8,128)(2,1)}, f32[512,768]{1,0:T(8,128)}, bf16[512,768]{1,0:T(8,128)(2,1)}, bf16[512,768]{1,0:T(8,128)(2,1)}, bf16[512,768]...) custom-call(s32[1]{0:T(128)} %bitcast.own_ref, ...), custom_call_target="tpu_custom_call" | custom-call | tf_op jit(solution)/shard_map/feed_query/pallas_call | solution.py:1167
  197.9 2.3 fusion.13
  200.2 1.6 pad_maximum_fusion
  201.8 0.3 copy-done.24
  202.1 0.8 fusion.15
  203.0 0.3 copy-done.7
  203.3 0.8 fusion.16
  204.1 1.6 pad_maximum_fusion.1
  205.7 0.0 all-reduce.9.cloned.1.call-update
  205.8 15.7 %cross_backward.1 = (bf16[512,768]{1,0:T(8,128)(2,1)}, f32[3,4112,128]{2,1,0:T(8,128)}, bf16[384,768]{1,0:T(8,128)(2,1)}) custom-call(bf16[512,768]{1,0:T(8,128)(2,1)} %get-tuple-element.70.down_ref, f32[512,768]{1,0:T(8,128)} %get-tuple-element.56.x_ref.fq_ref, bf16[192,768]{1,0:T(8,128)(2,1)} %bitcast.77, bf16[192,768]{1,0:T(8,128)(2,1)} %wo_ref.3, ...), custom_call_target="tpu_custom_call" | custom-call | tf_op jit(solution)/shard_map/cross_backward/pallas_call | solution.py:1020
  221.5 32.7 %sum_shards.1 = bf16[2,8,32,768]{3,2,1,0:T(8,128)(2,1)} custom-call(bf16[2,8,32,768]{3,2,1,0:T(8,128)(2,1)} %bitcast.82), custom_call_target="tpu_custom_call" | custom-call | tf_op jit(solution)/shard_map/sum_shards/pallas_call | solution.py:293
  254.2 11.4 %visual_backward.1.kv_ref = bf16[384,1408]{1,0:T(8,128)(2,1)} custom-call(bf16[257,16,1408]{2,1,0:T(8,128)(2,1)} %bitcast.65, bf16[257,16,1408]{2,1,0:T(8,128)(2,1)} %bitcast.66, f32[3,4112,128]{2,1,0:T(8,128)} %get-tuple-element.82.d_ref.rest_ref, f32[3,4112,128]{2,1,0:T(8,128)} %get-tuple-element.82.d_ref.rest_ref), custom_call_target="tpu_custom_call" | custom-call | tf_op jit(solution)/shard_map/visual_backward/pallas_call | solution.py:1072
  265.6 0.0 copy-start.16
  265.6 1.3 pad_maximum_fusion.2
  266.8 0.1 copy-done.9
  266.9 0.9 copy-done.16
  267.8 1.4 convert_add_fusion.gq_ref
  269.2 2.4 convert_add_fusion.1.gt_ref
  271.6 33.6 %self_backward.1 = (f32[1024,768]{1,0:T(8,128)}, bf16[768,768]{1,0:T(8,128)(2,1)}, f32[1,768]{1,0:T(1,128)}, f32[1,768]{1,0:T(1,128)}) custom-call(s32[1]{0:T(128)} %bitcast.own_ref, bf16[1024,768]{1,0:T(8,128)(2,1)} %x_ref.3, bf16[4,768,768]{2,1,0:T(8,128)(2,1)} %get-tuple-element.55.w_ref, f32[4,768]{1,0:T(4,128)} %gain_ref.5, ...), custom_call_target="tpu_custom_call" | custom-call | tf_op jit(solution)/shard_map/self_backward/pallas_call | solution.py:871
  305.2 1.3 concatenate.11.rows_ref
  306.6 44.7 %last_sums.1 = (f32[2,192,1408]{2,1,0:T(8,128)}, f32[192,768]{1,0:T(8,128)}, f32[192,768]{1,0:T(8,128)}, f32[3,192,768]{2,1,0:T(8,128)}, f32[192,768]{1,0:T(8,128)}, /*index=5*/f32[8,768]{1,0:T(8,128)}) custom-call(bf16[384,1408]{1,0:T(8,128)(2,1)} %visual_backward.1.kv_ref, bf16[384,768]{1,0:T(8,128)(2,1)} %get-tuple-element.83.cross_ref, ...), custom_call_target="tpu_custom_call" | custom-call | tf_op jit(solution)/shard_map/last_sums/pallas_call | solution.py:470
  351.3 1.4 fusion.31
  352.7 4.4 %convert_element_type.65 = f32[2,768,768]{2,1,0:T(8,128)} convert(bf16[2,768,768]{2,1,0:T(8,128)(2,1)} %get-tuple-element.103) | non-fusion elementwise | flops 1179648 | bytes 7077888 | tf_op jit(solution)/shard_map/convert_element_type | solution.py:1271
  357.1 2.5 convert_element_type.66
  359.7 1.2 copy.38
  360.9 0.2 copy-done.20
  361.1 0.8 copy.39
  361.9 0.8 copy.40
  362.7 0.3 copy-done.13
  363.0 1.3 copy.41
  364.4 0.1 copy-done.18
  364.5 0.8 copy.42
  (43 shorter events, 0.1 us)
Async XLA Ops:
  7.2 145.9 %all-reduce.5.cloned.1.call-start = ((), (), s32[]{:S(2)}) async-start(), calls=%async_computation | async-start | bytes 1572864 | tf_op jit(solution)/shard_map/psum | solution.py:1239
  48.9 33.5 %copy-start.3 = (bf16[2,768,768]{2,1,0:T(8,128)(2,1)S(1)}, bf16[2,768,768]{2,1,0:T(8,128)(2,1)}, u32[]{:S(2)}) copy-start(bf16[2,768,768]{2,1,0:T(8,128)(2,1)} %in_ref.1) | copy-start | bytes 7077892
  82.3 4.4 %copy-start.11 = (bf16[2,768,768]{2,1,0:T(8,128)(2,1)S(1)}, bf16[2,768,768]{2,1,0:T(8,128)(2,1)}, u32[]{:S(2)}) copy-start(bf16[2,768,768]{2,1,0:T(8,128)(2,1)} %out_ref.1) | copy-start | bytes 7077892
  85.9 0.9 copy-start.6
  86.8 1.7 copy-start.1
  88.5 180.7 %all-reduce.7.cloned.1.call-start = ((), (), s32[]{:S(2)}) async-start(), calls=%async_computation.1 | async-start | bytes 1572864 | tf_op jit(solution)/shard_map/psum | solution.py:1249
  99.0 54.1 %copy-start = (f32[512,768]{1,0:T(8,128)S(1)}, f32[512,768]{1,0:T(8,128)}, u32[]{:S(2)}) copy-start(f32[512,768]{1,0:T(8,128)} %get-tuple-element.57) | copy-start | bytes 4718596
  154.7 1.4 copy-start.2
  156.1 1.9 copy-start.12
  156.1 2.4 copy-start.15
  159.7 1.9 copy-start.4
  163.2 189.5 %all-reduce.9.cloned.1.call-start = ((), (), s32[]{:S(2)}) async-start(), calls=%async_computation.2 | async-start | bytes 9437184 | tf_op jit(solution)/shard_map/psum | solution.py:1196
  197.9 2.3 copy-start.5
  200.2 1.6 copy-start.23
  200.2 2.0 copy-start.24
  202.1 1.1 copy-start.7
  254.2 11.4 %copy-start.8 = (bf16[512,768]{1,0:T(8,128)(2,1)S(1)}, bf16[512,768]{1,0:T(8,128)(2,1)}, u32[]{:S(2)}) copy-start(bf16[512,768]{1,0:T(8,128)(2,1)} %get-tuple-element.108) | copy-start | bytes 2359300
  254.2 11.4 %copy-start.17 = (bf16[512,768]{1,0:T(8,128)(2,1)S(1)}, bf16[512,768]{1,0:T(8,128)(2,1)}, u32[]{:S(2)}) copy-start(bf16[512,768]{1,0:T(8,128)(2,1)} %get-tuple-element.67) | copy-start | bytes 2359300
  265.6 1.3 copy-start.9
  265.6 2.2 copy-start.16
  271.6 33.6 %copy-start.21 = (f32[2,768]{1,0:T(2,128)S(1)}, f32[2,768]{1,0:T(2,128)}, u32[]{:S(2)}) copy-start(f32[2,768]{1,0:T(2,128)} %get-tuple-element.86) | copy-start | bytes 18436
  271.6 33.6 %copy-start.22 = (f32[2,768]{1,0:T(2,128)S(1)}, f32[2,768]{1,0:T(2,128)}, u32[]{:S(2)}) copy-start(f32[2,768]{1,0:T(2,128)} %get-tuple-element.88) | copy-start | bytes 18436
  352.7 4.4 %copy-start.10 = (bf16[2,768,768]{2,1,0:T(8,128)(2,1)S(1)}, bf16[2,768,768]{2,1,0:T(8,128)(2,1)}, u32[]{:S(2)}) copy-start(bf16[2,768,768]{2,1,0:T(8,128)(2,1)} %get-tuple-element.104) | copy-start | bytes 7077892
  357.1 2.6 copy-start.14
  359.7 1.4 copy-start.20
  359.7 2.3 copy-start.19
  361.1 1.9 copy-start.13
  363.0 1.5 copy-start.18
Sparse Core Ops, SparseCore 0:
  88.6 57.1 all-reduce.4
  163.4 43.0 all-reduce.6
  211.0 86.3 all-reduce.8

commit v3 on v2

v3 whole, which is shorter than its diff:
```python
import functools
import math
import types

import jax
import jax.numpy as jnp
from jax import lax
from jax.experimental import pallas as pl
from jax.experimental.pallas import tpu as pltpu
from jax.sharding import PartitionSpec as P

HEAD = 64
NQ = 32
TXT = 32
QUAD = 4
UNITS = 12
VISUAL_STEPS = 16
EPSILON = 1e-06
MASKED_SCORE = -1e30
SCALE = 1.0 / math.sqrt(HEAD)
WIDE = jnp.float32
NARROW = jnp.bfloat16
VMEM_BYTES = 60 * 2**20


def mm(a, b):
    return lax.dot_general(a, b, (((1,), (0,)), ((), ())), preferred_element_type=WIDE)


def mm_nt(a, b):
    return lax.dot_general(a, b, (((1,), (1,)), ((), ())), preferred_element_type=WIDE)


def mm_tn(a, b):
    return lax.dot_general(a, b, (((0,), (0,)), ((), ())), preferred_element_type=WIDE)


def lane_group(rows, lanes, size):
    return lax.broadcasted_iota(jnp.int32, (rows, lanes), 1) // size


def spread_heads(block, count):
    group = lane_group(1, block.shape[1], HEAD)
    return jnp.concatenate(
        [block * jnp.where(group == h, 1.0, 0.0).astype(NARROW) for h in range(QUAD)], axis=0
    )


def gather_heads(block, count):
    rows, lanes = block.shape[0] // QUAD, block.shape[1]
    group = lane_group(rows, lanes, HEAD)
    out = block[:rows]
    for h in range(1, count):
        out = jnp.where(group == h, block[h * rows : (h + 1) * rows], out)
    return out


def norm_parts(residue):
    mean = jnp.mean(residue, axis=-1, keepdims=True)
    centered = residue - mean
    variance = jnp.mean(centered * centered, axis=-1, keepdims=True)
    inverse = lax.rsqrt(variance + EPSILON)
    return centered * inverse, inverse


def norm_back(unit, inverse, gain_row, cotangent):
    scaled = gain_row * cotangent
    first = jnp.mean(scaled, axis=-1, keepdims=True)
    second = jnp.mean(scaled * unit, axis=-1, keepdims=True)
    return inverse * (scaled - first - unit * second)


def column_sums(unit, cotangent):
    return (
        jnp.sum(cotangent * unit, axis=0, keepdims=True),
        jnp.sum(cotangent, axis=0, keepdims=True),
    )


def gelu_parts(pre):
    bell = jnp.exp(-0.5 * pre * pre)
    half = 0.5 * lax.erf(pre * math.sqrt(0.5)) + 0.5
    return pre * half, half + pre * bell * (1.0 / math.sqrt(2.0 * math.pi))


MESH = pl.DeviceIdType.MESH
PEERS = 8


def flip(index, bit):
    return index + bit - 2 * bit * ((index // bit) % 2)


def greet(targets):
    barrier = pltpu.get_barrier_semaphore()
    for target in targets:
        pl.semaphore_signal(barrier, inc=1, device_id=target, device_id_type=MESH)
    pl.semaphore_wait(barrier, len(targets))


def remote(src, dst, send, recv, target):
    return pltpu.make_async_remote_copy(
        src_ref=src, dst_ref=dst, send_sem=send, recv_sem=recv, device_id=target, device_id_type=MESH
    )


class Spread:
    COPIES = 9

    def __init__(self, at, send, recv, base):
        self.at, self.send, self.recv, self.base = at, send, recv, base
        self.dp, self.tensor = lax.axis_index("dp"), lax.axis_index("tensor")
        self.shards = lax.axis_size("tensor")
        self.peer = self.dp % PEERS

    def hop(self, slot, s, src, dst, target):
        index = self.base + (s - 1) * self.COPIES + slot
        return remote(src, dst, self.send.at[index], self.recv.at[index], target)

    def came(self, s):
        return (self.tensor + self.shards - s) % self.shards

    def along(self, s, own):
        return self.hop(0, s, own, self.at(self.tensor, self.peer, None), (self.dp, (self.tensor + s) % self.shards))

    def hand(self, slot, s, bit, peer, half):
        place = self.at(self.came(s), peer, half)
        return self.hop(slot, s, place, place, (flip(self.dp, bit), self.tensor))

    def across(self, s):
        return [self.hand(1, s, 2, self.peer, None), self.hand(2, s, 4, self.peer, None), self.hand(3, s, 1, self.peer, None)]

    def onward(self, s):
        x, y = flip(self.peer, 2), flip(self.peer, 4)
        return (
            [self.hand(4, s, 4, x, 0), self.hand(5, s, 1, x, None)],
            [self.hand(6, s, 2, y, 1), self.hand(7, s, 1, y, None)],
        )

    def last(self, s):
        return self.hand(8, s, 1, flip(flip(self.peer, 2), 4), None)

    def start_across(self, s):
        for made in self.across(s):
            made.start()

    def wait_across(self, s):
        for made in self.across(s):
            made.wait()

    def start_onward(self, s, arrived=False):
        over_x, over_y, _ = self.across(s)
        by_x, by_y = self.onward(s)
        if not arrived:
            over_x.wait_recv()
        for made in by_x:
            made.start()
        if not arrived:
            over_y.wait_recv()
        for made in by_y:
            made.start()

    def start_last(self, s):
        by_x, by_y = self.onward(s)
        by_x[0].wait_recv()
        by_y[0].wait_recv()
        self.last(s).start()

    def finish(self, s, arrived=False):
        over = self.across(s)
        by_x, by_y = self.onward(s)
        final = self.last(s)
        for made in ([] if arrived else [over[2]]) + [by_x[1], by_y[1], final]:
            made.wait_recv()
        for made in ([] if arrived else over) + by_x + by_y + [final]:
            made.wait_send()

    def targets(self):
        return self.along_targets() + self.peer_targets()

    def along_targets(self):
        return [(self.dp, (self.tensor + s) % self.shards) for s in range(1, self.shards)]

    def peer_targets(self):
        return [(flip(self.dp, bit), self.tensor) for bit in (2, 4, 1)]


FAR = 2


def one_shard(ref):
    rows = ref.shape[0] // PEERS

    def at(shard, peer, half):
        return ref.at[half_rows(peer * rows, rows, half)]

    return at


def half_rows(first, rows, half):
    split = (rows // 2 + 15) // 16 * 16
    start, count = {None: (0, rows), 0: (0, split), 1: (split, rows - split)}[half]
    return pl.ds(pl.multiple_of(first + start, 16), count)


def eighth(ref):
    rows = ref.shape[1] // PEERS

    def at(shard, peer, half):
        return ref.at[shard, half_rows(peer * rows, rows, half)]

    return at


class HeadGather:
    def __init__(self, buffer, send, recv):
        self.buffer, self.send, self.recv = buffer, send, recv
        self.dp, self.tensor = lax.axis_index("dp"), lax.axis_index("tensor")
        self.shards = lax.axis_size("tensor")

    def copies(self, half):
        count = self.buffer.shape[1] // 2
        place = self.buffer.at[self.tensor, pl.ds(half * count, count)]
        return [
            remote(place, place, self.send.at[half, s], self.recv.at[half, s], (self.dp, (self.tensor + s) % self.shards))
            for s in range(1, self.shards)
        ]

    def start(self, half):
        for made in self.copies(half):
            made.start()

    def wait(self, half):
        for made in self.copies(half):
            made.wait()

    def product(self, weights):
        total = mm(self.buffer[0], weights[0])
        for shard in range(1, self.shards):
            total += mm(self.buffer[shard], weights[shard])
        return total


PIECES = 8


class PeerSum:
    def __init__(self, parts, source, total, land, higher, send, recv, base=0, pieces=None):
        self.parts, self.source, self.total, self.land, self.higher = parts, source, total, land, higher
        self.pieces = pieces
        self.send, self.recv, self.base = send, recv, base
        self.dp, self.tensor = lax.axis_index("dp"), lax.axis_index("tensor")
        self.bits = [(self.dp // b) % 2 for b in (1, 2, 4)]

    @staticmethod
    def far_bits():
        return [PEERS << k for k in range((lax.axis_size("dp") // PEERS - 1).bit_length())]

    @staticmethod
    def copies(parts, far):
        return len(parts) * (6 + far)

    def way(self, part):
        order = ((2, self.bits[1]), (4, self.bits[2]))
        return order if part[5] == 0 else order[::-1]

    def rows(self, refs, part, piece, count):
        array, first, size, column, columns, _ = part
        start = pl.multiple_of(first + piece * size, 16)
        return refs[array].at[pl.ds(start, count * size), pl.ds(column, columns)]

    def hop(self, n, stage, src, dst, bit):
        index = self.base + n * (6 + len(self.far_bits())) + stage
        return remote(src, dst, self.send.at[index], self.recv.at[index], (flip(self.dp, bit), self.tensor))

    def landed(self, n, piece, count):
        size = self.parts[n][2]
        return self.land[n].at[pl.ds(pl.multiple_of(piece * size, 16), count * size)]

    def halving(self, n, stage):
        part = self.parts[n]
        core = self.bits[0]
        (bit_1, own_1), (bit_2, own_2) = self.way(part)
        if stage == 0:
            bit, place = 1, self.landed(n, 0, 4)
            out = self.rows(self.source, part, (1 - core) * 4, 4)
            kept = self.rows(self.source, part, core * 4, 4)
        elif stage == 1:
            bit, place = bit_1, self.landed(n, 4, 2)
            out, kept = self.landed(n, (1 - own_1) * 2, 2), self.landed(n, own_1 * 2, 2)
        else:
            bit, place = bit_2, self.landed(n, 6, 1)
            out, kept = self.landed(n, 4 + 1 - own_2, 1), self.landed(n, 4 + own_2, 1)
        goal = self.final_place(n) if stage == 2 else place
        return self.hop(n, stage, out, place, bit), kept, place, goal

    def final_place(self, n):
        if self.pieces is not None:
            return self.pieces[n]
        return self.rows(self.total, self.parts[n], self.final_piece(self.parts[n]), 1)

    def final_piece(self, part):
        (_, own_1), (_, own_2) = self.way(part)
        return self.bits[0] * 4 + own_1 * 2 + own_2

    def gathering(self, n, stage):
        part = self.parts[n]
        core = self.bits[0]
        (bit_1, own_1), (bit_2, _) = self.way(part)
        piece, count, bit = (
            (self.final_piece(part), 1, bit_2), (core * 4 + own_1 * 2, 2, bit_1), (core * 4, 4, 1),
        )[stage]
        place = self.rows(self.total, part, piece, count)
        return self.hop(n, 3 + stage, place, place, bit)

    def targets(self):
        return [(flip(self.dp, bit), self.tensor) for bit in [1, 2, 4] + self.far_bits()]

    def start_halving(self, stage):
        for n in range(len(self.parts)):
            self.halving(n, stage)[0].start()

    def end_halving(self, stage):
        for n in range(len(self.parts)):
            made, kept, place, goal = self.halving(n, stage)
            made.wait_recv()
            goal[...] = (kept[...].astype(WIDE) + place[...].astype(WIDE)).astype(goal.dtype)
        for n in range(len(self.parts)):
            self.halving(n, stage)[0].wait_send()

    def far(self):
        for k, bit in enumerate(self.far_bits()):
            for n in range(len(self.parts)):
                place = self.final_place(n)
                made = self.hop(n, 6 + k, place, self.higher[n].at[k], bit)
                made.start()
                made.wait()
                place[...] = (place[...].astype(WIDE) + self.higher[n][k].astype(WIDE)).astype(place.dtype)

    def start_gathering(self, stage):
        for n in range(len(self.parts)):
            self.gathering(n, stage).start()

    def end_gathering(self, stage):
        for n in range(len(self.parts)):
            self.gathering(n, stage).wait()


def peer_scratch(parts, shapes, far):
    dma = pltpu.SemaphoreType.DMA
    count = PeerSum.copies(parts, far)
    land = [pltpu.VMEM((7 * p[2], p[4]), NARROW) for p in parts]
    higher = [pltpu.VMEM((far, p[2], p[4]) if far else (1, 16, 128), NARROW) for p in parts]
    return [pltpu.VMEM(shape, NARROW) for shape in shapes] + land + higher + [dma((count,)), dma((count,))]


def sum_rows(values, out, land, send, recv):
    dp, tensor = lax.axis_index("dp"), lax.axis_index("tensor")
    bits = [1, 2, 4] + PeerSum.far_bits()

    def hop(k):
        source = values if k == 0 else out.at[k - 1]
        return remote(source, land.at[k], send.at[k], recv.at[k], (flip(dp, bits[k]), tensor))

    def run(k):
        if k > 0:
            hop(k - 1).wait()
            out[k - 1] = (values if k == 1 else out.at[k - 2])[...] + land[k - 1]
        if k < len(bits):
            hop(k).start()

    return [functools.partial(run, k) for k in range(len(bits) + 1)]


def cross_parts(kv, cross):
    width = cross[1]
    return (
        (0, 0, kv[0] // PIECES, 0, width, 0),
        (0, 0, kv[0] // PIECES, width, kv[1] - width, 1),
        (1, 0, cross[0] // PIECES, 0, width, 0),
    )


def self_parts(own):
    third, width = own[0] // 3, own[1]
    return ((0, 0, third // PIECES, 0, width, 0), (0, third, 2 * third // PIECES, 0, width, 1))


def last_sums_kernel(
    own_ref, kv_low, kv_high, cross_piece, first_gain, first_shift, other_gain, other_shift, feed_ref,
    kv_out, cq_out, co_out, qkv_out, so_out, rows_out, feed_total, *rest,
):
    parts = self_parts(own_ref.shape)
    kv_total, cross_total, total = rest[:3]
    land, higher = rest[3:5], rest[5:7]
    send, recv, cross_send, cross_recv, few, few_land, few_send, few_recv, few_in, feed_send, feed_recv = rest[7:]
    del feed_ref
    feed = PeerSum(feed_parts(own_ref.shape[1]), (), (feed_total,), (), (), feed_send, feed_recv)
    late_parts = cross_parts(kv_total.shape, cross_total.shape)
    late = PeerSum(late_parts, (), (kv_total, cross_total), (), (), cross_send, cross_recv)
    peers = PeerSum(parts, (own_ref,), (total,), land, higher, send, recv)
    cols = co_out.shape[0]
    greet(peers.targets())
    peers.start_halving(0)
    feed.start_gathering(2)
    for piece, part in zip((kv_low, kv_high, cross_piece), late_parts):
        late.rows(late.total, part, late.final_piece(part), 1)[...] = piece[...]
    few_in[0:1] = first_gain[...]
    few_in[1:4] = other_gain[...]
    few_in[4:5] = first_shift[...]
    few_in[5:8] = other_shift[...]
    late.start_gathering(0)
    few_steps = sum_rows(few_in, few, few_land, few_send, few_recv)
    few_steps[0]()
    peers.end_halving(0)
    peers.start_halving(1)
    late.end_gathering(0)
    peers.end_halving(1)
    peers.start_halving(2)
    late.start_gathering(1)
    for run in few_steps[1:]:
        run()
    rows_out[...] = few[few.shape[0] - 1]
    peers.end_halving(2)
    peers.far()
    peers.start_gathering(0)
    late.end_gathering(1)
    late.start_gathering(2)
    peers.end_gathering(0)
    peers.start_gathering(1)
    late.end_gathering(2)
    kv_out[0] = kv_total[:cols].astype(WIDE)
    kv_out[1, 128:] = kv_total[cols : 2 * cols - 128].astype(WIDE)
    kv_out[1, :128] = kv_total[2 * cols - 128 :].astype(WIDE)
    cq_out[...] = cross_total[:cols].astype(WIDE)
    co_out[...] = cross_total[cols:].astype(WIDE)
    peers.end_gathering(1)
    peers.start_gathering(2)
    peers.end_gathering(2)
    feed.end_gathering(2)
    for c in range(3):
        qkv_out[c] = total[c * cols : (c + 1) * cols].astype(WIDE)
    so_out[...] = total[3 * cols :].astype(WIDE)


def last_sums(own, pieces, norms, feed, kv, cross, ident, peers):
    cols = own.shape[0] // 4
    width, depth = cross[1], kv[1]
    far = (peers // PEERS - 1).bit_length()
    vmem = pl.BlockSpec(memory_space=pltpu.VMEM)
    steps = 3 + far
    dma = pltpu.SemaphoreType.DMA
    count = PeerSum.copies(cross_parts(kv, cross), far)
    more = PeerSum.copies(feed_parts(width), far)
    hbm = pl.BlockSpec(memory_space=pl.ANY)
    rows = (8, width)

    def wide(*shape):
        return jax.ShapeDtypeStruct(shape, WIDE)

    return pl.pallas_call(
        last_sums_kernel,
        in_specs=[vmem] * (4 + len(norms)) + [hbm],
        out_specs=[vmem] * 6 + [hbm],
        out_shape=[
            wide(2, cols, depth), wide(cols, width), wide(cols, width),
            wide(3, cols, width), wide(cols, width), wide(*rows), jax.ShapeDtypeStruct(feed.shape, feed.dtype),
        ],
        input_output_aliases={4 + len(norms): 6},
        scratch_shapes=[pltpu.VMEM(kv, NARROW), pltpu.VMEM(cross, NARROW)]
        + peer_scratch(self_parts(own.shape), [own.shape], far)
        + [dma((count,)), dma((count,))]
        + [pltpu.VMEM((steps,) + rows, WIDE)] * 2
        + [dma((steps,)), dma((steps,)), pltpu.VMEM(rows, WIDE), dma((more,)), dma((more,))],
        compiler_params=pltpu.CompilerParams(
            collective_id=ident, has_side_effects=True, vmem_limit_bytes=VMEM_BYTES
        ),
        name="last_sums",
    )(own, *pieces, *norms, feed)


def start_kernel(
    x_ref, tail_ref, wkv_ref, qkv_ref, so_ref, cq_ref, co_ref, in_ref,
    k_ref, v_ref, attn_ref, win_ref, cross_ref, w_ref, y_ref, send, recv, local,
):
    step = pl.program_id(0)
    last = pl.num_programs(0) - 1
    block, items, depth = x_ref.shape
    cols = so_ref.shape[0]
    per = PEERS // 4
    rows = cols // per

    def at(shard, peer, half):
        return attn_ref.at[peer // per, half_rows(shard * cols + (peer % per) * rows, rows, half)]

    spread = Spread(at, send, recv, 0)
    peer, tensor = spread.peer, spread.tensor
    steps = range(1, spread.shards)
    base = Spread.COPIES * (spread.shards - 1)
    feed = Spread(eighth(win_ref), send, recv, base)
    cross = Spread(eighth(cross_ref), send, recv, 2 * base)
    few = 2 * cols // PEERS

    def eighth_of(ref, first, count):
        return ref.at[pl.ds(pl.multiple_of(first, 16), count)]

    def start_self(s):
        @pl.when(peer < 3 * per)
        def _():
            spread.along(s, eighth_of(qkv_ref.at[peer // per], (peer % per) * rows, rows)).start()

        @pl.when(peer >= 3 * per)
        def _():
            spread.along(s, eighth_of(so_ref, (peer - 3 * per) * rows, rows)).start()

    def start_cross(s):
        @pl.when(peer < PEERS // 2)
        def _():
            cross.along(s, eighth_of(cq_ref, peer * few, few)).start()

        @pl.when(peer >= PEERS // 2)
        def _():
            cross.along(s, eighth_of(co_ref, (peer - PEERS // 2) * few, few)).start()

    self_any, cross_any = so_ref.at[pl.ds(0, rows)], co_ref.at[pl.ds(0, few)]
    feed_mine = eighth(in_ref)(0, peer, None)
    here = pl.ds(pl.multiple_of(tensor * cols, 16), cols)
    own_copies = [
        pltpu.make_async_copy(source, goal, local.at[n])
        for n, (source, goal) in enumerate(
            [(qkv_ref.at[c], attn_ref.at[c, here]) for c in range(3)]
            + [
                (so_ref, attn_ref.at[3, here]),
                (cq_ref, cross_ref.at[tensor, pl.ds(0, cols)]),
                (co_ref, cross_ref.at[tensor, pl.ds(cols, cols)]),
                (in_ref.at[0], win_ref.at[tensor]),
            ]
        )
    ]

    @pl.when(step == 0)
    def _():
        greet(spread.targets())
        for s in steps:
            start_self(s)
        for made in own_copies:
            made.start()

    @pl.when(step == 0)
    def _():
        low = 128
        w_ref[:cols] = wkv_ref[0]
        w_ref[cols : 2 * cols - low] = wkv_ref[1, low:]
        w_ref[2 * cols - low :] = wkv_ref[1, :low]

    def project(x, first, count):
        y = mm_nt(x, w_ref[...])
        for tile in range(y_ref.shape[0]):
            y_ref[tile, : count * items] = y[:, tile * 128 : (tile + 1) * 128]
        for item in range(items):
            k_low, high, v_low = [
                y_ref[tile, pl.ds(item, count, stride=items)].astype(NARROW) for tile in range(3)
            ]
            k_ref[item, first, :128] = k_low
            k_ref[item, first, 128:] = high[:, : cols - 128]
            v_ref[item, first, :128] = v_low
            v_ref[item, first, 128:] = high[:, cols - 128 :]

    project(
        x_ref[...].reshape(block * items, depth),
        pl.ds(pl.multiple_of(step * block, block), block),
        block,
    )

    @pl.when(step == last)
    def _():
        count = tail_ref.shape[0]
        project(
            tail_ref[...].reshape(count * items, depth),
            pl.ds(k_ref.shape[1] - count, count),
            count,
        )
        for s in steps:
            spread.along(s, self_any).wait_recv()
            spread.start_across(s)
        for s in steps:
            start_cross(s)
            feed.along(s, feed_mine).start()
        for s in steps:
            spread.start_onward(s)
        for s in steps:
            spread.start_last(s)
        for s in steps:
            spread.finish(s)
            spread.along(s, self_any).wait_send()
            cross.along(s, cross_any).wait()
            feed.along(s, feed_mine).wait()
        for made in own_copies:
            made.wait()


def start_layer(visual, wkv, qkv, so, cq, co, ffn_in, shards):
    span, items, depth = visual.shape
    cols, width = so.shape
    steps = 4
    tail = span % (16 * steps)
    block = (span - tail) // steps
    out = pl.BlockSpec((items, span, cols), lambda i: (0, 0, 0))
    shape = jax.ShapeDtypeStruct((items, span, cols), NARROW)
    copies = 3 * Spread.COPIES * (shards - 1)
    dma = pltpu.SemaphoreType.DMA
    hbm = pl.BlockSpec(memory_space=pl.ANY)

    def whole(array):
        return pl.BlockSpec(array.shape, lambda i: (0,) * array.ndim)

    return pl.pallas_call(
        start_kernel,
        grid=(steps,),
        in_specs=[
            pl.BlockSpec((block, items, depth), lambda i: (i, 0, 0)),
            pl.BlockSpec((tail, items, depth), lambda i: (span // tail - 1, 0, 0)),
            pl.BlockSpec(wkv.shape, lambda i: (0, 0, 0)),
            whole(qkv), whole(so), whole(cq), whole(co),
            pl.BlockSpec((1,) + ffn_in.shape[1:], lambda i: (0, 0, 0)),
        ],
        out_specs=[out, out, hbm, hbm, hbm],
        out_shape=[
            shape, shape,
            jax.ShapeDtypeStruct((4, shards * cols, width), NARROW),
            jax.ShapeDtypeStruct((shards,) + ffn_in.shape[1:], NARROW),
            jax.ShapeDtypeStruct((shards, 2 * cols, width), NARROW),
        ],
        scratch_shapes=[
            pltpu.VMEM((2 * cols, depth), NARROW),
            pltpu.VMEM((2 * cols // 128, block * items, 128), WIDE),
            dma((copies,)), dma((copies,)), dma((7,)),
        ],
        compiler_params=pltpu.CompilerParams(
            collective_id=0, has_side_effects=True, vmem_limit_bytes=VMEM_BYTES
        ),
        name="start_layer",
    )(visual, visual, wkv, qkv, so, cq, co, ffn_in)


def feed_copies(shards):
    return 5 * Spread.COPIES * (shards - 1)


def labels_of(position, ends):
    place = position - NQ
    label = jnp.zeros_like(position)
    for end in ends:
        label = label + jnp.where(place >= end, 1, 0)
    return jnp.where(position < NQ, -1, label)


def allowed_pairs(lens_ref, item, span, lanes):
    ends = []
    total = jnp.int32(0)
    for c in range(lens_ref.shape[1]):
        total = total + lens_ref[item, c]
        ends.append(total)
    key_label = labels_of(lax.broadcasted_iota(jnp.int32, (span, lanes), 0), ends)
    query_label = labels_of(lax.broadcasted_iota(jnp.int32, (span, lanes), 1) % span, ends)
    return (key_label == query_label) | (key_label == -1)


def self_forward_kernel(
    lens_ref, x_ref, w_ref, gain_ref, shift_ref, out_ref, in_ref, cross_in, ffn_in, ffn_out,
    q_ref, k_ref, v_ref, p_ref, ctx_ref, res_ref, fq_ref, ft_ref, win_ref, wout_ref, cross_ref, tin_ref, tout_ref,
    send, recv, local,
):
    del in_ref, cross_in
    step = pl.program_id(0)
    tensor = lax.axis_index("tensor")
    shards = lax.axis_size("tensor")
    base = Spread.COPIES * (shards - 1)
    first_in = Spread(eighth(win_ref), send, recv, 0)
    first_out = Spread(eighth(wout_ref), send, recv, base)
    cross = Spread(eighth(cross_ref), send, recv, 2 * base)
    mine = eighth(out_ref)(0, first_out.peer, None)
    text = [
        Spread(one_shard(ref), send, recv, n * base).along(FAR, eighth(own)(1, first_out.peer, None))
        for n, ref, own in ((3, tin_ref, ffn_in), (4, tout_ref, ffn_out))
    ]
    own = pltpu.make_async_copy(out_ref.at[0], wout_ref.at[tensor], local.at[0])
    hops = range(1, shards)

    @pl.when(step == 0)
    def _():
        greet(first_out.targets())
        for s in hops:
            first_out.along(s, mine).start()
            cross.start_across(s)
        for s in hops:
            first_in.start_across(s)
        for made in text:
            made.start()
        own.start()

    span = NQ + TXT
    items = x_ref.shape[0] // span
    lanes = QUAD * HEAD
    x = x_ref[...]
    q_ref[...] = (mm_nt(x, w_ref[0]) .astype(NARROW).astype(WIDE) * SCALE).astype(NARROW)
    k_ref[...] = mm_nt(x, w_ref[1]).astype(NARROW)
    v_ref[...] = mm_nt(x, w_ref[2]).astype(NARROW)

    units = []
    for item in range(items):
        rows = slice(item * span, (item + 1) * span)
        allowed = allowed_pairs(lens_ref, pl.program_id(0) * items + item, span, lanes)
        for quad in range(x_ref.shape[1] // lanes):
            units.append((rows, slice(quad * lanes, (quad + 1) * lanes), allowed))
    scores = [mm_nt(k_ref[r, c], spread_heads(q_ref[r, c], QUAD)) for r, c, _ in units]
    lows = []
    for value, (r, c, allowed) in zip(scores, units):
        value = jnp.where(allowed, value, MASKED_SCORE)
        lifted = jnp.exp(value - jnp.max(value, axis=0, keepdims=True))
        lows.append((lifted * (1.0 / jnp.sum(lifted, axis=0, keepdims=True))).astype(NARROW))
        p_ref[r, c] = lows[-1]
    parts = [mm_tn(low, v_ref[r, c]) for low, (r, c, _) in zip(lows, units)]
    for part, (r, c, _) in zip(parts, units):
        ctx_ref[r, c] = gather_heads(part, QUAD).astype(NARROW)

    residue = x.astype(WIDE) + mm(ctx_ref[...], w_ref[3])
    res_ref[...] = residue
    unit, _ = norm_parts(residue)
    first = unit * gain_ref[0:1] + shift_ref[0:1]
    for item in range(items):
        fq_ref[item * NQ : (item + 1) * NQ] = first[item * span : item * span + NQ]
        ft_ref[item * TXT : (item + 1) * TXT] = first[item * span + NQ : (item + 1) * span]

    @pl.when(step == pl.num_programs(0) - 1)
    def _():
        for s in hops:
            cross.wait_across(s)
            first_in.wait_across(s)
            first_out.along(s, mine).wait()
        for made in text:
            made.wait()
        own.wait()


def self_forward(hidden, lens, weights, gain, shift, ffn_in, ffn_out, win, cross, shards):
    rows, width = hidden.shape
    block = min(rows, 256)
    half = block // 2
    full = pl.BlockSpec((block, width), lambda i: (i, 0))
    halves = pl.BlockSpec((half, width), lambda i: (i, 0))
    low = jax.ShapeDtypeStruct((rows, width), NARROW)
    hbm = pl.BlockSpec(memory_space=pl.ANY)
    dma = pltpu.SemaphoreType.DMA
    return pl.pallas_call(
        self_forward_kernel,
        grid=(rows // block,),
        in_specs=[
            pl.BlockSpec(memory_space=pltpu.SMEM),
            full,
            pl.BlockSpec(weights.shape, lambda i: (0, 0, 0)),
            pl.BlockSpec(gain.shape, lambda i: (0, 0)),
            pl.BlockSpec(shift.shape, lambda i: (0, 0)),
            pl.BlockSpec((1,) + ffn_out.shape[1:], lambda i: (0, 0, 0)), hbm, hbm, hbm, hbm,
        ],
        out_specs=[full, full, full, full, full, full, halves, halves, hbm, hbm, hbm, hbm, hbm],
        out_shape=[
            low, low, low, low, low,
            jax.ShapeDtypeStruct((rows, width), WIDE),
            jax.ShapeDtypeStruct((rows // 2, width), WIDE),
            jax.ShapeDtypeStruct((rows // 2, width), WIDE),
            jax.ShapeDtypeStruct(win.shape, NARROW),
            jax.ShapeDtypeStruct((shards,) + ffn_out.shape[1:], NARROW),
            jax.ShapeDtypeStruct(cross.shape, NARROW),
            jax.ShapeDtypeStruct(ffn_in.shape[1:], NARROW),
            jax.ShapeDtypeStruct(ffn_out.shape[1:], NARROW),
        ],
        input_output_aliases={6: 8, 7: 10},
        scratch_shapes=[
            dma((feed_copies(shards),)), dma((feed_copies(shards),)), dma((1,)),
        ],
        compiler_params=pltpu.CompilerParams(
            collective_id=3, has_side_effects=True, vmem_limit_bytes=VMEM_BYTES
        ),
        name="self_forward",
    )(lens, hidden, weights, gain, shift, ffn_out, win, cross, ffn_in, ffn_out)


def self_backward_kernel(
    x_ref, w_ref, gain_ref, res_ref, gq_ref, gt_ref, q_ref, k_ref, v_ref, p_ref, ctx_ref,
    kv_ref, cross_ref, piece0_ref, piece1_ref,
    grad_ref, grads_ref, gain_out, shift_out, kv_low, kv_high, cross_piece, feed_total,
    down, dctx, dq, dk, dv, acc, *rest,
):
    parts = cross_parts(kv_ref.shape, cross_ref.shape)
    total, land, higher = rest[:2], rest[2:5], rest[5:8]
    send, recv, feed_send, feed_recv, local = rest[8:]
    later = PeerSum(feed_parts(x_ref.shape[1]), (), (feed_total,), (), (), feed_send, feed_recv)
    peers = PeerSum(parts, (kv_ref, cross_ref), total, land, higher, send, recv)
    span = NQ + TXT
    block = res_ref.shape[0]
    items = block // span
    lanes = QUAD * HEAD
    placed = [
        pltpu.make_async_copy(ref, later.rows((feed_total,), part, later.final_piece(part), 1), local.at[n])
        for n, (ref, part) in enumerate(zip((piece0_ref, piece1_ref), later.parts))
    ]
    step = pl.program_id(0)

    @pl.when(step == 0)
    def _():
        for made in placed:
            made.start()
        greet(peers.targets())
        peers.start_halving(0)
        for made in placed:
            made.wait()
        later.start_gathering(0)

    @pl.when(step == 1)
    def _():
        later.end_gathering(0)
        later.start_gathering(1)
        peers.end_halving(0)
        peers.start_halving(1)

    @pl.when(step == 3)
    def _():
        peers.end_halving(1)
        peers.start_halving(2)

    unit, inverse = norm_parts(res_ref[...])
    pieces = []
    for item in range(items):
        pieces.append(gq_ref[item * NQ : (item + 1) * NQ])
        pieces.append(gt_ref[item * TXT : (item + 1) * TXT])
    cotangent = jnp.concatenate(pieces, axis=0)
    grad_res = norm_back(unit, inverse, gain_ref[0:1], cotangent)
    gain_sum, shift_sum = column_sums(unit, cotangent)

    @pl.when(step == 0)
    def _():
        gain_out[...] = gain_sum
        shift_out[...] = shift_sum

    @pl.when(step > 0)
    def _():
        gain_out[...] += gain_sum
        shift_out[...] += shift_sum

    grad_ref[...] = grad_res
    low = grad_res.astype(NARROW)
    down[...] = low
    dctx[...] = mm_nt(low, w_ref[3]).astype(NARROW)

    units = [
        (slice(item * span, (item + 1) * span), slice(quad * lanes, (quad + 1) * lanes))
        for item in range(items)
        for quad in range(w_ref.shape[2] // lanes)
    ]
    for at in range(0, len(units), UNITS):
        some = units[at : at + UNITS]
        spread = [spread_heads(dctx[u], QUAD) for u in some]
        grad_chances = [mm_nt(v_ref[u], one) for u, one in zip(some, spread)]
        scores = []
        for u, value in zip(some, grad_chances):
            weighted = p_ref[u].astype(WIDE)
            inner = jnp.sum(value * weighted, axis=0, keepdims=True)
            scores.append((weighted * (value - inner)).astype(NARROW))
        for u, one in zip(some, spread):
            dv[u] = mm(p_ref[u], one).astype(NARROW)
        for u, one in zip(some, scores):
            dk[u] = mm(one, spread_heads(q_ref[u], QUAD)).astype(NARROW)
        values = [mm_tn(one, k_ref[u]) for u, one in zip(some, scores)]
        for u, value in zip(some, values):
            dq[u] = (gather_heads(value, QUAD) * SCALE).astype(NARROW)

    grad_ref[...] += mm(dq[...], w_ref[0]) + mm(dk[...], w_ref[1]) + mm(dv[...], w_ref[2])

    own = lax.axis_index("tensor")
    cols = grads_ref.shape[0] // 4
    window = acc.shape[1]
    start = pl.multiple_of((own * cols) // 128 * 128, 128)
    here = pl.ds(start, window)
    x = x_ref[...]
    products = (
        mm_tn(dq[:, here], x), mm_tn(dk[:, here], x), mm_tn(dv[:, here], x),
        mm_tn(ctx_ref[:, here], down[...]),
    )

    @pl.when(step == 0)
    def _():
        for c, product in enumerate(products):
            acc[c] = product

    @pl.when(step > 0)
    def _():
        for c, product in enumerate(products):
            acc[c] += product

    @pl.when(step == pl.num_programs(0) - 1)
    def _():
        offset = pl.multiple_of(own * cols - start, 64)
        for c in range(4):
            grads_ref[c * cols : (c + 1) * cols] = acc[c, pl.ds(offset, cols), :].astype(NARROW)
        peers.end_halving(2)
        peers.far()
        for out, part in zip((kv_low, kv_high, cross_piece), parts):
            out[...] = peers.rows(total, part, peers.final_piece(part), 1)[...]
        later.end_gathering(1)


def self_backward(
    hidden, weights, gain, residue, grad_q, grad_t, q, k, v, p, ctx, kv, cross, piece0, piece1,
    cols, ident, peers
):
    rows, width = hidden.shape
    block = min(rows, 256)
    half = block // 2
    full = pl.BlockSpec((block, width), lambda i: (i, 0))
    halves = pl.BlockSpec((half, width), lambda i: (i, 0))
    row = pl.BlockSpec((1, width), lambda i: (0, 0))
    parts = cross_parts(kv.shape, cross.shape)
    far = (peers // PEERS - 1).bit_length()
    pieces = [(p_[2], p_[4]) for p_ in parts]
    hbm = pl.BlockSpec(memory_space=pl.ANY)
    dma = pltpu.SemaphoreType.DMA
    count = PeerSum.copies(feed_parts(width), far)

    def whole(shape):
        return pl.BlockSpec(shape, lambda i: (0,) * len(shape))

    return pl.pallas_call(
        self_backward_kernel,
        grid=(rows // block,),
        in_specs=[
            full,
            pl.BlockSpec(weights.shape, lambda i: (0, 0, 0)),
            pl.BlockSpec(gain.shape, lambda i: (0, 0)),
            full, halves, halves, full, full, full, full, full,
            whole(kv.shape), whole(cross.shape), whole(piece0.shape), whole(piece1.shape),
        ],
        out_specs=[full, whole((4 * cols, width)), row, row] + [whole(p_) for p_ in pieces] + [hbm],
        out_shape=[
            jax.ShapeDtypeStruct((rows, width), WIDE),
            jax.ShapeDtypeStruct((4 * cols, width), NARROW),
            jax.ShapeDtypeStruct((1, width), WIDE),
            jax.ShapeDtypeStruct((1, width), WIDE),
        ]
        + [jax.ShapeDtypeStruct(p_, NARROW) for p_ in pieces]
        + [jax.ShapeDtypeStruct((4 * width, width), NARROW)],
        scratch_shapes=[pltpu.VMEM((block, width), NARROW)] * 5
        + [pltpu.VMEM((4, (cols + 64 + 127) // 128 * 128, width), WIDE)]
        + peer_scratch(parts, [kv.shape, cross.shape], far)
        + [dma((count,)), dma((count,)), dma((2,))],
        compiler_params=pltpu.CompilerParams(
            collective_id=ident, has_side_effects=True, vmem_limit_bytes=VMEM_BYTES
        ),
        name="self_backward",
    )(hidden, weights, gain, residue, grad_q, grad_t, q, k, v, p, ctx, kv, cross, piece0, piece1)


def feed_parts(width):
    rows = 4 * width
    return ((0, 0, rows // 2 // PIECES, 0, width, 0), (0, rows // 2, rows // 2 // PIECES, 0, width, 1))


LOADS = (
    "fq", "wq_own", "k", "v", "ft", "tin", "tout", "cotq", "tcot", "wo_own", "w_all", "tin2", "tout2",
)
STORES = ("outq", "outt", "gq", "gt", "grads", "kv", "piece0", "piece1")


def middle_kernel(names, *refs):
    r = types.SimpleNamespace(**dict(zip(names, refs)))
    cols = r.wq_own.shape[0]
    heads = cols // HEAD
    items, span = r.k.shape[:2]
    width = r.fq.shape[1]
    depth = r.visual.shape[2]
    chunks = r.win.shape[0]
    tensor = lax.axis_index("tensor")
    sources = dict(
        tin=r.ffn_in.at[1], tout=r.ffn_out.at[1],
        w_all=r.cross_o.at[:, pl.ds(cols, cols)], tin2=r.tin2_o, tout2=r.tout2_o,
    )
    rows = [slice(item * NQ, (item + 1) * NQ) for item in range(items)]
    tall = r.fq.shape

    def load(name, goal=None):
        return pltpu.make_async_copy(
            sources.get(name, getattr(r, name, None)),
            getattr(r, name + "_v") if goal is None else goal,
            r.load_sem.at[LOADS.index(name)],
        )

    def store(name, source):
        return pltpu.make_async_copy(source, getattr(r, name + "_o"), r.store_sem.at[STORES.index(name)])

    pair = (lax.axis_index("dp"), tensor + 1 - 2 * (tensor % 2))
    swaps = [remote(r.tpart.at[n], r.tland.at[n], r.swap_send.at[n], r.swap_recv.at[n], pair) for n in range(2)]
    forth = HeadGather(r.heads1, r.head_send1, r.head_recv1)
    gather = HeadGather(r.heads2, r.head_send2, r.head_recv2)
    base = Spread.COPIES * (chunks - 1)
    hops = range(1, chunks)
    first_in = Spread(eighth(r.win_o), r.spread_send, r.spread_recv, 0)
    first_out = Spread(eighth(r.wout_o), r.spread_send, r.spread_recv, base)
    cross = Spread(eighth(r.cross_o), r.spread_send, r.spread_recv, 2 * base)
    text = [
        Spread(one_shard(ref), r.spread_send, r.spread_recv, n * base) for n, ref in ((3, r.tin2_o), (4, r.tout2_o))
    ]
    parts = feed_parts(width)
    feed = [None]
    peers = PeerSum(
        parts, feed, (), r.land, r.higher, r.peer_send, r.peer_recv, pieces=(r.piece0, r.piece1)
    )
    early = ("tin_v", "tout_v", "tin2_v", "tout2_v", "tslope", "tslope2", "cotq_v", "tcot_v")

    def to_feed_forward(*buffers):
        for name, buffer in zip(early, buffers):
            setattr(r, name, buffer)
        for name in LOADS[:10]:
            load(name).start()
        greet(first_in.along_targets() + peers.targets())
        for s in hops:
            cross.start_onward(s, True)
        for s in hops:
            first_in.start_onward(s, True)
            first_out.start_across(s)
        for one in text:
            one.start_across(FAR)
        for name in ("fq", "wq_own", "k", "v"):
            load(name).wait()
        r.q[...] = (
            mm_nt(r.fq_v[...].astype(NARROW), r.wq_own_v[...]).astype(NARROW).astype(WIDE) * SCALE
        ).astype(NARROW)
        for half in range(2):
            some = range(half * items // 2, (half + 1) * items // 2)
            scores = [mm_nt(r.k_v[item], spread_heads(r.q[rows[item]], heads)) for item in some]
            lows = []
            for item, value in zip(some, scores):
                lifted = jnp.exp(value - jnp.max(value, axis=0, keepdims=True))
                lows.append((lifted * (1.0 / jnp.sum(lifted, axis=0, keepdims=True))).astype(NARROW))
                r.p[item] = lows[-1]
            values = [mm_tn(low, r.v_v[item]) for item, low in zip(some, lows)]
            for item, value in zip(some, values):
                r.ctx[rows[item]] = gather_heads(value, heads).astype(NARROW)
            count = items // 2 * NQ
            here = slice(half * count, (half + 1) * count)
            r.heads1[tensor, here] = r.ctx[here]
            forth.start(half)
        for s in hops:
            cross.start_last(s)

        def text_part(win, wout, slope_v, act_v):
            act, slope = gelu_parts(mm(r.ft_v[...].astype(NARROW), win[...]))
            slope_v[...] = slope.astype(NARROW)
            act = act.astype(NARROW)
            if act_v is not None:
                act_v[...] = act
            return mm(act, wout[...])

        for name in ("ft", "tin", "tout"):
            load(name).wait()
        r.gt_v[...] = text_part(r.tin_v, r.tout_v, r.tslope, r.tact)
        for s in hops:
            cross.finish(s, True)
        load("w_all").start()
        for one in text:
            one.start_onward(FAR)
        for s in hops:
            first_out.start_onward(s)
        for s in hops:
            first_in.start_last(s)
        for one in text:
            one.start_last(FAR)
        for one in text:
            one.finish(FAR)
        load("tin2").start()
        load("tout2").start()
        forth.wait(0)
        forth.wait(1)
        load("w_all").wait()
        r.gq_v[...] = forth.product(r.w_all_v)
        sources["w_all"] = r.cross_o.at[:, pl.ds(0, cols)]
        load("w_all").start()
        load("tin2").wait()
        load("tout2").wait()
        r.tpart[0] = (r.gt_v[...] + text_part(r.tin2_v, r.tout2_v, r.tslope2, None)).astype(NARROW)
        swaps[0].start()
        for s in hops:
            first_out.start_last(s)
        for s in hops:
            first_in.finish(s, True)

        def text_rows():
            load("tcot").wait()
            unit, inverse = norm_parts(r.ft_v[...] + r.tpart[0].astype(WIDE) + r.tland[0].astype(WIDE))
            r.outt[...] = (unit * r.gain[3:4] + r.shift[3:4]).astype(NARROW)
            store("outt", r.outt).start()
            cotangent = r.tcot_v[...].astype(WIDE)
            gain_sum, shift_sum = column_sums(unit, cotangent)
            r.gains[2:3] = gain_sum
            r.shifts[2:3] = shift_sum
            grad = norm_back(unit, inverse, r.gain[3:4], cotangent)
            r.gt_v[...] = grad
            r.ttop[...] = grad.astype(NARROW)
            r.tdpre[...] = (mm_nt(r.ttop[...], r.tout_v[...]) * r.tslope[...].astype(WIDE)).astype(NARROW)
            far = (mm_nt(r.ttop[...], r.tout2_v[...]) * r.tslope2[...].astype(WIDE)).astype(NARROW)
            r.tpart[1] = (mm_nt(r.tdpre[...], r.tin_v[...]) + mm_nt(far, r.tin2_v[...])).astype(NARROW)
            swaps[1].start()

        def query_rows(slopes, total, weights, outq):
            def fetch(j):
                slot, chunk = j % 2, j % chunks
                return [
                    pltpu.make_async_copy(ref.at[chunk], weights.at[slot, n], r.weight_sem.at[slot, n])
                    for n, ref in enumerate((r.win_o, r.wout_o))
                ]

            unit, _ = norm_parts(r.fq_v[...] + r.gq_v[...])
            value = unit * r.gain[1:2] + r.shift[1:2]
            r.low[...] = value.astype(NARROW)
            total[...] = value
            for s in hops:
                first_out.finish(s)
            for made in fetch(0):
                made.start()

            def next_weights(j):
                for made in fetch(j):
                    made.wait()

                @pl.when(j + 1 < 2 * chunks)
                def _():
                    for made in fetch(j + 1):
                        made.start()

                return weights.at[j % 2, 0], weights.at[j % 2, 1]

            @pl.loop(0, chunks)
            def _(j):
                win, wout = next_weights(j)
                act, slope = gelu_parts(mm(r.low[...], win[...]))
                slopes[j] = slope.astype(NARROW)
                act = act.astype(NARROW)
                total[...] += mm(act, wout[...])

                @pl.when(j == tensor)
                def _():
                    r.act[...] = act


            unit, inverse = norm_parts(total[...])
            outq[...] = (unit * r.gain[2:3] + r.shift[2:3]).astype(NARROW)
            store("outq", outq).start()
            load("cotq").wait()
            cotangent = r.cotq_v[...].astype(WIDE)
            gain_sum, shift_sum = column_sums(unit, cotangent)
            r.gains[1:2] = gain_sum
            r.shifts[1:2] = shift_sum
            grad = norm_back(unit, inverse, r.gain[2:3], cotangent)
            total[...] = grad
            r.top[...] = grad.astype(NARROW)

            @pl.loop(chunks, 2 * chunks)
            def _(j):
                win, wout = next_weights(j)
                chunk = j - chunks
                dpre = (mm_nt(r.top[...], wout[...]) * slopes[chunk].astype(WIDE)).astype(NARROW)
                total[...] += mm_nt(dpre, win[...])

                @pl.when(chunk == tensor)
                def _():
                    r.dpre[...] = dpre

                @pl.when(chunk == 2)
                def _():
                    swaps[0].wait()
                    text_rows()


            grad_second = total[...]
            unit, inverse = norm_parts(r.fq_v[...] + r.gq_v[...])
            gain_sum, shift_sum = column_sums(unit, grad_second)
            r.gains[0:1] = gain_sum
            r.shifts[0:1] = shift_sum
            grad = norm_back(unit, inverse, r.gain[1:2], grad_second)
            r.gq_v[...] = grad
            r.down[...] = grad.astype(NARROW)
            store("outq", outq).wait()

        pl.run_scoped(
            query_rows,
            pltpu.VMEM((chunks, tall[0], r.win.shape[2]), NARROW),
            pltpu.VMEM(tall, WIDE),
            pltpu.VMEM((2, 2) + r.win.shape[1:], NARROW),
            pltpu.VMEM(tall, NARROW),
        )

    inner, outer = r.ffn_in.shape[1:], r.ffn_out.shape[1:]
    pl.run_scoped(
        to_feed_forward,
        *[pltpu.VMEM(shape, NARROW) for shape in (inner, outer, inner, outer, (tall[0], inner[1]), (tall[0], inner[1]), tall, tall)],
    )

    def feed_gradients(goal):
        feed[0] = goal
        goal[:width] = mm_tn(r.low[...], r.dpre[...]).astype(NARROW)
        goal[width : 2 * width] = mm_tn(r.ft_v[...].astype(NARROW), r.tdpre[...]).astype(NARROW)
        goal[2 * width : 3 * width] = mm_tn(r.act[...], r.top[...]).astype(NARROW)
        goal[3 * width :] = mm_tn(r.tact[...], r.ttop[...]).astype(NARROW)
        peers.start_halving(0)

    def cross_rows(dctx, dq, score, dkv, acc, x, x_tail, kv, feed_v):
        group = items // 4
        steps = VISUAL_STEPS
        tail = span % steps
        block = (span - tail) // steps

        def fetch(j):
            return pltpu.make_async_copy(r.visual.at[pl.ds(j * block, block)], x.at[j % 2], r.x_sem.at[j % 2])

        rest = pltpu.make_async_copy(r.visual.at[pl.ds(span - tail, tail)], x_tail, r.x_sem.at[2])
        fetch(0).start()
        rest.start()
        load("wo_own").wait()
        dctx[...] = mm_nt(r.down[...], r.wo_own_v[...]).astype(NARROW)
        for g in range(4):
            some = range(g * group, (g + 1) * group)
            spread = [spread_heads(dctx[rows[item]], heads) for item in some]
            grad_chances = [mm_nt(r.v_v[item], one) for item, one in zip(some, spread)]
            scores = []
            for item, value in zip(some, grad_chances):
                weighted = r.p[item].astype(WIDE)
                inner = jnp.sum(value * weighted, axis=0, keepdims=True)
                scores.append((weighted * (value - inner)).astype(NARROW))
                score[item] = scores[-1]
            values = [mm_tn(one, r.k_v[item]) for item, one in zip(some, scores)]
            for item, value in zip(some, values):
                dq[rows[item]] = (gather_heads(value, heads) * SCALE).astype(NARROW)
            if g % 2:
                count = 2 * group * NQ
                here = slice(g // 2 * count, (g // 2 + 1) * count)
                r.heads2[tensor, here] = dq[here]
                gather.start(g // 2)
        feed_gradients(feed_v)
        none = jnp.zeros((QUAD * NQ, cols), NARROW)
        for g in range(4):
            some = range(g * group, (g + 1) * group)
            both = []
            for item in some:
                one = spread_heads(dctx[rows[item]], heads)
                both.append(
                    mm(
                        jnp.concatenate([score[item], r.p[item]], axis=1),
                        jnp.concatenate(
                            [
                                jnp.concatenate([spread_heads(r.q[rows[item]], heads), none], axis=1),
                                jnp.concatenate([none, one[:, 128:], one[:, :128]], axis=1),
                            ],
                            axis=0,
                        ),
                    )
                )
            for item, value in zip(some, both):
                for tile in range(dkv.shape[0]):
                    dkv[tile, pl.ds(item, span, stride=items)] = value[:, tile * 128 : (tile + 1) * 128]
            if g == 2:
                peers.end_halving(0)
                peers.start_halving(1)
        r.grads[:cols] = mm_tn(dq[...], r.fq_v[...].astype(NARROW)).astype(NARROW)
        r.grads[cols:] = mm_tn(r.ctx[...], r.down[...]).astype(NARROW)
        store("grads", r.grads).start()

        def product(first, count, value):
            grads = [dkv[tile, pl.ds(first, count)].astype(NARROW) for tile in range(dkv.shape[0])]
            return mm_tn(jnp.concatenate(grads, axis=1), value.reshape(count, depth))

        rest.wait()
        acc[...] = product((span - tail) * items, tail * items, x_tail[...])

        @pl.loop(0, steps)
        def _(j):
            fetch(j).wait()

            @pl.when(j + 1 < steps)
            def _():
                fetch(j + 1).start()

            acc[...] += product(pl.multiple_of(j * block * items, 16), block * items, x[j % 2])

            @pl.when(j == 11)
            def _():
                peers.end_halving(1)
                peers.start_halving(2)

        kv[...] = acc[...].astype(kv.dtype)
        store("kv", kv).start()
        gather.wait(0)
        gather.wait(1)
        load("w_all").wait()
        r.gq_v[...] += gather.product(r.w_all_v)
        store("gq", r.gq_v).start()
        swaps[1].wait()
        r.gt_v[...] += r.tpart[1].astype(WIDE) + r.tland[1].astype(WIDE)
        store("gt", r.gt_v).start()
        peers.end_halving(2)
        peers.far()
        store("piece0", r.piece0).start()
        store("piece1", r.piece1).start()
        store("kv", kv).wait()

    pl.run_scoped(
        cross_rows,
        pltpu.VMEM((tall[0], cols), NARROW),
        pltpu.VMEM((tall[0], cols), NARROW),
        pltpu.VMEM((items, span, QUAD * NQ), NARROW),
        pltpu.VMEM((2 * cols // 128, items * span, 128), WIDE),
        pltpu.VMEM((2 * cols, depth), WIDE),
        pltpu.VMEM((2, span // VISUAL_STEPS, items, depth), NARROW),
        pltpu.VMEM((span % VISUAL_STEPS, items, depth), NARROW),
        pltpu.VMEM((2 * cols, depth), NARROW),
        pltpu.VMEM((4 * width, width), NARROW),
    )
    for name, source in (
        ("outt", r.outt), ("gq", r.gq_v), ("gt", r.gt_v), ("grads", r.grads), ("piece0", r.piece0), ("piece1", r.piece1),
    ):
        store(name, source).wait()


def middle(arrays, ident, peers):
    rows, width = arrays["fq"].shape
    cols = arrays["wq_own"].shape[0]
    items, span = arrays["k"].shape[:2]
    hidden = arrays["ffn_in"].shape[2]
    depth = arrays["visual"].shape[2]
    shards = arrays["win"].shape[0]
    far = (peers // PEERS - 1).bit_length()
    parts = feed_parts(width)
    piece = (parts[0][2], width)
    dma = pltpu.SemaphoreType.DMA
    hbm, vmem = pl.BlockSpec(memory_space=pl.ANY), pl.BlockSpec(memory_space=pltpu.VMEM)

    def low(*dims):
        return pltpu.VMEM(dims, NARROW)

    def wide(*dims):
        return pltpu.VMEM(dims, WIDE)

    out = jax.ShapeDtypeStruct
    outs = dict(
        outq_o=out((rows, width), NARROW), outt_o=out((rows, width), NARROW),
        gq_o=out((rows, width), WIDE), gt_o=out((rows, width), WIDE),
        grads_o=out((2 * cols, width), NARROW), kv_o=out((2 * cols, depth), NARROW),
        piece0_o=out(piece, NARROW), piece1_o=out(piece, NARROW),
        gains=out((3, width), WIDE), shifts=out((3, width), WIDE),
        win_o=out(arrays["win"].shape, NARROW), wout_o=out(arrays["wout"].shape, NARROW),
        cross_o=out(arrays["cross_w"].shape, NARROW),
        tin2_o=out(arrays["tin2"].shape, NARROW), tout2_o=out(arrays["tout2"].shape, NARROW),
    )
    copies = feed_copies(shards)
    total = peer_scratch(parts, [], far)
    scratch = dict(
        fq_v=wide(rows, width), wq_own_v=low(cols, width), wo_own_v=low(cols, width),
        k_v=low(*arrays["k"].shape), v_v=low(*arrays["v"].shape), ft_v=wide(rows, width),
        w_all_v=low(shards, cols, width),
        q=low(rows, cols), ctx=low(rows, cols), p=low(items, span, QUAD * NQ),
        tact=low(rows, hidden),
        low=low(rows, width), top=low(rows, width), down=low(rows, width),
        act=low(rows, hidden), dpre=low(rows, hidden),
        ttop=low(rows, width), tdpre=low(rows, hidden), outt=low(rows, width),
        gq_v=wide(rows, width), gt_v=wide(rows, width), grads=low(2 * cols, width),
        tpart=low(2, rows, width), tland=low(2, rows, width), swap_send=dma((2,)), swap_recv=dma((2,)),
        heads1=low(shards, rows, cols), head_send1=dma((2, shards)), head_recv1=dma((2, shards)),
        heads2=low(shards, rows, cols), head_send2=dma((2, shards)), head_recv2=dma((2, shards)),
        spread_send=dma((copies,)), spread_recv=dma((copies,)),
        piece0=low(*piece), piece1=low(*piece),
        land=total[:2], higher=total[2:4], peer_send=total[4], peer_recv=total[5],
        load_sem=dma((len(LOADS),)), store_sem=dma((len(STORES),)), weight_sem=dma((2, 2)), x_sem=dma((3,)),
    )
    names = tuple(arrays) + tuple(outs) + tuple(scratch)
    return dict(
        zip(
            outs,
            pl.pallas_call(
                functools.partial(middle_kernel, names),
                in_specs=[vmem if name in ("gain", "shift") else hbm for name in arrays],
                out_specs=[vmem if name in ("gains", "shifts") else hbm for name in outs],
                out_shape=list(outs.values()),
                input_output_aliases={
                    list(arrays).index(a): list(outs).index(b)
                    for a, b in (
                        ("win", "win_o"), ("wout", "wout_o"), ("cross_w", "cross_o"), ("tin2", "tin2_o"), ("tout2", "tout2_o"),
                    )
                },
                scratch_shapes=list(scratch.values()),
                compiler_params=pltpu.CompilerParams(
                    collective_id=ident, has_side_effects=True, vmem_limit_bytes=62 * 2**20
                ),
                name="middle",
            )(*arrays.values()),
        )
    )


def on_device(
    hidden_in,
    visual_feats,
    caption_lengths,
    self_qkv,
    self_out,
    cross_query,
    cross_kv,
    cross_out,
    ffn_in,
    ffn_out,
    norm_gain,
    norm_shift,
    out_grad,
):
    items = visual_feats.shape[0]
    rows, width = hidden_in.shape
    span = rows // items
    cols = self_qkv.shape[2]
    shards = lax.axis_size("tensor")

    visual = jnp.swapaxes(visual_feats, 0, 1)
    cross_wq = jnp.swapaxes(cross_query, 0, 1)
    cross_k, cross_v, attn, win_q, cross_w = start_layer(
        visual, jnp.swapaxes(cross_kv, 1, 2), jnp.swapaxes(self_qkv, 1, 2), self_out, cross_wq, cross_out, ffn_in, shards
    )
    q, k, v, p, ctx, residue, first_q, first_t, win_q, wout_q, cross_w, tin_far, tout_far = self_forward(
        hidden_in, caption_lengths, attn, norm_gain, norm_shift, ffn_in, ffn_out, win_q, cross_w, shards
    )
    cot = out_grad.reshape(items, span, width)
    cot_q = cot[:, :NQ].reshape(items * NQ, width)
    cot_t = cot[:, NQ:].reshape(items * TXT, width)
    peers = lax.axis_size("dp")
    mid = middle(
        dict(
            fq=first_q, wq_own=cross_wq, k=cross_k, v=cross_v, ft=first_t, cotq=cot_q, tcot=cot_t, wo_own=cross_out,
            ffn_in=ffn_in, ffn_out=ffn_out, win=win_q, wout=wout_q, cross_w=cross_w, tin2=tin_far, tout2=tout_far, visual=visual,
            gain=norm_gain, shift=norm_shift,
        ),
        2, peers,
    )
    out_q, out_t, g_cross, g_kv = mid["outq_o"], mid["outt_o"], mid["grads_o"], mid["kv_o"]
    grad_hidden, g_self, gain_first, shift_first, *pieces, g_feed = self_backward(
        hidden_in, attn, norm_gain, residue, mid["gq_o"], mid["gt_o"], q, k, v, p, ctx, g_kv, g_cross,
        mid["piece0_o"], mid["piece1_o"], cols, 6, peers,
    )
    norms = (gain_first, shift_first, mid["gains"], mid["shifts"])
    kv_shape, cross_shape = g_kv.shape, g_cross.shape
    g_kv, g_cq, g_co, g_qkv, g_so, gains, g_feed = last_sums(
        g_self, pieces, norms, g_feed, kv_shape, cross_shape, 4, peers
    )
    g_feed = g_feed.reshape(2, 2, width, width).astype(WIDE)
    g_in, g_out = g_feed[0], g_feed[1]
    out = jnp.concatenate(
        [out_q.reshape(items, NQ, width), out_t.reshape(items, TXT, width)], axis=1
    ).reshape(rows, width)
    return (
        out,
        grad_hidden,
        jnp.swapaxes(g_qkv, 1, 2),
        g_so,
        jnp.swapaxes(g_cq, 0, 1),
        jnp.swapaxes(g_kv, 1, 2),
        g_co,
        g_in,
        g_out,
        gains[:4],
        gains[4:],
    )


def solution(mesh):
    placed = (
        P("dp", None),
        P("dp", None, None),
        P("dp", None),
        P(None, None, "tensor"),
        P("tensor", None),
        P(None, "tensor"),
        P(None, None, "tensor"),
        P("tensor", None),
        P(None, None, "tensor"),
        P(None, "tensor", None),
        P(),
        P(),
        P("dp", None),
    )
    return jax.shard_map(
        on_device,
        mesh=mesh,
        in_specs=placed,
        out_specs=(
            P("dp", None),
            P("dp", None),
            P(None, None, "tensor"),
            P("tensor", None),
            P(None, "tensor"),
            P(None, None, "tensor"),
            P("tensor", None),
            P(None, None, "tensor"),
            P(None, "tensor", None),
            P(),
            P(),
        ),
        check_vma=False,
    )
```

time: 373 us -> 294 us (0.79); the launches traced: 372 us -> 288 us
  Pallas kernels: 306 us -> 266 us
  other arithmetic: 21.9 us -> 1.26 us
  matrix products: 13.7 us -> 0 us
  between operations: 14 us -> 1.17 us
  local copies, waits for them, and re-layouts: 15.7 us -> 20.4 us
    pallas_call x8 -> x3, Pallas kernels: 235 us -> 186 us  [the longest x1 105 us: middle(): pl.pallas_call(functools.partial(middle_kernel, names), in_specs=[vmem if...]
    dot_general x8 -> x0, matrix products: 13.7 us -> none  [the longest x4 5.75 us: mm_tn(): lax.dot_general(a, b, (((0,), (0,)), ((), ())), preferred_element_type=WIDE)]
    slice x2, local copies, waits for them, and re-layouts: 1.69 us -> 9.62 us  [the longest x1 7 us: on_device(): g_in, g_out = (g_feed[0], g_feed[1])]
    convert_element_type x2 -> x0, other arithmetic: 6.91 us -> none  [on_device(): g_in, g_out = (g_in.astype(WIDE), g_out.astype(WIDE))]
    pallas_call x1, Pallas kernels: 33.5 us -> 39.3 us  [self_forward(): pl.pallas_call(self_forward_kernel, grid=(rows // block,), in_specs=[pl.B...]
    add x2 -> x0, other arithmetic: 3.83 us -> none  [the longest x1 2.42 us: on_device(): grad_t = grad_t + back_t.astype(WIDE)]
    unnamed x56 -> x23, local copies, waits for them, and re-layouts: 11.2 us -> 9.33 us
  transfers between devices with their start and end apart: 3 -> 0, of which waited for: 0 -> 0; matrix products, arithmetic and copies ran while one was open for 5% -> 0% of each run, Pallas kernels for 63% -> 0%
where the time goes in v3:
time: 294 us; the launch traced here: 288 us
  Pallas kernels  266 us (90%)
  local copies, waits for them, and re-layouts  20.4 us (7%)
    pallas_call x1, Pallas kernels, middle(): pl.pallas_call(functools.partial(middle_kernel, names), in_specs=[vmem if...  105 us
    pallas_call x1, Pallas kernels, self_backward(): pl.pallas_call(self_backward_kernel, grid=(rows // block,), in_specs=[ful...  41.1 us
    pallas_call x1, Pallas kernels, start_layer(): pl.pallas_call(start_kernel, grid=(steps,), in_specs=[pl.BlockSpec((block...  40.7 us
    pallas_call x1, Pallas kernels, self_forward(): pl.pallas_call(self_forward_kernel, grid=(rows // block,), in_specs=[pl.B...  39.3 us
    pallas_call x1, Pallas kernels, last_sums(): pl.pallas_call(last_sums_kernel, in_specs=[vmem] * (4 + len(norms)) + [hb...  39.1 us
    unnamed x23, local copies, waits for them, and re-layouts  9.33 us
    slice x1, local copies, waits for them, and re-layouts, on_device(): g_in, g_out = (g_feed[0], g_feed[1])  7 us

profile of v3, /device:TPU:0, one launch (start us, length us, event | category | flops | bytes accessed | tf_op | source)
XLA Modules:
  0.0 288.4 jit_solution(12469375928135863050)
XLA Ops:
  0.6 1.4 copy.32.lens_ref
  2.0 2.6 fusion.1
  4.6 40.7 %start_layer.1 = (bf16[16,257,192]{2,1,0:T(8,128)(2,1)}, bf16[16,257,192]{2,1,0:T(8,128)(2,1)}, bf16[4,768,768]{2,1,0:T(8,128)(2,1)}, bf16[4,768,768]{2,1,0:T(8,128)(2,1)}, bf16[4,384,768]{2,1,0:T(8,128)(2,1)}) custom-call(bf16[257,16,1408]{2,1,0:T(8,128)(2,1)} %bitcast.15, bf16[257,16,1408]{2,1,0:T(8,128)(2,1)} %bitcast.16, bf16[2,192,1408]{2,1,0:T(8,128)(2,1)} %bitcast.28, ...), custom_call_target="tpu_custom_call" | custom-call | tf_op jit(solution)/shard_map/start_layer/pallas_call | solution.py:617
  45.3 39.3 %self_forward.1 = (bf16[1024,768]{1,0:T(8,128)(2,1)}, bf16[1024,768]{1,0:T(8,128)(2,1)}, bf16[1024,768]{1,0:T(8,128)(2,1)}, bf16[1024,768]{1,0:T(8,128)(2,1)}, b...) custom-call(s32[16,4]{1,0:T(8,128)} %copy.32.lens_ref, ...), custom_call_target="tpu_custom_call", output_to_operand_aliasing={{8}: (6, {}), {10}: (7, {})} | custom-call | tf_op jit(solution)/shard_map/self_forward/pallas_call | solution.py:755
  84.7 105.3 %middle.1 = (bf16[512,768]{1,0:T(8,128)(2,1)}, bf16[512,768]{1,0:T(8,128)(2,1)}, f32[512,768]{1,0:T(8,128)}, f32[512,768]{1,0:T(8,128)}, bf16[384,768]{1,0:T(8,1...) custom-call(f32[512,768]{1,0:T(8,128)} %get-tuple-element.57.refs_0_, ...), custom_call_target="tpu_custom_call", output_to_operand_aliasing={{10}: (10, {}), {11}: (11, {}), {12}: (12, {}), {13}: (13, ... | custom-call | tf_op jit(solution)/shard_map/middle/pallas_call | solution.py:1386
  190.0 0.0 copy-start.3
  190.0 0.0 copy-start.4
  190.0 41.1 %self_backward.1 = (f32[1024,768]{1,0:T(8,128)}, bf16[768,768]{1,0:T(8,128)(2,1)}, f32[1,768]{1,0:T(1,128)}, f32[1,768]{1,0:T(1,128)}, bf16[48,768]{1,0:T(8,128)...) custom-call(bf16[1024,768]{1,0:T(8,128)(2,1)} %x_ref.3, ...), custom_call_target="tpu_custom_call" | custom-call | tf_op jit(solution)/shard_map/self_backward/pallas_call | solution.py:933
  231.1 0.0 copy-done.3
  231.1 0.0 copy-done.4
  231.1 1.3 pad_maximum_fusion
  232.4 39.1 %last_sums.1 = (f32[2,192,1408]{2,1,0:T(8,128)}, f32[192,768]{1,0:T(8,128)}, f32[192,768]{1,0:T(8,128)}, f32[3,192,768]{2,1,0:T(8,128)}, f32[192,768]{1,0:T(8,12...) custom-call(bf16[768,768]{1,0:T(8,128)(2,1)} %get-tuple-element.81.own_ref, ...), custom_call_target="tpu_custom_call", output_to_operand_aliasing={{6}: (8, {})} | custom-call | tf_op jit(solution)/shard_map/last_sums/pallas_call | solution.py:461
  271.5 1.4 fusion.2
  273.0 0.0 copy-start
  273.0 7.0 %fusion = (f32[1536,768]{1,0:T(8,128)}, f32[1536,768]{1,0:T(8,128)}) fusion(bf16[3072,768]{1,0:T(8,128)(2,1)} %get-tuple-element.95), kind=kLoop, calls=%fused_computation.1 | loop fusion | bytes 18874368 | tf_op jit(solution)/shard_map/slice | solution.py:1459
  280.0 0.0 copy-done
  280.0 0.0 copy-start.2
  280.0 1.7 copy.47
  281.6 0.9 copy-done.2
  282.6 0.0 copy-start.7
  282.6 0.0 copy-start.6
  282.6 0.0 copy-start.1
  282.6 1.2 copy.48
  283.8 0.2 copy-done.7
  284.0 0.8 copy.49
  284.8 0.0 copy-done.6
  284.8 0.8 copy.50
  285.7 0.0 copy-done.1
  285.7 0.0 copy-start.5
  285.7 1.3 copy.51
  287.0 0.1 copy-done.5
  287.1 0.8 copy.52
Async XLA Ops:
  190.0 41.1 %copy-start.3 = (bf16[512,768]{1,0:T(8,128)(2,1)S(1)}, bf16[512,768]{1,0:T(8,128)(2,1)}, u32[]{:S(2)}) copy-start(bf16[512,768]{1,0:T(8,128)(2,1)} %get-tuple-element.66) | copy-start | bytes 2359300
  190.0 41.1 %copy-start.4 = (bf16[512,768]{1,0:T(8,128)(2,1)S(1)}, bf16[512,768]{1,0:T(8,128)(2,1)}, u32[]{:S(2)}) copy-start(bf16[512,768]{1,0:T(8,128)(2,1)} %get-tuple-element.67) | copy-start | bytes 2359300
  273.0 7.0 %copy-start = (f32[1024,768]{1,0:T(8,128)S(1)}, f32[1024,768]{1,0:T(8,128)}, u32[]{:S(2)}) copy-start(f32[1024,768]{1,0:T(8,128)} %get-tuple-element.115) | copy-start | bytes 9437188
  280.0 2.6 copy-start.2
  282.6 1.4 copy-start.7
  282.6 2.3 copy-start.6
  282.6 3.1 %copy-start.1 = (f32[2,192,1408]{2,1,0:T(8,128)S(1)}, f32[2,192,1408]{2,1,0:T(8,128)}, u32[]{:S(2)}) copy-start(f32[2,192,1408]{2,1,0:T(8,128)} %get-tuple-element.93) | copy-start | bytes 6488068
  285.7 1.5 copy-start.5
